TPU v7x, 256 devices: a whole 4x4x8 slice. The times are simulated.
256 devices in a mesh: seq: 32 (over z, x), head: 8 (over y, core).
Axes of the slice: x: 4, y: 4, z: 8, core: 2. Of those that a mesh axis runs over, the one named last changes fastest.
Arguments:
- queries: bfloat16 [2, 32, 14336], P(None, 'seq', 'head'), may hold values from -150 to 150
- new_keys: bfloat16 [2, 32, 14336], P(None, 'seq', 'head'), may hold values from -6 to 6
- new_values: bfloat16 [2, 32, 14336], P(None, 'seq', 'head'), may hold values from -6 to 6
- cache_keys: bfloat16 [32768, 14336], P('seq', 'head'), may hold values from -6 to 6
- cache_values: bfloat16 [32768, 14336], P('seq', 'head'), may hold values from -6 to 6
- slopes: float32 [112], P('head'), may hold values from 1.8310548e-05 to 0.025
- seg_blocks: int32 [32], replicated, may hold values from 1 to 128, 192 in all
- request_row: int32 [32], replicated, may hold values from 0 to 31, each once
- out_weight: bfloat16 [14336, 14336], P('head', 'seq'), may hold values from -0.046875 to 0.046875
- residual: bfloat16 [2, 32, 14336], P(None, 'head', 'seq'), may hold values from -6 to 6
Outputs:
- mixed: bfloat16 [2, 32, 14336], P(None, 'head', 'seq')
Inputs may be any that keep to these rules, and one draw needn't show every extreme that they name: `seg_blocks`: the requests are packed in order from block 0; 192 blocks are used and the rest of the cache is unused. `request_row`: each query row belongs to exactly one request.
All inputs are finite; a program needn't handle non-finite values.
Results may differ from a plain program's by a relative error of at most 0.006.
Values may be sent and summed in bfloat16 or wider, within the bound.
No kernel may reach another device: no remote copies, remote signals or barrier semaphores. Data moves between devices by JAX's collectives and lax.ppermute only.
A program may use at most 64 MiB of HBM per device.

v0:
```python
import math

import jax
import jax.numpy as jnp
from jax import lax
from jax.sharding import PartitionSpec as P

BLK = 128


NEG = -1e30


def from_everyone(x, axis):
    peers = lax.axis_size(axis)
    return lax.all_to_all(jnp.broadcast_to(x[None], (peers, *x.shape)), axis, 0, 0, tiled=True)


def in_order(blocks, dim):
    dims = list(blocks.shape[1:])
    dims[dim] *= blocks.shape[0]
    return jnp.moveaxis(blocks, 0, dim).reshape(dims)


def collect(x, axis, dim):
    blocks = from_everyone(x, axis)
    return in_order(blocks, dim)


def side_by_side(arrays, axis, split_dim, concat_dim, along):
    widths = [math.prod(a.shape[along:]) for a in arrays]
    both = jnp.concatenate(
        [a.reshape(*a.shape[:along], w) for a, w in zip(arrays, widths)], axis=along
    )
    out = lax.all_to_all(both, axis, split_axis=split_dim, concat_axis=concat_dim, tiled=True)
    blocks = jnp.split(out, [sum(widths[:k]) for k in range(1, len(widths))], axis=along)
    return tuple((b.reshape(*out.shape[:along], *a.shape[along:]) for a, b in zip(arrays, blocks)))


def split_up(x, dim, peers):
    before, after = (x.shape[:dim], x.shape[dim + 1 :])
    return jnp.moveaxis(x.reshape(*before, peers, -1, *after), dim, 0)


def summed_on_arrival(x, axis, dim):
    peers = lax.axis_size(axis)
    blocks = lax.all_to_all(split_up(x, dim, peers), axis, 0, 0, tiled=True)
    return jnp.sum(blocks.astype(jnp.float32), axis=0)


def combine(first, second):
    top_a, sum_a, acc_a = first
    top_b, sum_b, acc_b = second
    top = jnp.maximum(top_a, top_b)
    weight_a = jnp.exp(top_a - top)
    weight_b = jnp.exp(top_b - top)
    return (
        top,
        sum_a * weight_a + sum_b * weight_b,
        acc_a * weight_a[..., None] + acc_b * weight_b[..., None],
    )


def self_terms(query, key_new, value_new, slopes, scale):
    query = query.astype(jnp.float32)
    key_new = key_new.astype(jnp.float32)
    value_new = value_new.astype(jnp.float32)
    first = jnp.sum(query[0] * key_new[0], axis=-1) * scale
    cross = jnp.sum(query[1] * key_new[0], axis=-1) * scale - slopes
    second = jnp.sum(query[1] * key_new[1], axis=-1) * scale
    upper = jnp.maximum(cross, second)
    e_cross = jnp.exp(cross - upper)
    e_second = jnp.exp(second - upper)
    top = jnp.stack([first, upper])
    total = jnp.stack([jnp.ones_like(first), e_cross + e_second])
    acc = jnp.stack(
        [value_new[0], e_cross[..., None] * value_new[0] + e_second[..., None] * value_new[1]]
    )
    return (top, total, acc)


def body(
    queries,
    new_keys,
    new_values,
    cache_keys,
    cache_values,
    slopes,
    seg_blocks,
    request_row,
    out_weight,
    residual,
):
    heads = slopes.shape[0]
    width = queries.shape[2]
    hdim = width // heads
    requests = seg_blocks.shape[0]
    own_rows = queries.shape[1]
    blocks = cache_keys.shape[0] // BLK
    scale = 1.0 / math.sqrt(hdim)
    everyone = collect(queries, "seq", 1)
    place = lax.axis_index("seq")
    starts = jnp.cumsum(seg_blocks) - seg_blocks
    index = place * blocks + jnp.arange(blocks, dtype=jnp.int32)
    hit = (index[:, None] >= starts[None, :]) & (index[:, None] < (starts + seg_blocks)[None, :])
    live = jnp.any(hit, axis=1)
    block_row = jnp.sum(jnp.where(hit, request_row[None, :], 0), axis=1)
    first = jnp.sum(jnp.where(hit, starts[None, :], 0), axis=1)
    length = jnp.sum(jnp.where(hit, seg_blocks[None, :], 0), axis=1)
    base = length * BLK - (index - first) * BLK
    block_query = jnp.take(everyone, block_row, axis=1).reshape(2, blocks, heads, hdim)
    keys = cache_keys.reshape(blocks, BLK, heads, hdim)
    values = cache_values.reshape(blocks, BLK, heads, hdim)
    scores = (
        jnp.einsum("sbhd,bthd->bsht", block_query, keys, preferred_element_type=jnp.float32) * scale
    )
    dist = (
        base[:, None, None]
        + jnp.arange(2, dtype=jnp.int32)[None, :, None]
        - jnp.arange(BLK, dtype=jnp.int32)[None, None, :]
    ).astype(jnp.float32)
    scores = scores - slopes[None, None, :, None] * dist[:, :, None, :]
    top = jnp.max(scores, axis=-1)
    probs = jnp.exp(scores - top[..., None])
    total = jnp.sum(probs, axis=-1)
    acc = jnp.einsum(
        "bsht,bthd->bshd", probs.astype(jnp.bfloat16), values, preferred_element_type=jnp.float32
    )
    top = jnp.where(live[:, None, None], top, NEG)
    total = jnp.where(live[:, None, None], total, 0.0)
    acc = jnp.where(live[:, None, None, None], acc, 0.0)
    rowhot = (block_row[:, None] == jnp.arange(requests, dtype=jnp.int32)[None, :]) & live[:, None]
    tab_top = jnp.max(jnp.where(rowhot[:, :, None, None], top[:, None], NEG), axis=0).transpose(
        1, 0, 2
    )
    ratio = jnp.exp(top - jnp.take(tab_top, block_row, axis=1).transpose(1, 0, 2))
    onehot = rowhot.astype(jnp.float32)
    tab_sum = jnp.einsum("br,bsh->srh", onehot, ratio * total, precision=lax.Precision.HIGHEST)
    tab_acc = jnp.einsum(
        "br,bshd->srhd", onehot, ratio[..., None] * acc, precision=lax.Precision.HIGHEST
    )
    mine = self_terms(
        queries.reshape(2, own_rows, heads, hdim),
        new_keys.reshape(2, own_rows, heads, hdim),
        new_values.reshape(2, own_rows, heads, hdim),
        slopes,
        scale,
    )
    got_top, got_sum, got_acc = side_by_side(
        (tab_top[None], tab_sum[None], tab_acc[None]), "seq", 2, 0, 4
    )
    highest = jnp.max(got_top, axis=0)
    factor = jnp.exp(got_top - highest[None])
    gathered_sum = jnp.sum(got_sum * factor, axis=0)
    gathered_acc = jnp.sum(got_acc * factor[..., None], axis=0)
    top_own, sum_own, acc_own = combine((highest, gathered_sum, gathered_acc), mine)
    attended = (acc_own / sum_own[..., None]).astype(jnp.bfloat16).reshape(2, own_rows, width)
    projected = jnp.einsum(
        "srx,xy->sry", collect(attended, "seq", 1), out_weight, preferred_element_type=jnp.float32
    )
    summed = summed_on_arrival(projected.astype(jnp.bfloat16), "head", 1)
    return (residual.astype(jnp.float32) + summed).astype(jnp.bfloat16)


def solution(mesh):
    in_specs = (
        P(None, "seq", "head"),
        P(None, "seq", "head"),
        P(None, "seq", "head"),
        P("seq", "head"),
        P("seq", "head"),
        P("head"),
        P(),
        P(),
        P("head", "seq"),
        P(None, "head", "seq"),
    )
    out_specs = P(None, "head", "seq")
    return jax.shard_map(body, mesh=mesh, in_specs=in_specs, out_specs=out_specs, check_vma=False)
```

profile of v0, /device:TPU:1, one launch (start us, length us, event | category | flops | bytes accessed | tf_op | source)
XLA Modules:
  0.0 118.4 jit_solution(3140204100438308121)
XLA Ops:
  0.0 1.6 %broadcast_in_dim.144 = bf16[32,2,1,1792]{3,1,2,0:T(2,128)(2,1)} broadcast(bf16[2,1792]{1,0:T(2,128)(2,1)} %bitcast.154), dimensions={1,3} | broadcast | bytes 236544 | tf_op jit(solution)/shard_map/broadcast_in_dim | solution.py:16
  1.6 11.9 %all-to-all-start = ((bf16[32,2,1,1792]{3,1,2,0:T(2,128)(2,1)}), bf16[32,2,1,1792]{3,1,2,0:T(2,128)(2,1)S(1)}, u32[]{:S(2)}, u32[]{:S(2)}) async-start(bf16[32,2,1,1792]{3,1,2,0:T(2,128)(2,1)} %broadcast_in_dim.144), calls=%async_computation | async-start | bytes 458752 | tf_op jit(solution)/shard_map/all_to_all | solution.py:16
  13.5 0.7 convert_element_type.71
  14.2 0.7 copy.239
  15.1 0.7 sub.117
  15.8 0.2 fusion.66
  16.0 0.9 select_reduce_fusion.2
  17.0 7.4 %reshape.627 = bf16[8,128,14,128]{3,2,1,0:T(8,128)(2,1)} reshape(bf16[1024,1792]{1,0:T(8,128)(2,1)} %param.13) | data formatting | bytes 7340032 | tf_op jit(solution)/shard_map/reshape | solution.py:112
  24.4 7.4 %reshape.628 = bf16[8,128,14,128]{3,2,1,0:T(8,128)(2,1)} reshape(bf16[1024,1792]{1,0:T(8,128)(2,1)} %param.14) | data formatting | bytes 7340032 | tf_op jit(solution)/shard_map/reshape | solution.py:113
  32.1 0.2 copy.241
  32.3 0.7 gather_fusion
  33.1 4.3 %fusion.67 = (f32[8,2,14]{1,2,0:T(8,128)S(1)}, f32[8,2,14,128]{3,1,2,0:T(2,128)S(1)}) fusion(f32[8,2,128]{2,1,0:T(2,128)S(1)} %subtract_convert_fusion, f32[14]{0:T(128)S(1)} %copy-done.4, bf16[8,128,14,128]{3,2,1,0:T(8,128)(2,1)} %reshape.627, bf16[2,8,14,128]{3,1,2,0:T(8,128)(2,1)S(1)} %bitcast_select_fusion), kind=kOutput, calls=%fused_computation.111 | convolution fusion | flops 7454496 | bytes 3851192 | tf_op jit(solution)/shard_map/sbhd,bthd->bsht/dot_general | solution.py:115
  37.3 0.1 copy.246
  37.9 0.6 gather_fusion.1
  38.5 0.4 fusion.32
  39.2 0.3 convolution_bitcast_fusion.1
  39.4 0.2 copy.257
  39.7 3.3 %fusion.22 = f32[8,2,14,128]{3,1,2,0:T(2,128)S(1)} fusion(bf16[8,128,14,128]{3,2,1,0:T(8,128)(2,1)} %reshape.628, pred[8]{0:T(512)(128)(4,1)S(1)} %fusion.66, f32[8,2,14,128]{3,1,2,0:T(2,128)S(1)} %get-tuple-element.23, f32[8,2,14]{1,2,0:T(8,128)S(1)} %copy.252, f32[8,2,14]{1,2,0:T(8,128)S(1)} %get-tuple-element.22), kind=kOutput, calls=%fused_computation.16 | convolution fusion | flops 7454720 | bytes 3901192 | tf_op jit(solution)/shard_map/bsht,bthd->bshd/dot_general | solution.py:126
  43.0 0.5 convolution_bitcast_fusion
  43.5 0.2 copy.256
  43.7 0.5 pad_maximum_fusion
  44.3 1.7 %copy.258 = f32[1,2,32,14,130]{4,1,3,0,2:T(2,128)} copy(f32[1,2,32,14,130]{4,2,3,1,0:T(8,128)S(1)} %pad_maximum_fusion) | data formatting | bytes 931840 | tf_op jit(solution)/shard_map/concatenate | solution.py:32
  45.9 9.3 %all-to-all-start.1 = ((f32[1,2,32,14,130]{4,1,3,0,2:T(2,128)}), f32[1,2,32,14,130]{4,1,3,0,2:T(2,128)}, u32[]{:S(2)}, u32[]{:S(2)}) async-start(f32[1,2,32,14,130]{4,1,3,0,2:T(2,128)} %copy.258), calls=%async_computation.1 | async-start | bytes 1835008 | tf_op jit(solution)/shard_map/all_to_all | solution.py:35
  55.7 22.8 %all-to-all-done.1 = f32[1,2,32,14,130]{4,1,3,0,2:T(2,128)} async-done(((f32[1,2,32,14,130]{4,1,3,0,2:T(2,128)}), f32[1,2,32,14,130]{4,1,3,0,2:T(2,128)}, u32[]{:S(2)}, u32[]{:S(2)}) %all-to-all-start.1) | async-done | bytes 465952 | tf_op jit(solution)/shard_map/all_to_all | solution.py:35
  78.5 4.2 %copy.259 = f32[1,2,32,14,130]{2,1,4,3,0:T(2,128)S(1)} copy(f32[1,2,32,14,130]{4,1,3,0,2:T(2,128)} %all-to-all-done.1) | data formatting | bytes 931840 | tf_op jit(solution)/shard_map/all_to_all | solution.py:35
  83.0 0.2 fusion.38
  83.1 2.9 %fusion.4 = f32[2,14,128]{0,2,1:T(8,128)} fusion(f32[32,2,1,14,130]{0,1,4,3,2:T(2,128)S(1)} %bitcast.147, f32[32,2,14]{0,1,2:T(2,128)S(1)} %exponential_bitcast_fusion), kind=kLoop, calls=%fused_computation.7 | loop fusion | flops 225792 | bytes 476672 | tf_op jit(solution)/shard_map/reduce_sum | solution.py:155
  86.1 1.5 %copy.279 = f32[2,14,128]{2,0,1:T(2,128)S(1)} copy(f32[2,14,128]{0,2,1:T(8,128)} %fusion.4) | data formatting | bytes 28672
  88.1 16.3 %all_to_all.33 = bf16[32,2,1,1792]{3,1,2,0:T(2,128)(2,1)S(1)} all-to-all(bf16[32,2,1,1792]{3,1,2,0:T(2,128)(2,1)S(1)} %broadcast_in_dim.156), channel_id=1, replica_groups=mesh['seq'=32,'head'=8] {'seq'}, dimensions={0} | all-to-all | bytes 458752 | tf_op jit(solution)/shard_map/all_to_all | solution.py:16
  104.5 0.6 fusion.25
  105.1 12.7 %all_to_all.34 = bf16[8,2,4,448]{3,2,1,0:T(4,128)(2,1)S(1)} all-to-all(bf16[8,2,4,448]{3,2,1,0:T(4,128)(2,1)S(1)} %bitcast.149), channel_id=1, replica_groups=mesh['seq'=32,'head'=8] {'head'}, dimensions={0} | all-to-all | bytes 114688 | tf_op jit(solution)/shard_map/all_to_all | solution.py:47
  117.8 0.6 add_convert_fusion
  (55 shorter events, 2.7 us)
Async XLA Ops:
  0.0 104.5 %copy-start = (bf16[1792,448]{0,1:T(8,128)(2,1)S(1)}, bf16[1792,448]{0,1:T(8,128)(2,1)}, u32[]{:S(2)}) copy-start(bf16[1792,448]{0,1:T(8,128)(2,1)} %param.18) | copy-start | bytes 4816900
  1.6 30.4 %all-to-all-start = ((bf16[32,2,1,1792]{3,1,2,0:T(2,128)(2,1)}), bf16[32,2,1,1792]{3,1,2,0:T(2,128)(2,1)S(1)}, u32[]{:S(2)}, u32[]{:S(2)}) async-start(bf16[32,2,1,1792]{3,1,2,0:T(2,128)(2,1)} %broadcast_in_dim.144), calls=%async_computation | async-start | bytes 458752 | tf_op jit(solution)/shard_map/all_to_all | solution.py:16
  24.4 7.4 %copy-start.2 = (bf16[2,1,1792]{2,0,1:T(2,128)(2,1)S(1)}, bf16[2,1,1792]{2,0,1:T(2,128)(2,1)}, u32[]{:S(2)}) copy-start(bf16[2,1,1792]{2,0,1:T(2,128)(2,1)} %param.11) | copy-start | bytes 21508
  24.4 8.6 %copy-start.4 = (f32[14]{0:T(128)S(1)}, f32[14]{0:T(128)}, u32[]{:S(2)}) copy-start(f32[14]{0:T(128)} %param.15) | copy-start | bytes 172
  43.0 12.4 %copy-start.3 = (bf16[2,1,1792]{2,0,1:T(2,128)(2,1)S(1)}, bf16[2,1,1792]{2,0,1:T(2,128)(2,1)}, u32[]{:S(2)}) copy-start(bf16[2,1,1792]{2,0,1:T(2,128)(2,1)} %param.12) | copy-start | bytes 21508
  45.9 32.5 %all-to-all-start.1 = ((f32[1,2,32,14,130]{4,1,3,0,2:T(2,128)}), f32[1,2,32,14,130]{4,1,3,0,2:T(2,128)}, u32[]{:S(2)}, u32[]{:S(2)}) async-start(f32[1,2,32,14,130]{4,1,3,0,2:T(2,128)} %copy.258), calls=%async_computation.1 | async-start | bytes 1835008 | tf_op jit(solution)/shard_map/all_to_all | solution.py:35
  82.7 35.2 %copy-start.1 = (bf16[2,4,448]{2,1,0:T(4,128)(2,1)S(1)}, bf16[2,4,448]{2,1,0:T(4,128)(2,1)}, u32[]{:S(2)}) copy-start(bf16[2,4,448]{2,1,0:T(4,128)(2,1)} %param.19) | copy-start | bytes 21508
where the time goes:
time: 119 us; the launch traced here: 118 us
  blocking collectives  29 us (24%)
  local copies, waits for them, and re-layouts  27.8 us (23%)
  waiting for transfers between devices  22.8 us (19%)
  starting transfers between devices  21.2 us (18%)
  matrix products  8.86 us (7%)
  other arithmetic  8.55 us (7%)
    all_to_all x1, waiting for transfers between devices, side_by_side(): lax.all_to_all(both, axis, split_axis=split_dim, concat_axis=concat_dim,...  22.8 us
    all_to_all x1, blocking collectives, from_everyone(): lax.all_to_all(jnp.broadcast_to(x[None], (peers, *x.shape)), axis, 0, 0,...  16.3 us
    all_to_all x1, blocking collectives, summed_on_arrival(): blocks = lax.all_to_all(split_up(x, dim, peers), axis, 0, 0, tiled=True)  12.7 us
    all_to_all x1, starting transfers between devices, from_everyone(): lax.all_to_all(jnp.broadcast_to(x[None], (peers, *x.shape)), axis, 0, 0,...  11.9 us
    all_to_all x1, starting transfers between devices, side_by_side(): lax.all_to_all(both, axis, split_axis=split_dim, concat_axis=concat_dim,...  9.33 us
    reshape x1, local copies, waits for them, and re-layouts, body(): values = cache_values.reshape(blocks, BLK, heads, hdim)  7.41 us
    reshape x1, local copies, waits for them, and re-layouts, body(): keys = cache_keys.reshape(blocks, BLK, heads, hdim)  7.38 us
    dot_general x1, matrix products, body(): jnp.einsum('sbhd,bthd->bsht', block_query, keys, preferred_element_type=j...  4.26 us
  transfers between devices with their start and end apart: 2, of which 1 were waited for; matrix products, arithmetic and copies ran while one was open for 16% of the time, Pallas kernels for 0%

commit v1 on v0

v1 whole, which is shorter than its diff:
```python
import functools
import math

import jax
import jax.numpy as jnp
from jax import lax
from jax.experimental import pallas as pl
from jax.experimental.pallas import tpu as pltpu
from jax.sharding import PartitionSpec as P

BLK = 128
NEG = -1e30
STEPS = 2
GROUP = 16
STATS = 128
VMEM_LIMIT = 48 * 1024 * 1024


def iota(shape, dim):
    return lax.broadcasted_iota(jnp.int32, shape, dim)


def head_mask(width, hdim):
    return iota((GROUP, width), 1) // hdim == iota((GROUP, width), 0)


def by_step(x, mask):
    rows = [
        jnp.sum(jnp.where(mask, x[s * GROUP : (s + 1) * GROUP], 0.0), axis=0, keepdims=True)
        for s in range(STEPS)
    ]
    return jnp.concatenate(rows, axis=0)


def in_bf16_parts(x, parts):
    out = []
    for _ in range(parts):
        part = x.astype(jnp.bfloat16).astype(jnp.float32)
        out.append(part)
        x = x - part
    return out


def attend_kernel(blocks, hdim, meta, slopes, query, keys, values, out, kbuf, vbuf, ksem, vsem):
    width = kbuf.shape[1]
    scale = 1.0 / math.sqrt(hdim)
    kcopy, vcopy = [], []
    for b in range(blocks):
        rows = pl.ds(b * BLK, BLK)
        kcopy.append(pltpu.make_async_copy(keys.at[rows], kbuf.at[rows], ksem.at[b]))
        vcopy.append(pltpu.make_async_copy(values.at[rows], vbuf.at[rows], vsem.at[b]))
    for copy in kcopy:
        copy.start()
    for copy in vcopy:
        copy.start()

    mask = head_mask(width, hdim)
    lane = iota((STEPS, STATS), 1)
    empty = jnp.concatenate(
        [jnp.zeros((STEPS, width), jnp.float32), jnp.where(lane < GROUP, NEG, 0.0)], axis=1
    ).astype(out.dtype)
    for r in range(out.shape[0]):
        out[r] = empty

    shape = (STEPS * GROUP, BLK)
    when = iota(shape, 0) // GROUP - iota(shape, 1)
    slope = slopes[...]
    scores = []
    for b in range(blocks):
        q = query[meta[0, b]].astype(jnp.float32)
        spread = jnp.concatenate(
            [jnp.where(mask, q[s : s + 1], 0.0) for s in range(STEPS)], axis=0
        ).astype(jnp.bfloat16)
        kcopy[b].wait()
        raw = lax.dot_general(
            spread,
            kbuf[b * BLK : (b + 1) * BLK],
            (((1,), (1,)), ((), ())),
            preferred_element_type=jnp.float32,
        )
        dist = (when + meta[1, b]).astype(jnp.float32)
        scores.append(raw * scale - slope * dist)

    joined = [meta[3, b] == 1 for b in range(blocks)]
    tops = [jnp.max(x, axis=1, keepdims=True) for x in scores]
    for b in range(1, blocks):
        tops[b] = jnp.where(joined[b], jnp.maximum(tops[b], tops[b - 1]), tops[b])
    for b in range(blocks - 2, -1, -1):
        tops[b] = jnp.where(joined[b + 1], tops[b + 1], tops[b])
    probs = [jnp.exp(x - top) for x, top in zip(scores, tops)]
    totals = [jnp.sum(p, axis=1, keepdims=True) for p in probs]
    for b in range(1, blocks):
        totals[b] = totals[b] + jnp.where(joined[b], totals[b - 1], 0.0)

    offset = iota((STEPS * GROUP, STATS), 1) - iota((STEPS * GROUP, STATS), 0) % GROUP
    every = jnp.full((GROUP, STATS), True)
    acc = None
    for b in range(blocks):
        vcopy[b].wait()
        full = jnp.dot(
            probs[b].astype(jnp.bfloat16),
            vbuf[b * BLK : (b + 1) * BLK],
            preferred_element_type=jnp.float32,
        )
        mine = by_step(full, mask)
        acc = mine if acc is None else mine + jnp.where(joined[b], acc, 0.0)
        stats = jnp.zeros((STEPS * GROUP, STATS), jnp.float32)
        for k, part in enumerate(in_bf16_parts(tops[b], 3) + in_bf16_parts(totals[b], 2)):
            stats = jnp.where(offset == k * GROUP, part, stats)
        row = jnp.concatenate([acc, by_step(stats, every)], axis=1).astype(out.dtype)

        @pl.when(meta[2, b] == 1)
        def _():
            out[meta[0, b]] = row


def own_kernel(heads, hdim, query, key, value, slopes, stats, acc):
    scale = 1.0 / math.sqrt(hdim)
    q = query[...].astype(jnp.float32)
    k = key[...].astype(jnp.float32)
    v = value[...].astype(jnp.float32)
    q0, q1 = q[0:1], q[1:2]
    k0, k1 = k[0:1], k[1:2]
    v0, v1 = v[0:1], v[1:2]
    lane = iota((1, STATS), 1)
    tops = [jnp.zeros((1, STATS), jnp.float32) for _ in range(STEPS)]
    sums = [jnp.zeros((1, STATS), jnp.float32) for _ in range(STEPS)]
    rows = [[], []]
    products = jnp.concatenate([q0 * k0, q1 * k0, q1 * k1], axis=0)
    for h in range(heads):
        at = slice(h * hdim, (h + 1) * hdim)
        dots = jnp.sum(products[:, at], axis=1, keepdims=True) * scale
        first = dots[0:1]
        cross = dots[1:2] - slopes[h : h + 1]
        second = dots[2:3]
        upper = jnp.maximum(cross, second)
        e_cross = jnp.exp(cross - upper)
        e_second = jnp.exp(second - upper)
        tops[0] = jnp.where(lane == h, first, tops[0])
        tops[1] = jnp.where(lane == h, upper, tops[1])
        sums[0] = jnp.where(lane == h + GROUP, 1.0, sums[0])
        sums[1] = jnp.where(lane == h + GROUP, e_cross + e_second, sums[1])
        rows[0].append(v0[:, at])
        rows[1].append(e_cross * v0[:, at] + e_second * v1[:, at])
    stats[...] = jnp.concatenate([tops[0] + sums[0], tops[1] + sums[1]], axis=0)
    acc[...] = jnp.concatenate([jnp.concatenate(r, axis=1) for r in rows], axis=0)


def left(x, lanes):
    return pltpu.roll(x, x.shape[1] - lanes, 1) if lanes else x


def join_kernel(heads, hdim, parts, own_stats, own_acc, out):
    width = heads * hdim
    count = parts.shape[0]
    stats = parts[:, width : width + STATS].astype(jnp.float32)
    top = (stats + left(stats, GROUP)) + left(stats, 2 * GROUP)
    total = left(stats, 3 * GROUP) + left(stats, 4 * GROUP)
    step = iota((count, STATS), 0) % STEPS
    lane = iota((count, STATS), 1)
    real = lane < heads
    top = jnp.where(real, top, NEG)
    total = jnp.where(real, total, 0.0)
    own = own_stats[...]
    own_real = iota(own.shape, 1) < heads
    own_top = jnp.where(own_real, own, 0.0)
    own_total = jnp.where(own_real, left(own, GROUP), 1.0)
    highest = [
        jnp.maximum(
            jnp.max(jnp.where(step == s, top, NEG), axis=0, keepdims=True), own_top[s : s + 1]
        )
        for s in range(STEPS)
    ]
    weight = jnp.exp(top - jnp.where(step == 0, highest[0], highest[1]))
    weight = jnp.where(real, weight, 0.0)
    own_weight = jnp.exp(own_top - jnp.concatenate(highest, axis=0))
    weighted = weight * total
    sums = [
        jnp.sum(jnp.where(step == s, weighted, 0.0), axis=0, keepdims=True) for s in range(STEPS)
    ]
    inverse = 1.0 / (jnp.concatenate(sums, axis=0) + own_weight * own_total)
    own_weight = own_weight * inverse
    weight = weight * jnp.where(step == 0, inverse[0:1], inverse[1:2])
    placed = jnp.where(step == 0, weight, 0.0) + pltpu.roll(
        jnp.where(step == 1, weight, 0.0), GROUP, 1
    )
    high, low = in_bf16_parts(placed, 2)
    both = high + pltpu.roll(low, STEPS * GROUP, 1)
    both = both.T[: 2 * STEPS * GROUP].astype(jnp.bfloat16)
    full = jnp.dot(both, parts[:, :width], preferred_element_type=jnp.float32)
    full = full[: STEPS * GROUP] + full[STEPS * GROUP :]
    acc = by_step(full, head_mask(width, hdim))
    mine = own_acc[...]
    mine = jnp.concatenate(
        [mine[:, h * hdim : (h + 1) * hdim] * own_weight[:, h : h + 1] for h in range(heads)],
        axis=1,
    )
    attended = (acc + mine).astype(out.dtype)
    for r in range(out.shape[0]):
        out[r] = attended


def copies_kernel(x, out):
    for r in range(out.shape[0]):
        out[r] = x[...]


def on_device(kernel, out_shape, in_spaces, **more):
    return pl.pallas_call(
        kernel,
        out_shape=out_shape,
        in_specs=[pl.BlockSpec(memory_space=m) for m in in_spaces],
        compiler_params=pltpu.CompilerParams(vmem_limit_bytes=VMEM_LIMIT),
        **more,
    )


def block_table(seg_blocks, request_row, blocks):
    requests = seg_blocks.shape[0]
    order = jnp.arange(requests, dtype=jnp.int32)
    starts = jnp.sum(jnp.where(order[None, :] < order[:, None], seg_blocks[None, :], 0), axis=1)
    index = lax.axis_index("seq") * blocks + jnp.arange(blocks, dtype=jnp.int32)
    ends = starts + seg_blocks
    hit = (index[:, None] >= starts[None, :]) & (index[:, None] < ends[None, :])
    pick = lambda x: jnp.sum(jnp.where(hit, x[None, :], 0), axis=1)
    row = pick(request_row)
    base = pick(ends) * BLK - index * BLK
    live = jnp.any(hit, axis=1)
    before = hit & (index[:, None] > starts[None, :]) & (jnp.arange(blocks)[:, None] > 0)
    joined = jnp.any(before, axis=1)
    return jnp.stack([row, base, live.astype(jnp.int32), joined.astype(jnp.int32)])


def body(
    queries,
    new_keys,
    new_values,
    cache_keys,
    cache_values,
    slopes,
    seg_blocks,
    request_row,
    out_weight,
    residual,
):
    heads = slopes.shape[0]
    width = queries.shape[2]
    hdim = width // heads
    peers = lax.axis_size("seq")
    groups = lax.axis_size("head")
    blocks = cache_keys.shape[0] // BLK
    vmem, smem, anywhere = pltpu.VMEM, pltpu.SMEM, pl.ANY
    own_query = queries.reshape(STEPS, width)

    copies = on_device(
        copies_kernel, jax.ShapeDtypeStruct((peers, STEPS, width), jnp.bfloat16), [vmem]
    )(own_query)
    everyone = lax.all_to_all(copies, "seq", 0, 0, tiled=True)

    table = block_table(seg_blocks, request_row, blocks)
    column = jnp.tile(jnp.pad(slopes, (0, GROUP - heads)), STEPS)[:, None]
    own_stats, own_acc = on_device(
        functools.partial(own_kernel, heads, hdim),
        (
            jax.ShapeDtypeStruct((STEPS, STATS), jnp.float32),
            jax.ShapeDtypeStruct((STEPS, width), jnp.float32),
        ),
        [vmem] * 4,
    )(own_query, new_keys.reshape(STEPS, width), new_values.reshape(STEPS, width), column)

    partials = on_device(
        functools.partial(attend_kernel, blocks, hdim),
        jax.ShapeDtypeStruct((peers, STEPS, width + STATS), jnp.bfloat16),
        [smem, vmem, vmem, anywhere, anywhere],
        scratch_shapes=[
            pltpu.VMEM(cache_keys.shape, jnp.bfloat16),
            pltpu.VMEM(cache_values.shape, jnp.bfloat16),
            pltpu.SemaphoreType.DMA((blocks,)),
            pltpu.SemaphoreType.DMA((blocks,)),
        ],
    )(table, column, everyone, cache_keys, cache_values)
    arrived = lax.all_to_all(partials, "seq", 0, 0, tiled=True)

    attended = on_device(
        functools.partial(join_kernel, heads, hdim),
        jax.ShapeDtypeStruct((peers, STEPS, width), jnp.bfloat16),
        [vmem] * 3,
    )(arrived.reshape(peers * STEPS, width + STATS), own_stats, own_acc)
    rows = lax.all_to_all(attended, "seq", 0, 0, tiled=True).reshape(peers * STEPS, width)

    projected = jnp.dot(rows, out_weight, preferred_element_type=jnp.float32)
    projected = projected.astype(jnp.bfloat16).reshape(groups, -1, out_weight.shape[1])
    shares = lax.all_to_all(projected, "head", 0, 0, tiled=True)
    summed = jnp.sum(shares.astype(jnp.float32), axis=0)
    summed = summed.reshape(-1, STEPS, out_weight.shape[1]).transpose(1, 0, 2)
    return (residual.astype(jnp.float32) + summed).astype(jnp.bfloat16)


def solution(mesh):
    in_specs = (
        P(None, "seq", "head"),
        P(None, "seq", "head"),
        P(None, "seq", "head"),
        P("seq", "head"),
        P("seq", "head"),
        P("head"),
        P(),
        P(),
        P("head", "seq"),
        P(None, "head", "seq"),
    )
    out_specs = P(None, "head", "seq")
    return jax.shard_map(body, mesh=mesh, in_specs=in_specs, out_specs=out_specs, check_vma=False)
```

time: 119 us -> 79.3 us (0.67)
  local copies, waits for them, and re-layouts: 27.8 us -> 3.82 us
  Pallas kernels: 0 us -> 9.92 us
  matrix products: 8.86 us -> 0.58 us
  waiting for transfers between devices: 22.8 us -> 17.4 us
  other arithmetic: 8.55 us -> 3.18 us
  starting transfers between devices: 21.2 us -> 16.4 us
  blocking collectives: 29 us -> 27.6 us
    reshape x5 -> x3, local copies, waits for them, and re-layouts: 15.1 us -> 0.2 us  [the longest x1 0.09 us: body(): arrived.reshape(peers * STEPS, width + STATS)]
    pallas_call x0 -> x4, Pallas kernels: none -> 9.92 us  [the longest x1 8.41 us: body(): on_device(functools.partial(attend_kernel, blocks, hdim), jax.ShapeDtypeS...]
    dot_general x5 -> x1, matrix products: 8.86 us -> 0.58 us  [body(): projected = jnp.dot(rows, out_weight, preferred_element_type=jnp.float32)]
    all_to_all x2, waiting for transfers between devices: 22.8 us -> 17.4 us  [the longest x1 9.98 us: body(): arrived = lax.all_to_all(partials, 'seq', 0, 0, tiled=True)]
    all_to_all x2, starting transfers between devices: 21.2 us -> 16.4 us  [the longest x1 11.9 us: body(): everyone = lax.all_to_all(copies, 'seq', 0, 0, tiled=True)]
    all_to_all x2 -> x0, local copies, waits for them, and re-layouts: 4.21 us -> none  [the longest x1 4.18 us: side_by_side(): lax.all_to_all(both, axis, split_axis=split_dim, concat_axis=concat_dim,...]
    reduce_sum x7 -> x3, other arithmetic: 4.6 us -> 1.65 us  [the longest x1 0.86 us: block_table(): pick = lambda x: jnp.sum(jnp.where(hit, x[None, :], 0), axis=1)]
    broadcast_in_dim x2 -> x0, local copies, waits for them, and re-layouts: 1.75 us -> none  [from_everyone(): jnp.broadcast_to(x[None], (peers, *x.shape))]
  transfers between devices with their start and end apart: 2 -> 2, of which waited for: 1 -> 2; matrix products, arithmetic and copies ran while one was open for 16% -> 4% of each run, Pallas kernels for 0% -> 0%
where the time goes in v1:
time: 79.3 us; the launch traced here: 78.9 us
  blocking collectives  27.6 us (35%)
  waiting for transfers between devices  17.4 us (22%)
  starting transfers between devices  16.4 us (21%)
  Pallas kernels  9.92 us (13%)
  local copies, waits for them, and re-layouts  3.82 us (5%)
  other arithmetic  3.18 us (4%)
    all_to_all x1, blocking collectives, body(): lax.all_to_all(attended, 'seq', 0, 0, tiled=True)  14.1 us
    all_to_all x1, blocking collectives, body(): shares = lax.all_to_all(projected, 'head', 0, 0, tiled=True)  13.5 us
    all_to_all x1, starting transfers between devices, body(): everyone = lax.all_to_all(copies, 'seq', 0, 0, tiled=True)  11.9 us
    all_to_all x1, waiting for transfers between devices, body(): arrived = lax.all_to_all(partials, 'seq', 0, 0, tiled=True)  9.98 us
    pallas_call x1, Pallas kernels, body(): on_device(functools.partial(attend_kernel, blocks, hdim), jax.ShapeDtypeS...  8.41 us
    all_to_all x1, waiting for transfers between devices, body(): everyone = lax.all_to_all(copies, 'seq', 0, 0, tiled=True)  7.39 us
    all_to_all x1, starting transfers between devices, body(): arrived = lax.all_to_all(partials, 'seq', 0, 0, tiled=True)  4.5 us
    unnamed x14, local copies, waits for them, and re-layouts  2.87 us
  transfers between devices with their start and end apart: 2, of which 2 were waited for; matrix products, arithmetic and copies ran while one was open for 4% of the time, Pallas kernels for 0%

profile of v1, /device:TPU:1, one launch (start us, length us, event | category | flops | bytes accessed | tf_op | source)
XLA Modules:
  0.0 78.9 jit_solution(10996970186705985941)
XLA Ops:
  0.0 0.0 copy-start
  0.0 0.0 copy-start.2
  0.0 0.8 %copy-done.2 = bf16[2,1,1792]{2,0,1:T(2,128)(2,1)S(1)} copy-done((bf16[2,1,1792]{2,0,1:T(2,128)(2,1)S(1)}, bf16[2,1,1792]{2,0,1:T(2,128)(2,1)}, u32[]{:S(2)}) %copy-start.2) | copy-done | bytes 7192
  0.8 0.7 shard_map.100
  1.5 11.9 %all-to-all-start = ((bf16[32,2,1792]{2,1,0:T(2,128)(2,1)}), bf16[32,2,1792]{2,1,0:T(2,128)(2,1)S(1)}, u32[]{:S(2)}, u32[]{:S(2)}) async-start(bf16[32,2,1792]{2,1,0:T(2,128)(2,1)} %shard_map.100), calls=%async_computation | async-start | bytes 458752 | tf_op jit(solution)/shard_map/all_to_all | solution.py:258
  13.4 0.8 select_reduce_fusion
  14.2 0.7 add.31
  14.8 0.9 %select_reduce_fusion.2 = (s32[8]{0:T(128)S(1)}, s32[8]{0:T(128)S(1)}) fusion(s32[32]{0:T(128)} %param.17, s32[32]{0:T(128)S(1)} %add.31, s32[32]{0:T(128)S(1)} %select_reduce_fusion, s32[8]{0:T(128)S(1)} %iota_add_fusion), kind=kLoop, calls=%fused_computation.8 | loop fusion | flops 1776 | bytes 480 | tf_op jit(solution)/shard_map/reduce_sum | solution.py:225
  15.7 0.7 pad.4
  16.4 0.1 broadcast_in_dim_tile.4.slopes
  16.5 0.2 fusion.2
  16.7 7.4 %all-to-all-done.query = bf16[32,2,1792]{2,1,0:T(2,128)(2,1)S(1)} async-done(((bf16[32,2,1792]{2,1,0:T(2,128)(2,1)}), bf16[32,2,1792]{2,1,0:T(2,128)(2,1)S(1)}, u32[]{:S(2)}, u32[]{:S(2)}) %all-to-all-start) | async-done | bytes 229408 | tf_op jit(solution)/shard_map/all_to_all | solution.py:258
  24.1 0.0 copy-start.1
  24.1 2.0 %copy-done.1 = bf16[1024,1792]{1,0:T(8,128)(2,1)S(1)} copy-done((bf16[1024,1792]{1,0:T(8,128)(2,1)S(1)}, bf16[1024,1792]{1,0:T(8,128)(2,1)}, u32[]{:S(2)}) %copy-start.1) | copy-done | bytes 3670040
  26.2 0.0 copy-start.3
  26.2 8.4 %shard_map.101 = bf16[32,2,1920]{2,1,0:T(2,128)(2,1)} custom-call(s32[4,8]{1,0:T(4,128)S(1)} %pad_add_fusion.meta, f32[32,1]{1,0:T(8,128)S(1)} %broadcast_in_dim_tile.4.slopes, bf16[32,2,1792]{2,1,0:T(2,128)(2,1)S(1)} %all-to-all-done.query, bf16[1024,1792]{1,0:T(8,128)(2,1)S(1)} %copy-done.1, bf16[1024,1792]{1,0:T(8,128)(2,1)} %values.1), custom_call_target="tpu_custom_call" | custom-call | tf_op jit(solution)/shard_map/pallas_call | solution.py:271
  34.6 4.5 %all-to-all-start.1 = ((bf16[32,2,1920]{2,1,0:T(2,128)(2,1)}), bf16[32,2,1920]{2,1,0:T(2,128)(2,1)S(1)}, u32[]{:S(2)}, u32[]{:S(2)}) async-start(bf16[32,2,1920]{2,1,0:T(2,128)(2,1)} %shard_map.101), calls=%async_computation.1 | async-start | bytes 491520 | tf_op jit(solution)/shard_map/all_to_all | solution.py:282
  39.1 0.0 copy-done.3
  39.1 0.0 copy-done.4
  39.1 0.0 copy-done.5
  39.1 0.3 shard_map.102
  39.4 10.0 %all-to-all-done.1 = bf16[32,2,1920]{2,1,0:T(2,128)(2,1)S(1)} async-done(((bf16[32,2,1920]{2,1,0:T(2,128)(2,1)}), bf16[32,2,1920]{2,1,0:T(2,128)(2,1)S(1)}, u32[]{:S(2)}, u32[]{:S(2)}) %all-to-all-start.1) | async-done | bytes 245792 | tf_op jit(solution)/shard_map/all_to_all | solution.py:282
  49.4 0.1 reshape.76.parts
  49.4 0.6 shard_map.103
  50.0 0.0 copy-start.6
  50.0 14.1 %all_to_all.20 = bf16[32,2,1792]{2,1,0:T(2,128)(2,1)S(1)} all-to-all(bf16[32,2,1792]{2,1,0:T(2,128)(2,1)S(1)} %shard_map.103), channel_id=1, replica_groups=mesh['seq'=32,'head'=8] {'seq'}, dimensions={0} | all-to-all | bytes 458752 | tf_op jit(solution)/shard_map/all_to_all | solution.py:289
  64.1 0.1 reshape.79
  64.2 0.0 copy-done
  64.2 0.6 fusion
  64.8 13.5 %all_to_all.21 = bf16[8,8,448]{2,1,0:T(8,128)(2,1)S(1)} all-to-all(bf16[8,8,448]{2,1,0:T(8,128)(2,1)S(1)} %fusion), channel_id=1, replica_groups=mesh['seq'=32,'head'=8] {'head'}, dimensions={0} | all-to-all | bytes 114688 | tf_op jit(solution)/shard_map/all_to_all | solution.py:293
  78.3 0.0 copy-done.6
  78.3 0.6 fusion.1
  (10 shorter events, 0.1 us)
Async XLA Ops:
  0.0 64.2 %copy-start = (bf16[1792,448]{0,1:T(8,128)(2,1)S(1)}, bf16[1792,448]{0,1:T(8,128)(2,1)}, u32[]{:S(2)}) copy-start(bf16[1792,448]{0,1:T(8,128)(2,1)} %param.18) | copy-start | bytes 4816900
  0.0 0.8 %copy-start.2 = (bf16[2,1,1792]{2,0,1:T(2,128)(2,1)S(1)}, bf16[2,1,1792]{2,0,1:T(2,128)(2,1)}, u32[]{:S(2)}) copy-start(bf16[2,1,1792]{2,0,1:T(2,128)(2,1)} %param.10) | copy-start | bytes 21508
  1.5 22.6 %all-to-all-start = ((bf16[32,2,1792]{2,1,0:T(2,128)(2,1)}), bf16[32,2,1792]{2,1,0:T(2,128)(2,1)S(1)}, u32[]{:S(2)}, u32[]{:S(2)}) async-start(bf16[32,2,1792]{2,1,0:T(2,128)(2,1)} %shard_map.100), calls=%async_computation | async-start | bytes 458752 | tf_op jit(solution)/shard_map/all_to_all | solution.py:258
  24.1 2.0 %copy-start.1 = (bf16[1024,1792]{1,0:T(8,128)(2,1)S(1)}, bf16[1024,1792]{1,0:T(8,128)(2,1)}, u32[]{:S(2)}) copy-start(bf16[1024,1792]{1,0:T(8,128)(2,1)} %keys.1) | copy-start | bytes 11010052
  26.2 12.9 %copy-start.3 = (bf16[2,1,1792]{2,0,1:T(2,128)(2,1)S(1)}, bf16[2,1,1792]{2,0,1:T(2,128)(2,1)}, u32[]{:S(2)}) copy-start(bf16[2,1,1792]{2,0,1:T(2,128)(2,1)} %param.10) | copy-start | bytes 21508
  26.2 12.9 %copy-start.4 = (bf16[2,1,1792]{2,0,1:T(2,128)(2,1)S(1)}, bf16[2,1,1792]{2,0,1:T(2,128)(2,1)}, u32[]{:S(2)}) copy-start(bf16[2,1,1792]{2,0,1:T(2,128)(2,1)} %param.11) | copy-start | bytes 21508
  26.2 12.9 %copy-start.5 = (bf16[2,1,1792]{2,0,1:T(2,128)(2,1)S(1)}, bf16[2,1,1792]{2,0,1:T(2,128)(2,1)}, u32[]{:S(2)}) copy-start(bf16[2,1,1792]{2,0,1:T(2,128)(2,1)} %param.12) | copy-start | bytes 21508
  34.6 14.8 %all-to-all-start.1 = ((bf16[32,2,1920]{2,1,0:T(2,128)(2,1)}), bf16[32,2,1920]{2,1,0:T(2,128)(2,1)S(1)}, u32[]{:S(2)}, u32[]{:S(2)}) async-start(bf16[32,2,1920]{2,1,0:T(2,128)(2,1)} %shard_map.101), calls=%async_computation.1 | async-start | bytes 491520 | tf_op jit(solution)/shard_map/all_to_all | solution.py:282
  50.0 28.3 %copy-start.6 = (bf16[2,4,448]{2,1,0:T(4,128)(2,1)S(1)}, bf16[2,4,448]{2,1,0:T(4,128)(2,1)}, u32[]{:S(2)}) copy-start(bf16[2,4,448]{2,1,0:T(4,128)(2,1)} %param.19) | copy-start | bytes 21508

commit v2 on v1

--- a/solution.py
+++ b/solution.py
@@ -13,7 +13,7 @@
 STEPS = 2
 GROUP = 16
 STATS = 128
-VMEM_LIMIT = 48 * 1024 * 1024
+MIB = 1024 * 1024
 
 
 def iota(shape, dim):
@@ -41,19 +41,24 @@
     return out
 
 
-def attend_kernel(blocks, hdim, meta, slopes, query, keys, values, out, kbuf, vbuf, ksem, vsem):
-    width = kbuf.shape[1]
+def left(x, lanes):
+    return pltpu.roll(x, x.shape[1] - lanes, 1) if lanes else x
+
+
+def attend_kernel(
+    blocks, hdim, meta, slopes, query, own_stats, keys, values, out, kbuf, vbuf, sems
+):
+    width = keys.shape[1]
+    per = STEPS * GROUP
+    packs = BLK // per
     scale = 1.0 / math.sqrt(hdim)
-    kcopy, vcopy = [], []
-    for b in range(blocks):
-        rows = pl.ds(b * BLK, BLK)
-        kcopy.append(pltpu.make_async_copy(keys.at[rows], kbuf.at[rows], ksem.at[b]))
-        vcopy.append(pltpu.make_async_copy(values.at[rows], vbuf.at[rows], vsem.at[b]))
-    for copy in kcopy:
+    copies = []
+    for i, (src, dst) in enumerate(((keys, kbuf), (values, vbuf))):
+        for b in range(blocks):
+            rows = pl.ds(b * BLK, BLK)
+            copies.append(pltpu.make_async_copy(src.at[rows], dst.at[rows], sems.at[i, b]))
+    for copy in copies:
         copy.start()
-    for copy in vcopy:
-        copy.start()
-
     mask = head_mask(width, hdim)
     lane = iota((STEPS, STATS), 1)
     empty = jnp.concatenate(
@@ -62,56 +67,87 @@
     for r in range(out.shape[0]):
         out[r] = empty
 
-    shape = (STEPS * GROUP, BLK)
-    when = iota(shape, 0) // GROUP - iota(shape, 1)
+    raw = []
+    for g in range(blocks // packs):
+        spread = []
+        for b in range(g * packs, (g + 1) * packs):
+            q = query[meta[0, b]].astype(jnp.float32)
+            for s in range(STEPS):
+                spread.append(jnp.where(mask, q[s : s + 1], 0.0).astype(jnp.bfloat16))
+        for b in range(g * packs, (g + 1) * packs):
+            copies[b].wait()
+        raw.append(
+            lax.dot_general(
+                kbuf[g * packs * BLK : (g + 1) * packs * BLK],
+                jnp.concatenate(spread, axis=0),
+                (((1,), (1,)), ((), ())),
+                preferred_element_type=jnp.float32,
+            )
+        )
+
+    pack = iota((BLK, BLK), 1) // per
+    when = (iota((BLK, BLK), 1) % per) // GROUP - iota((BLK, BLK), 0)
     slope = slopes[...]
+    joined = [meta[3, b] == 1 for b in range(blocks)]
     scores = []
-    for b in range(blocks):
-        q = query[meta[0, b]].astype(jnp.float32)
-        spread = jnp.concatenate(
-            [jnp.where(mask, q[s : s + 1], 0.0) for s in range(STEPS)], axis=0
-        ).astype(jnp.bfloat16)
-        kcopy[b].wait()
-        raw = lax.dot_general(
-            spread,
-            kbuf[b * BLK : (b + 1) * BLK],
-            (((1,), (1,)), ((), ())),
-            preferred_element_type=jnp.float32,
-        )
-        dist = (when + meta[1, b]).astype(jnp.float32)
-        scores.append(raw * scale - slope * dist)
-
-    joined = [meta[3, b] == 1 for b in range(blocks)]
-    tops = [jnp.max(x, axis=1, keepdims=True) for x in scores]
+    tops = []
+    for g in range(blocks // packs):
+        for k in range(packs):
+            b = g * packs + k
+            tile = raw[g][k * BLK : (k + 1) * BLK]
+            base = meta[1, b]
+            x = tile if k == 0 else jnp.where(pack == k, tile, x)
+            dist = when + base if k == 0 else jnp.where(pack == k, when + base, dist)
+        x = x * scale - slope * dist.astype(jnp.float32)
+        scores.append(x)
+        top = jnp.max(x, axis=0, keepdims=True)
+        tops += [left(top, k * per) for k in range(packs)]
     for b in range(1, blocks):
         tops[b] = jnp.where(joined[b], jnp.maximum(tops[b], tops[b - 1]), tops[b])
     for b in range(blocks - 2, -1, -1):
         tops[b] = jnp.where(joined[b + 1], tops[b + 1], tops[b])
-    probs = [jnp.exp(x - top) for x, top in zip(scores, tops)]
-    totals = [jnp.sum(p, axis=1, keepdims=True) for p in probs]
+
+    place = iota((1, BLK), 1) // per
+    totals = []
+    weights = []
+    for g in range(blocks // packs):
+        top = tops[g * packs]
+        for k in range(1, packs):
+            top = jnp.where(place == k, pltpu.roll(tops[g * packs + k], k * per, 1), top)
+        probs = jnp.exp(scores[g] - top)
+        total = jnp.sum(probs, axis=0, keepdims=True)
+        totals += [left(total, k * per) for k in range(packs)]
+        weights.append(probs.T.astype(jnp.bfloat16))
     for b in range(1, blocks):
         totals[b] = totals[b] + jnp.where(joined[b], totals[b - 1], 0.0)
 
-    offset = iota((STEPS * GROUP, STATS), 1) - iota((STEPS * GROUP, STATS), 0) % GROUP
-    every = jnp.full((GROUP, STATS), True)
+    parts = in_bf16_parts(jnp.concatenate(tops, axis=0), 3)
+    parts += in_bf16_parts(jnp.concatenate(totals, axis=0), 2)
+    field = iota((blocks, STATS), 1) // GROUP
+    stats = []
+    for s in range(STEPS):
+        row = jnp.zeros((blocks, STATS), jnp.float32)
+        for k, part in enumerate(parts):
+            row = jnp.where(field == k, left(part, (s - k) * GROUP % STATS), row)
+        stats.append(row)
+
+    rows = []
     acc = None
     for b in range(blocks):
-        vcopy[b].wait()
+        k = b % packs
+        copies[blocks + b].wait()
         full = jnp.dot(
-            probs[b].astype(jnp.bfloat16),
+            weights[b // packs][k * per : (k + 1) * per],
             vbuf[b * BLK : (b + 1) * BLK],
             preferred_element_type=jnp.float32,
         )
         mine = by_step(full, mask)
         acc = mine if acc is None else mine + jnp.where(joined[b], acc, 0.0)
-        stats = jnp.zeros((STEPS * GROUP, STATS), jnp.float32)
-        for k, part in enumerate(in_bf16_parts(tops[b], 3) + in_bf16_parts(totals[b], 2)):
-            stats = jnp.where(offset == k * GROUP, part, stats)
-        row = jnp.concatenate([acc, by_step(stats, every)], axis=1).astype(out.dtype)
-
-        @pl.when(meta[2, b] == 1)
-        def _():
-            out[meta[0, b]] = row
+        tail = jnp.concatenate([x[b : b + 1] for x in stats], axis=0)
+        row = jnp.concatenate([acc, tail], axis=1).astype(out.dtype)
+        rows.append(jnp.where(meta[2, b] == 1, row, empty))
+    for b in range(blocks):
+        out[meta[0, b]] = rows[b]
 
 
 def own_kernel(heads, hdim, query, key, value, slopes, stats, acc):
@@ -131,7 +167,7 @@
         at = slice(h * hdim, (h + 1) * hdim)
         dots = jnp.sum(products[:, at], axis=1, keepdims=True) * scale
         first = dots[0:1]
-        cross = dots[1:2] - slopes[h : h + 1]
+        cross = dots[1:2] - slopes[:, h : h + 1]
         second = dots[2:3]
         upper = jnp.maximum(cross, second)
         e_cross = jnp.exp(cross - upper)
@@ -144,10 +180,6 @@
         rows[1].append(e_cross * v0[:, at] + e_second * v1[:, at])
     stats[...] = jnp.concatenate([tops[0] + sums[0], tops[1] + sums[1]], axis=0)
     acc[...] = jnp.concatenate([jnp.concatenate(r, axis=1) for r in rows], axis=0)
-
-
-def left(x, lanes):
-    return pltpu.roll(x, x.shape[1] - lanes, 1) if lanes else x
 
 
 def join_kernel(heads, hdim, parts, own_stats, own_acc, out):
@@ -200,17 +232,52 @@
         out[r] = attended
 
 
+def project_kernel(rows, weight, mine, theirs):
+    full = lax.dot_general(
+        rows[...], weight[...], (((1,), (1,)), ((), ())), preferred_element_type=jnp.float32
+    )
+    first = lax.axis_index("head") % 2 == 0
+    chips, size = mine.shape[0], mine.shape[1]
+    for c in range(chips):
+        a = full[2 * c * size : (2 * c + 1) * size]
+        b = full[(2 * c + 1) * size : (2 * c + 2) * size]
+        mine[c] = jnp.where(first, a, b)
+        theirs[c] = jnp.where(first, b, a).astype(theirs.dtype)
+
+
+def pair_kernel(mine, got, total, *rest):
+    shares, both = rest[:-1], rest[-1]
+    chips = mine.shape[0]
+    chip = lax.axis_index("head") // 2
+    for c in range(chips):
+        both[c] = mine[c] + got[c].astype(jnp.float32)
+    total[...] = both[chip]
+    for hop, share in enumerate(shares, 1):
+        share[...] = both[lax.rem(chip + hop, chips)].astype(share.dtype)
+
+
+def finish_kernel(total, *rest):
+    shares, residual, out = rest[:-2], rest[-2], rest[-1]
+    x = total[...]
+    for share in shares:
+        x = x + share[...].astype(jnp.float32)
+    for s in range(STEPS):
+        rows = [x[r : r + 1] for r in range(s, x.shape[0], STEPS)]
+        y = residual[s].astype(jnp.float32) + jnp.concatenate(rows, axis=0)
+        out[s] = y.astype(out.dtype)
+
+
 def copies_kernel(x, out):
     for r in range(out.shape[0]):
         out[r] = x[...]
 
 
-def on_device(kernel, out_shape, in_spaces, **more):
+def on_device(kernel, out_shape, in_spaces, limit, **more):
     return pl.pallas_call(
         kernel,
         out_shape=out_shape,
         in_specs=[pl.BlockSpec(memory_space=m) for m in in_spaces],
-        compiler_params=pltpu.CompilerParams(vmem_limit_bytes=VMEM_LIMIT),
+        compiler_params=pltpu.CompilerParams(vmem_limit_bytes=limit * MIB),
         **more,
     )
 
@@ -229,6 +296,37 @@
     before = hit & (index[:, None] > starts[None, :]) & (jnp.arange(blocks)[:, None] > 0)
     joined = jnp.any(before, axis=1)
     return jnp.stack([row, base, live.astype(jnp.int32), joined.astype(jnp.int32)])
+
+
+def project_and_sum(rows, out_weight, residual, groups):
+    chips = groups // 2
+    size, columns = rows.shape[0] // groups, out_weight.shape[1]
+    each = (chips, size, columns)
+    mine, theirs = on_device(
+        project_kernel,
+        (jax.ShapeDtypeStruct(each, jnp.float32), jax.ShapeDtypeStruct(each, jnp.bfloat16)),
+        [pltpu.VMEM] * 2,
+        16,
+    )(rows, out_weight.T)
+    got = lax.ppermute(theirs, "head", [(i, i ^ 1) for i in range(groups)])
+    share = jax.ShapeDtypeStruct((size, columns), jnp.bfloat16)
+    total, *shares = on_device(
+        pair_kernel,
+        (jax.ShapeDtypeStruct((size, columns), jnp.float32), *[share] * (chips - 1)),
+        [pltpu.VMEM] * 2,
+        16,
+        scratch_shapes=[pltpu.VMEM(each, jnp.float32)],
+    )(mine, got)
+    arrived = [
+        lax.ppermute(x, "head", [(i, (i + 2 * hop) % groups) for i in range(groups)])
+        for hop, x in enumerate(shares, 1)
+    ]
+    return on_device(
+        finish_kernel,
+        jax.ShapeDtypeStruct(residual.shape, residual.dtype),
+        [pltpu.VMEM] * (chips + 1),
+        16,
+    )(total, *arrived, residual)
 
 
 def body(
@@ -253,12 +351,12 @@
     own_query = queries.reshape(STEPS, width)
 
     copies = on_device(
-        copies_kernel, jax.ShapeDtypeStruct((peers, STEPS, width), jnp.bfloat16), [vmem]
+        copies_kernel, jax.ShapeDtypeStruct((peers, STEPS, width), jnp.bfloat16), [vmem], 4
     )(own_query)
     everyone = lax.all_to_all(copies, "seq", 0, 0, tiled=True)
 
     table = block_table(seg_blocks, request_row, blocks)
-    column = jnp.tile(jnp.pad(slopes, (0, GROUP - heads)), STEPS)[:, None]
+    lanes = jnp.tile(jnp.pad(slopes, (0, GROUP - heads)), BLK // GROUP)[None]
     own_stats, own_acc = on_device(
         functools.partial(own_kernel, heads, hdim),
         (
@@ -266,34 +364,38 @@
             jax.ShapeDtypeStruct((STEPS, width), jnp.float32),
         ),
         [vmem] * 4,
-    )(own_query, new_keys.reshape(STEPS, width), new_values.reshape(STEPS, width), column)
+        4,
+    )(own_query, new_keys.reshape(STEPS, width), new_values.reshape(STEPS, width), lanes)
 
     partials = on_device(
         functools.partial(attend_kernel, blocks, hdim),
         jax.ShapeDtypeStruct((peers, STEPS, width + STATS), jnp.bfloat16),
-        [smem, vmem, vmem, anywhere, anywhere],
+        [smem, vmem, vmem, pl.ANY, pltpu.HBM, pltpu.HBM],
+        32,
         scratch_shapes=[
             pltpu.VMEM(cache_keys.shape, jnp.bfloat16),
             pltpu.VMEM(cache_values.shape, jnp.bfloat16),
-            pltpu.SemaphoreType.DMA((blocks,)),
-            pltpu.SemaphoreType.DMA((blocks,)),
+            pltpu.SemaphoreType.DMA((2, blocks)),
         ],
-    )(table, column, everyone, cache_keys, cache_values)
+    )(
+        table,
+        lanes,
+        everyone,
+        own_stats,
+        pltpu.with_memory_space_constraint(cache_keys, pltpu.HBM),
+        pltpu.with_memory_space_constraint(cache_values, pltpu.HBM),
+    )
     arrived = lax.all_to_all(partials, "seq", 0, 0, tiled=True)
 
     attended = on_device(
         functools.partial(join_kernel, heads, hdim),
         jax.ShapeDtypeStruct((peers, STEPS, width), jnp.bfloat16),
         [vmem] * 3,
+        16,
     )(arrived.reshape(peers * STEPS, width + STATS), own_stats, own_acc)
     rows = lax.all_to_all(attended, "seq", 0, 0, tiled=True).reshape(peers * STEPS, width)
 
-    projected = jnp.dot(rows, out_weight, preferred_element_type=jnp.float32)
-    projected = projected.astype(jnp.bfloat16).reshape(groups, -1, out_weight.shape[1])
-    shares = lax.all_to_all(projected, "head", 0, 0, tiled=True)
-    summed = jnp.sum(shares.astype(jnp.float32), axis=0)
-    summed = summed.reshape(-1, STEPS, out_weight.shape[1]).transpose(1, 0, 2)
-    return (residual.astype(jnp.float32) + summed).astype(jnp.bfloat16)
+    return project_and_sum(rows, out_weight, residual, groups)
 
 
 def solution(mesh):

time: 79.3 us -> 73.7 us (0.929)
  waiting for transfers between devices: 17.4 us -> 7.49 us
  starting transfers between devices: 16.4 us -> 21.3 us
  blocking collectives: 27.6 us -> 28.7 us
    all_to_all x1 -> x0, waiting for transfers between devices: 9.98 us -> none  [body(): arrived = lax.all_to_all(partials, 'seq', 0, 0, tiled=True)]
    ppermute x0 -> x4, starting transfers between devices: none -> 9.48 us  [the longest x3 5.06 us: project_and_sum(): lax.ppermute(x, 'head', [(i, (i + 2 * hop) % groups) for i in range(group...]
    all_to_all x1 -> x0, starting transfers between devices: 4.5 us -> none  [body(): arrived = lax.all_to_all(partials, 'seq', 0, 0, tiled=True)]
    ppermute x0 -> x4, waiting for transfers between devices: none -> 2.56 us  [the longest x3 1.7 us: project_and_sum(): lax.ppermute(x, 'head', [(i, (i + 2 * hop) % groups) for i in range(group...]
    all_to_all x1, waiting for transfers between devices: 7.39 us -> 4.93 us  [body(): everyone = lax.all_to_all(copies, 'seq', 0, 0, tiled=True)]
    pallas_call x1, Pallas kernels: 8.41 us -> 6.4 us  [body(): on_device(functools.partial(attend_kernel, blocks, hdim), jax.ShapeDtypeS...]
    pallas_call x0 -> x3, Pallas kernels: none -> 1.22 us  [the longest x1 0.62 us: project_and_sum(): on_device(finish_kernel, jax.ShapeDtypeStruct(residual.shape, residual.dt...]
    all_to_all x1, blocking collectives: 13.5 us -> 14.6 us  [body(): arrived = lax.all_to_all(partials, 'seq', 0, 0, tiled=True)]
  transfers between devices with their start and end apart: 2 -> 5, of which waited for: 2 -> 4; matrix products, arithmetic and copies ran while one was open for 4% -> 5% of each run, Pallas kernels for 0% -> 1%
where the time goes in v2:
time: 73.7 us; the launch traced here: 73.2 us
  blocking collectives  28.7 us (39%)
  starting transfers between devices  21.3 us (29%)
  Pallas kernels  9.25 us (13%)
  waiting for transfers between devices  7.49 us (10%)
  local copies, waits for them, and re-layouts  3.72 us (5%)
  other arithmetic  2.55 us (3%)
    all_to_all x1, blocking collectives, body(): arrived = lax.all_to_all(partials, 'seq', 0, 0, tiled=True)  14.6 us
    all_to_all x1, blocking collectives, body(): lax.all_to_all(attended, 'seq', 0, 0, tiled=True)  14.1 us
    all_to_all x1, starting transfers between devices, body(): everyone = lax.all_to_all(copies, 'seq', 0, 0, tiled=True)  11.9 us
    pallas_call x1, Pallas kernels, body(): on_device(functools.partial(attend_kernel, blocks, hdim), jax.ShapeDtypeS...  6.4 us
    ppermute x3, starting transfers between devices, project_and_sum(): lax.ppermute(x, 'head', [(i, (i + 2 * hop) % groups) for i in range(group...  5.06 us
    all_to_all x1, waiting for transfers between devices, body(): everyone = lax.all_to_all(copies, 'seq', 0, 0, tiled=True)  4.93 us
    ppermute x1, starting transfers between devices, project_and_sum(): got = lax.ppermute(theirs, 'head', [(i, i ^ 1) for i in range(groups)])  4.41 us
    unnamed x12, local copies, waits for them, and re-layouts  2.79 us
  transfers between devices with their start and end apart: 5, of which 4 were waited for; matrix products, arithmetic and copies ran while one was open for 5% of the time, Pallas kernels for 1%

profile of v2, /device:TPU:1, one launch (start us, length us, event | category | flops | bytes accessed | tf_op | source)
XLA Modules:
  0.0 73.2 jit_solution(4162912493023526703)
XLA Ops:
  0.0 0.7 copy-done.1
  0.7 0.7 shard_map.100
  1.4 11.9 %all-to-all-start = ((bf16[32,2,1792]{2,1,0:T(2,128)(2,1)}), bf16[32,2,1792]{2,1,0:T(2,128)(2,1)S(1)}, u32[]{:S(2)}, u32[]{:S(2)}) async-start(bf16[32,2,1792]{2,1,0:T(2,128)(2,1)} %shard_map.100), calls=%async_computation | async-start | bytes 458752 | tf_op jit(solution)/shard_map/all_to_all | solution.py:356
  13.3 0.8 %select_reduce_fusion = s32[32]{0:T(128)S(1)} fusion(s32[32]{0:T(128)} %param.16), kind=kLoop, calls=%fused_computation | loop fusion | flops 3040 | bytes 256 | tf_op jit(solution)/shard_map/reduce_sum | solution.py:288
  14.1 0.7 add.28
  14.7 0.9 %select_reduce_fusion.2 = (s32[8]{0:T(128)S(1)}, s32[8]{0:T(128)S(1)}) fusion(s32[32]{0:T(128)} %param.17, s32[32]{0:T(128)S(1)} %add.28, s32[32]{0:T(128)S(1)} %select_reduce_fusion, s32[8]{0:T(128)S(1)} %iota_add_fusion), kind=kLoop, calls=%fused_computation.3 | loop fusion | flops 1776 | bytes 480 | tf_op jit(solution)/shard_map/reduce_sum | solution.py:292
  15.6 0.7 pad.4
  16.3 0.1 broadcast_in_dim_tile.3.slopes
  16.4 0.7 copy-done.2
  17.1 0.7 copy-done.4
  17.7 0.7 copy-done.5
  18.4 0.4 shard_map.101
  18.8 0.2 fusion
  19.1 4.9 %all-to-all-done.query = bf16[32,2,1792]{2,1,0:T(2,128)(2,1)S(1)} async-done(((bf16[32,2,1792]{2,1,0:T(2,128)(2,1)}), bf16[32,2,1792]{2,1,0:T(2,128)(2,1)S(1)}, u32[]{:S(2)}, u32[]{:S(2)}) %all-to-all-start) | async-done | bytes 229408 | tf_op jit(solution)/shard_map/all_to_all | solution.py:356
  24.0 6.4 %shard_map.102 = bf16[32,2,1920]{2,1,0:T(2,128)(2,1)S(1)} custom-call(s32[4,8]{1,0:T(4,128)S(1)} %pad_add_fusion.meta, f32[1,128]{1,0:T(1,128)S(1)} %broadcast_in_dim_tile.3.slopes, bf16[32,2,1792]{2,1,0:T(2,128)(2,1)S(1)} %all-to-all-done.query, f32[2,128]{1,0:T(2,128)S(1)} %get-tuple-element.13.own_stats, bf16[1024,1792]{1,0:T(8,128)(2,1)} %keys.1, ...), custom_call_target="tpu_custom_call" | custom-call | tf_op jit(solution)/shard_map/pallas_call | solution.py:370
  30.4 0.0 copy-start.3
  30.4 14.6 %all_to_all.15 = bf16[32,2,1920]{2,1,0:T(2,128)(2,1)S(1)} all-to-all(bf16[32,2,1920]{2,1,0:T(2,128)(2,1)S(1)} %shard_map.102), channel_id=1, replica_groups=mesh['seq'=32,'head'=8] {'seq'}, dimensions={0} | all-to-all | bytes 491520 | tf_op jit(solution)/shard_map/all_to_all | solution.py:388
  45.0 0.1 reshape.72.parts
  45.1 0.6 shard_map.103
  45.7 14.1 %all_to_all.16 = bf16[32,2,1792]{2,1,0:T(2,128)(2,1)S(1)} all-to-all(bf16[32,2,1792]{2,1,0:T(2,128)(2,1)S(1)} %shard_map.103), channel_id=1, replica_groups=mesh['seq'=32,'head'=8] {'seq'}, dimensions={0} | all-to-all | bytes 458752 | tf_op jit(solution)/shard_map/all_to_all | solution.py:396
  59.8 0.1 reshape.73.rows
  59.9 0.6 shard_map.104
  60.5 4.4 %collective-permute-start = (bf16[4,8,448]{2,1,0:T(8,128)(2,1)S(1)}, bf16[4,8,448]{2,1,0:T(8,128)(2,1)S(1)}, u32[]{:S(2)}, u32[]{:S(2)}) collective-permute-start(bf16[4,8,448]{2,1,0:T(8,128)(2,1)S(1)} %get-tuple-element.16), channel_id=1, source_target_pairs={{0,1},{1,0},{2,3},{3,2},{4,5},{5,4},{6,7},{7,6},{8,9},{9,8},{10,11... | collective-permute-start | bytes 86024 | tf_op jit(solution)/shard_map/ppermute | solution.py:311
  64.9 0.9 %collective-permute-done.got = bf16[4,8,448]{2,1,0:T(8,128)(2,1)S(1)} collective-permute-done((bf16[4,8,448]{2,1,0:T(8,128)(2,1)S(1)}, bf16[4,8,448]{2,1,0:T(8,128)(2,1)S(1)}, u32[]{:S(2)}, u32[]{:S(2)}) %collective-permute-start) | collective-permute-done | bytes 28704 | tf_op jit(solution)/shard_map/ppermute | solution.py:311
  65.8 1.4 %collective-permute-start.1 = (bf16[8,448]{1,0:T(8,128)(2,1)S(1)}, bf16[8,448]{1,0:T(8,128)(2,1)S(1)}, u32[]{:S(2)}, u32[]{:S(2)}) collective-permute-start(bf16[8,448]{1,0:T(8,128)(2,1)S(1)} %get-tuple-element.18), channel_id=1, source_target_pairs={{0,2},{1,3},{2,4},{3,5},{4,6},{5,7},{6,0},{7,1},{8,10},{9,11},{10,... | collective-permute-start | bytes 21512 | tf_op jit(solution)/shard_map/ppermute | solution.py:321
  67.2 2.6 %collective-permute-start.2 = (bf16[8,448]{1,0:T(8,128)(2,1)S(1)}, bf16[8,448]{1,0:T(8,128)(2,1)S(1)}, u32[]{:S(2)}, u32[]{:S(2)}) collective-permute-start(bf16[8,448]{1,0:T(8,128)(2,1)S(1)} %get-tuple-element.19), channel_id=1, source_target_pairs={{0,4},{1,5},{2,6},{3,7},{4,0},{5,1},{6,2},{7,3},{8,12},{9,13},{10,... | collective-permute-start | bytes 21512 | tf_op jit(solution)/shard_map/ppermute | solution.py:321
  69.8 1.1 %collective-permute-start.3 = (bf16[8,448]{1,0:T(8,128)(2,1)S(1)}, bf16[8,448]{1,0:T(8,128)(2,1)S(1)}, u32[]{:S(2)}, u32[]{:S(2)}) collective-permute-start(bf16[8,448]{1,0:T(8,128)(2,1)S(1)} %get-tuple-element.20), channel_id=1, source_target_pairs={{0,6},{1,7},{2,0},{3,1},{4,2},{5,3},{6,4},{7,5},{8,14},{9,15},{10,... | collective-permute-start | bytes 21512 | tf_op jit(solution)/shard_map/ppermute | solution.py:321
  70.9 0.0 collective-permute-done.1.rest_0_
  70.9 0.3 collective-permute-done.2.rest_1_
  71.2 1.4 %collective-permute-done.3.rest_2_ = bf16[8,448]{1,0:T(8,128)(2,1)S(1)} collective-permute-done((bf16[8,448]{1,0:T(8,128)(2,1)S(1)}, bf16[8,448]{1,0:T(8,128)(2,1)S(1)}, u32[]{:S(2)}, u32[]{:S(2)}) %collective-permute-start.3) | collective-permute-done | bytes 7200 | tf_op jit(solution)/shard_map/ppermute | solution.py:321
  72.6 0.0 copy-done.3
  72.6 0.6 shard_map.106
  (13 shorter events, 0.1 us)
Async XLA Ops:
  0.0 0.7 copy-start.1
  1.4 22.6 %all-to-all-start = ((bf16[32,2,1792]{2,1,0:T(2,128)(2,1)}), bf16[32,2,1792]{2,1,0:T(2,128)(2,1)S(1)}, u32[]{:S(2)}, u32[]{:S(2)}) async-start(bf16[32,2,1792]{2,1,0:T(2,128)(2,1)} %shard_map.100), calls=%async_computation | async-start | bytes 458752 | tf_op jit(solution)/shard_map/all_to_all | solution.py:356
  16.4 0.7 copy-start.2
  17.1 0.7 copy-start.4
  17.7 0.7 copy-start.5
  24.0 35.9 %copy-start = (bf16[1792,448]{0,1:T(8,128)(2,1)S(1)}, bf16[1792,448]{0,1:T(8,128)(2,1)}, u32[]{:S(2)}) copy-start(bf16[1792,448]{0,1:T(8,128)(2,1)} %param.18) | copy-start | bytes 4816900
  30.4 42.2 %copy-start.3 = (bf16[2,4,448]{2,1,0:T(4,128)(2,1)S(1)}, bf16[2,4,448]{2,1,0:T(4,128)(2,1)}, u32[]{:S(2)}) copy-start(bf16[2,4,448]{2,1,0:T(4,128)(2,1)} %rest_3_.1) | copy-start | bytes 21508
  60.5 5.3 %collective-permute-start = (bf16[4,8,448]{2,1,0:T(8,128)(2,1)S(1)}, bf16[4,8,448]{2,1,0:T(8,128)(2,1)S(1)}, u32[]{:S(2)}, u32[]{:S(2)}) collective-permute-start(bf16[4,8,448]{2,1,0:T(8,128)(2,1)S(1)} %get-tuple-element.16), channel_id=1, source_target_pairs={{0,1},{1,0},{2,3},{3,2},{4,5},{5,4},{6,7},{7,6},{8,9},{9,8},{10,11... | collective-permute-start | bytes 86024 | tf_op jit(solution)/shard_map/ppermute | solution.py:311
  65.8 5.1 %collective-permute-start.1 = (bf16[8,448]{1,0:T(8,128)(2,1)S(1)}, bf16[8,448]{1,0:T(8,128)(2,1)S(1)}, u32[]{:S(2)}, u32[]{:S(2)}) collective-permute-start(bf16[8,448]{1,0:T(8,128)(2,1)S(1)} %get-tuple-element.18), channel_id=1, source_target_pairs={{0,2},{1,3},{2,4},{3,5},{4,6},{5,7},{6,0},{7,1},{8,10},{9,11},{10,... | collective-permute-start | bytes 21512 | tf_op jit(solution)/shard_map/ppermute | solution.py:321
  67.2 4.0 %collective-permute-start.2 = (bf16[8,448]{1,0:T(8,128)(2,1)S(1)}, bf16[8,448]{1,0:T(8,128)(2,1)S(1)}, u32[]{:S(2)}, u32[]{:S(2)}) collective-permute-start(bf16[8,448]{1,0:T(8,128)(2,1)S(1)} %get-tuple-element.19), channel_id=1, source_target_pairs={{0,4},{1,5},{2,6},{3,7},{4,0},{5,1},{6,2},{7,3},{8,12},{9,13},{10,... | collective-permute-start | bytes 21512 | tf_op jit(solution)/shard_map/ppermute | solution.py:321
  69.8 2.8 %collective-permute-start.3 = (bf16[8,448]{1,0:T(8,128)(2,1)S(1)}, bf16[8,448]{1,0:T(8,128)(2,1)S(1)}, u32[]{:S(2)}, u32[]{:S(2)}) collective-permute-start(bf16[8,448]{1,0:T(8,128)(2,1)S(1)} %get-tuple-element.20), channel_id=1, source_target_pairs={{0,6},{1,7},{2,0},{3,1},{4,2},{5,3},{6,4},{7,5},{8,14},{9,15},{10,... | collective-permute-start | bytes 21512 | tf_op jit(solution)/shard_map/ppermute | solution.py:321

commit v3 on v2

--- a/solution.py
+++ b/solution.py
@@ -46,9 +46,26 @@
 
 
 def attend_kernel(
-    blocks, hdim, meta, slopes, query, own_stats, keys, values, out, kbuf, vbuf, sems
+    blocks,
+    heads,
+    seg_blocks,
+    request_row,
+    slopes,
+    query,
+    own_query,
+    new_key,
+    new_value,
+    keys,
+    values,
+    out,
+    own_stats,
+    own_acc,
+    kbuf,
+    vbuf,
+    sems,
 ):
     width = keys.shape[1]
+    hdim = width // heads
     per = STEPS * GROUP
     packs = BLK // per
     scale = 1.0 / math.sqrt(hdim)
@@ -59,6 +76,7 @@
             copies.append(pltpu.make_async_copy(src.at[rows], dst.at[rows], sems.at[i, b]))
     for copy in copies:
         copy.start()
+    table = block_table(blocks, seg_blocks, request_row)
     mask = head_mask(width, hdim)
     lane = iota((STEPS, STATS), 1)
     empty = jnp.concatenate(
@@ -67,11 +85,13 @@
     for r in range(out.shape[0]):
         out[r] = empty
 
+    own_stats[...], own_acc[...] = own_terms(heads, hdim, own_query, new_key, new_value, slopes)
+
     raw = []
     for g in range(blocks // packs):
         spread = []
         for b in range(g * packs, (g + 1) * packs):
-            q = query[meta[0, b]].astype(jnp.float32)
+            q = query[table[b][0]].astype(jnp.float32)
             for s in range(STEPS):
                 spread.append(jnp.where(mask, q[s : s + 1], 0.0).astype(jnp.bfloat16))
         for b in range(g * packs, (g + 1) * packs):
@@ -87,15 +107,17 @@
 
     pack = iota((BLK, BLK), 1) // per
     when = (iota((BLK, BLK), 1) % per) // GROUP - iota((BLK, BLK), 0)
-    slope = slopes[...]
-    joined = [meta[3, b] == 1 for b in range(blocks)]
+    slope = jnp.zeros((1, BLK), jnp.float32)
+    for h in range(heads):
+        slope = jnp.where(iota((1, BLK), 1) % GROUP == h, slopes[h], slope)
+    joined = [table[b][3] for b in range(blocks)]
     scores = []
     tops = []
     for g in range(blocks // packs):
         for k in range(packs):
             b = g * packs + k
             tile = raw[g][k * BLK : (k + 1) * BLK]
-            base = meta[1, b]
+            base = table[b][1]
             x = tile if k == 0 else jnp.where(pack == k, tile, x)
             dist = when + base if k == 0 else jnp.where(pack == k, when + base, dist)
         x = x * scale - slope * dist.astype(jnp.float32)
@@ -145,12 +167,12 @@
         acc = mine if acc is None else mine + jnp.where(joined[b], acc, 0.0)
         tail = jnp.concatenate([x[b : b + 1] for x in stats], axis=0)
         row = jnp.concatenate([acc, tail], axis=1).astype(out.dtype)
-        rows.append(jnp.where(meta[2, b] == 1, row, empty))
+        rows.append(jnp.where(table[b][2], row, empty))
     for b in range(blocks):
-        out[meta[0, b]] = rows[b]
-
-
-def own_kernel(heads, hdim, query, key, value, slopes, stats, acc):
+        out[table[b][0]] = rows[b]
+
+
+def own_terms(heads, hdim, query, key, value, slopes):
     scale = 1.0 / math.sqrt(hdim)
     q = query[...].astype(jnp.float32)
     k = key[...].astype(jnp.float32)
@@ -167,7 +189,7 @@
         at = slice(h * hdim, (h + 1) * hdim)
         dots = jnp.sum(products[:, at], axis=1, keepdims=True) * scale
         first = dots[0:1]
-        cross = dots[1:2] - slopes[:, h : h + 1]
+        cross = dots[1:2] - slopes[h]
         second = dots[2:3]
         upper = jnp.maximum(cross, second)
         e_cross = jnp.exp(cross - upper)
@@ -178,8 +200,35 @@
         sums[1] = jnp.where(lane == h + GROUP, e_cross + e_second, sums[1])
         rows[0].append(v0[:, at])
         rows[1].append(e_cross * v0[:, at] + e_second * v1[:, at])
-    stats[...] = jnp.concatenate([tops[0] + sums[0], tops[1] + sums[1]], axis=0)
-    acc[...] = jnp.concatenate([jnp.concatenate(r, axis=1) for r in rows], axis=0)
+    stats = jnp.concatenate([tops[0] + sums[0], tops[1] + sums[1]], axis=0)
+    return stats, jnp.concatenate([jnp.concatenate(r, axis=1) for r in rows], axis=0)
+
+
+def block_table(blocks, seg_blocks, request_row):
+    requests = seg_blocks.shape[0]
+    index = lax.axis_index("seq") * blocks
+
+    def skip(i, carry):
+        request, end, total = carry
+        total = total + seg_blocks[i]
+        passed = total <= index
+        return request + passed.astype(jnp.int32), jnp.where(passed, total, end), total
+
+    zero = jnp.int32(0)
+    request, end, _ = lax.fori_loop(0, requests, skip, (zero, zero, zero))
+    last = requests - 1
+    end = end + seg_blocks[jnp.minimum(request, last)]
+    table = []
+    for b in range(blocks):
+        joined = jnp.bool_(False)
+        if b:
+            joined = index + b < end
+            request = jnp.where(joined, request, request + 1)
+            end = jnp.where(joined, end, end + seg_blocks[jnp.minimum(request, last)])
+        live = request <= last
+        row = request_row[jnp.minimum(request, last)]
+        table.append((row, (end - index - b) * BLK, live, joined & live))
+    return table
 
 
 def join_kernel(heads, hdim, parts, own_stats, own_acc, out):
@@ -267,9 +316,16 @@
         out[s] = y.astype(out.dtype)
 
 
-def copies_kernel(x, out):
-    for r in range(out.shape[0]):
-        out[r] = x[...]
+def copies_kernel(x, out, sems):
+    copies = [pltpu.make_async_copy(x, out.at[r], sems.at[r]) for r in range(out.shape[0])]
+    for copy in copies:
+        copy.start()
+    for copy in copies:
+        copy.wait()
+
+
+def in_hbm(x):
+    return pltpu.with_memory_space_constraint(x, pltpu.HBM)
 
 
 def on_device(kernel, out_shape, in_spaces, limit, **more):
@@ -280,22 +336,6 @@
         compiler_params=pltpu.CompilerParams(vmem_limit_bytes=limit * MIB),
         **more,
     )
-
-
-def block_table(seg_blocks, request_row, blocks):
-    requests = seg_blocks.shape[0]
-    order = jnp.arange(requests, dtype=jnp.int32)
-    starts = jnp.sum(jnp.where(order[None, :] < order[:, None], seg_blocks[None, :], 0), axis=1)
-    index = lax.axis_index("seq") * blocks + jnp.arange(blocks, dtype=jnp.int32)
-    ends = starts + seg_blocks
-    hit = (index[:, None] >= starts[None, :]) & (index[:, None] < ends[None, :])
-    pick = lambda x: jnp.sum(jnp.where(hit, x[None, :], 0), axis=1)
-    row = pick(request_row)
-    base = pick(ends) * BLK - index * BLK
-    live = jnp.any(hit, axis=1)
-    before = hit & (index[:, None] > starts[None, :]) & (jnp.arange(blocks)[:, None] > 0)
-    joined = jnp.any(before, axis=1)
-    return jnp.stack([row, base, live.astype(jnp.int32), joined.astype(jnp.int32)])
 
 
 def project_and_sum(rows, out_weight, residual, groups):
@@ -347,30 +387,26 @@
     peers = lax.axis_size("seq")
     groups = lax.axis_size("head")
     blocks = cache_keys.shape[0] // BLK
-    vmem, smem, anywhere = pltpu.VMEM, pltpu.SMEM, pl.ANY
+    vmem, smem = pltpu.VMEM, pltpu.SMEM
     own_query = queries.reshape(STEPS, width)
 
     copies = on_device(
-        copies_kernel, jax.ShapeDtypeStruct((peers, STEPS, width), jnp.bfloat16), [vmem], 4
-    )(own_query)
+        copies_kernel,
+        jax.ShapeDtypeStruct((peers, STEPS, width), jnp.bfloat16),
+        [pltpu.HBM],
+        4,
+        scratch_shapes=[pltpu.SemaphoreType.DMA((peers,))],
+    )(in_hbm(own_query))
     everyone = lax.all_to_all(copies, "seq", 0, 0, tiled=True)
 
-    table = block_table(seg_blocks, request_row, blocks)
-    lanes = jnp.tile(jnp.pad(slopes, (0, GROUP - heads)), BLK // GROUP)[None]
-    own_stats, own_acc = on_device(
-        functools.partial(own_kernel, heads, hdim),
+    partials, own_stats, own_acc = on_device(
+        functools.partial(attend_kernel, blocks, heads),
         (
+            jax.ShapeDtypeStruct((peers, STEPS, width + STATS), jnp.bfloat16),
             jax.ShapeDtypeStruct((STEPS, STATS), jnp.float32),
             jax.ShapeDtypeStruct((STEPS, width), jnp.float32),
         ),
-        [vmem] * 4,
-        4,
-    )(own_query, new_keys.reshape(STEPS, width), new_values.reshape(STEPS, width), lanes)
-
-    partials = on_device(
-        functools.partial(attend_kernel, blocks, hdim),
-        jax.ShapeDtypeStruct((peers, STEPS, width + STATS), jnp.bfloat16),
-        [smem, vmem, vmem, pl.ANY, pltpu.HBM, pltpu.HBM],
+        [smem] * 3 + [vmem] * 4 + [pltpu.HBM] * 2,
         32,
         scratch_shapes=[
             pltpu.VMEM(cache_keys.shape, jnp.bfloat16),
@@ -378,12 +414,15 @@
             pltpu.SemaphoreType.DMA((2, blocks)),
         ],
     )(
-        table,
-        lanes,
+        in_hbm(seg_blocks),
+        in_hbm(request_row),
+        in_hbm(slopes),
         everyone,
-        own_stats,
-        pltpu.with_memory_space_constraint(cache_keys, pltpu.HBM),
-        pltpu.with_memory_space_constraint(cache_values, pltpu.HBM),
+        in_hbm(own_query),
+        in_hbm(new_keys.reshape(STEPS, width)),
+        in_hbm(new_values.reshape(STEPS, width)),
+        in_hbm(cache_keys),
+        in_hbm(cache_values),
     )
     arrived = lax.all_to_all(partials, "seq", 0, 0, tiled=True)
 

time: 73.7 us -> 74.4 us (level)
  blocking collectives: 28.7 us -> 51.1 us
  starting transfers between devices: 21.3 us -> 9.47 us
  waiting for transfers between devices: 7.49 us -> 2.56 us
  local copies, waits for them, and re-layouts: 3.72 us -> 0.19 us
  other arithmetic: 2.55 us -> 0 us
  Pallas kernels: 9.25 us -> 10.6 us
    all_to_all x0 -> x1, blocking collectives: none -> 22.4 us  [body(): everyone = lax.all_to_all(copies, 'seq', 0, 0, tiled=True)]
    all_to_all x1 -> x0, starting transfers between devices: 11.9 us -> none  [body(): everyone = lax.all_to_all(copies, 'seq', 0, 0, tiled=True)]
    all_to_all x1 -> x0, waiting for transfers between devices: 4.93 us -> none  [body(): everyone = lax.all_to_all(copies, 'seq', 0, 0, tiled=True)]
    unnamed x12 -> x4, local copies, waits for them, and re-layouts: 2.79 us -> 0.01 us
    reduce_sum x2 -> x0, other arithmetic: 1.63 us -> none  [the longest x1 0.86 us: block_table(): pick = lambda x: jnp.sum(jnp.where(hit, x[None, :], 0), axis=1)]
    pallas_call x1, Pallas kernels: 0.7 us -> 2.12 us  [body(): on_device(copies_kernel, jax.ShapeDtypeStruct((peers, STEPS, width), jnp....]
    pallas_call x2 -> x1, Pallas kernels: 6.77 us -> 6.71 us  [body(): on_device(functools.partial(attend_kernel, blocks, heads), (jax.ShapeDtyp...]
  transfers between devices with their start and end apart: 5 -> 4, of which waited for: 4 -> 3; matrix products, arithmetic and copies ran while one was open for 5% -> 0% of each run, Pallas kernels for 1% -> 0%
where the time goes in v3:
time: 74.4 us; the launch traced here: 74 us
  blocking collectives  51.1 us (69%)
  Pallas kernels  10.6 us (14%)
  starting transfers between devices  9.47 us (13%)
  waiting for transfers between devices  2.56 us (3%)
    all_to_all x1, blocking collectives, body(): everyone = lax.all_to_all(copies, 'seq', 0, 0, tiled=True)  22.4 us
    all_to_all x1, blocking collectives, body(): arrived = lax.all_to_all(partials, 'seq', 0, 0, tiled=True)  14.6 us
    all_to_all x1, blocking collectives, body(): lax.all_to_all(attended, 'seq', 0, 0, tiled=True)  14.1 us
    pallas_call x1, Pallas kernels, body(): on_device(functools.partial(attend_kernel, blocks, heads), (jax.ShapeDtyp...  6.71 us
    ppermute x3, starting transfers between devices, project_and_sum(): lax.ppermute(x, 'head', [(i, (i + 2 * hop) % groups) for i in range(group...  5.06 us
    ppermute x1, starting transfers between devices, project_and_sum(): got = lax.ppermute(theirs, 'head', [(i, i ^ 1) for i in range(groups)])  4.41 us
    pallas_call x1, Pallas kernels, body(): on_device(copies_kernel, jax.ShapeDtypeStruct((peers, STEPS, width), jnp....  2.12 us
    ppermute x3, waiting for transfers between devices, project_and_sum(): lax.ppermute(x, 'head', [(i, (i + 2 * hop) % groups) for i in range(group...  1.7 us
  transfers between devices with their start and end apart: 4, of which 3 were waited for; matrix products, arithmetic and copies ran while one was open for 0% of the time, Pallas kernels for 0%

profile of v3, /device:TPU:1, one launch (start us, length us, event | category | flops | bytes accessed | tf_op | source)
XLA Modules:
  0.0 74.0 jit_solution(11935608736888699890)
XLA Ops:
  0.0 2.1 %shard_map.100 = bf16[32,2,1792]{2,1,0:T(2,128)(2,1)S(1)} custom-call(bf16[2,1792]{1,0:T(2,128)(2,1)} %bitcast.5), custom_call_target="tpu_custom_call" | custom-call | tf_op jit(solution)/shard_map/pallas_call | solution.py:393
  2.1 22.4 %all_to_all.15.query = bf16[32,2,1792]{2,1,0:T(2,128)(2,1)S(1)} all-to-all(bf16[32,2,1792]{2,1,0:T(2,128)(2,1)S(1)} %shard_map.100), channel_id=1, replica_groups=mesh['seq'=32,'head'=8] {'seq'}, dimensions={0} | all-to-all | bytes 458752 | tf_op jit(solution)/shard_map/all_to_all | solution.py:400
  24.5 0.0 copy-start
  24.5 6.7 %shard_map.101 = (bf16[32,2,1920]{2,1,0:T(2,128)(2,1)S(1)}, f32[2,128]{1,0:T(2,128)S(1)}, f32[2,1792]{1,0:T(2,128)S(1)}) custom-call(s32[32]{0:T(128)} %seg_blocks.1, s32[32]{0:T(128)} %request_row.1, f32[14]{0:T(128)} %slopes.1, bf16[32,2,1792]{2,1,0:T(2,128)(2,1)S(1)} %all_to_all.15.query, bf16[2,1792]{1,0:T(2,128)(2,1)} %bitcast.6, ...), custom_call_target="tpu_custom_call" | custom-call | tf_op jit(solution)/shard_map/pallas_call | solution.py:402
  31.2 0.0 copy-start.1
  31.3 14.6 %all_to_all.16 = bf16[32,2,1920]{2,1,0:T(2,128)(2,1)S(1)} all-to-all(bf16[32,2,1920]{2,1,0:T(2,128)(2,1)S(1)} %get-tuple-element.14), channel_id=1, replica_groups=mesh['seq'=32,'head'=8] {'seq'}, dimensions={0} | all-to-all | bytes 491520 | tf_op jit(solution)/shard_map/all_to_all | solution.py:427
  45.9 0.1 reshape.18.parts
  46.0 0.6 shard_map.102
  46.5 14.1 %all_to_all.17 = bf16[32,2,1792]{2,1,0:T(2,128)(2,1)S(1)} all-to-all(bf16[32,2,1792]{2,1,0:T(2,128)(2,1)S(1)} %shard_map.102), channel_id=1, replica_groups=mesh['seq'=32,'head'=8] {'seq'}, dimensions={0} | all-to-all | bytes 458752 | tf_op jit(solution)/shard_map/all_to_all | solution.py:435
  60.6 0.1 reshape.19.rows
  60.7 0.0 copy-done
  60.7 0.6 shard_map.103
  61.3 4.4 %collective-permute-start = (bf16[4,8,448]{2,1,0:T(8,128)(2,1)S(1)}, bf16[4,8,448]{2,1,0:T(8,128)(2,1)S(1)}, u32[]{:S(2)}, u32[]{:S(2)}) collective-permute-start(bf16[4,8,448]{2,1,0:T(8,128)(2,1)S(1)} %get-tuple-element.18), channel_id=1, source_target_pairs={{0,1},{1,0},{2,3},{3,2},{4,5},{5,4},{6,7},{7,6},{8,9},{9,8},{10,11... | collective-permute-start | bytes 86024 | tf_op jit(solution)/shard_map/ppermute | solution.py:351
  65.7 0.9 %collective-permute-done.got = bf16[4,8,448]{2,1,0:T(8,128)(2,1)S(1)} collective-permute-done((bf16[4,8,448]{2,1,0:T(8,128)(2,1)S(1)}, bf16[4,8,448]{2,1,0:T(8,128)(2,1)S(1)}, u32[]{:S(2)}, u32[]{:S(2)}) %collective-permute-start) | collective-permute-done | bytes 28704 | tf_op jit(solution)/shard_map/ppermute | solution.py:351
  66.6 1.4 %collective-permute-start.1 = (bf16[8,448]{1,0:T(8,128)(2,1)S(1)}, bf16[8,448]{1,0:T(8,128)(2,1)S(1)}, u32[]{:S(2)}, u32[]{:S(2)}) collective-permute-start(bf16[8,448]{1,0:T(8,128)(2,1)S(1)} %get-tuple-element.20), channel_id=1, source_target_pairs={{0,2},{1,3},{2,4},{3,5},{4,6},{5,7},{6,0},{7,1},{8,10},{9,11},{10,... | collective-permute-start | bytes 21512 | tf_op jit(solution)/shard_map/ppermute | solution.py:361
  68.0 2.6 %collective-permute-start.2 = (bf16[8,448]{1,0:T(8,128)(2,1)S(1)}, bf16[8,448]{1,0:T(8,128)(2,1)S(1)}, u32[]{:S(2)}, u32[]{:S(2)}) collective-permute-start(bf16[8,448]{1,0:T(8,128)(2,1)S(1)} %get-tuple-element.21), channel_id=1, source_target_pairs={{0,4},{1,5},{2,6},{3,7},{4,0},{5,1},{6,2},{7,3},{8,12},{9,13},{10,... | collective-permute-start | bytes 21512 | tf_op jit(solution)/shard_map/ppermute | solution.py:361
  70.6 1.1 %collective-permute-start.3 = (bf16[8,448]{1,0:T(8,128)(2,1)S(1)}, bf16[8,448]{1,0:T(8,128)(2,1)S(1)}, u32[]{:S(2)}, u32[]{:S(2)}) collective-permute-start(bf16[8,448]{1,0:T(8,128)(2,1)S(1)} %get-tuple-element.22), channel_id=1, source_target_pairs={{0,6},{1,7},{2,0},{3,1},{4,2},{5,3},{6,4},{7,5},{8,14},{9,15},{10,... | collective-permute-start | bytes 21512 | tf_op jit(solution)/shard_map/ppermute | solution.py:361
  71.7 0.0 collective-permute-done.1.rest_0_
  71.7 0.3 collective-permute-done.2.rest_1_
  72.0 1.4 %collective-permute-done.3.rest_2_ = bf16[8,448]{1,0:T(8,128)(2,1)S(1)} collective-permute-done((bf16[8,448]{1,0:T(8,128)(2,1)S(1)}, bf16[8,448]{1,0:T(8,128)(2,1)S(1)}, u32[]{:S(2)}, u32[]{:S(2)}) %collective-permute-start.3) | collective-permute-done | bytes 7200 | tf_op jit(solution)/shard_map/ppermute | solution.py:361
  73.4 0.0 copy-done.1
  73.4 0.6 shard_map.105
  (1 shorter events, 0.0 us)
Async XLA Ops:
  24.5 36.2 %copy-start = (bf16[1792,448]{0,1:T(8,128)(2,1)S(1)}, bf16[1792,448]{0,1:T(8,128)(2,1)}, u32[]{:S(2)}) copy-start(bf16[1792,448]{0,1:T(8,128)(2,1)} %param.18) | copy-start | bytes 4816900
  31.2 42.2 %copy-start.1 = (bf16[2,4,448]{2,1,0:T(4,128)(2,1)S(1)}, bf16[2,4,448]{2,1,0:T(4,128)(2,1)}, u32[]{:S(2)}) copy-start(bf16[2,4,448]{2,1,0:T(4,128)(2,1)} %rest_3_.1) | copy-start | bytes 21508
  61.3 5.3 %collective-permute-start = (bf16[4,8,448]{2,1,0:T(8,128)(2,1)S(1)}, bf16[4,8,448]{2,1,0:T(8,128)(2,1)S(1)}, u32[]{:S(2)}, u32[]{:S(2)}) collective-permute-start(bf16[4,8,448]{2,1,0:T(8,128)(2,1)S(1)} %get-tuple-element.18), channel_id=1, source_target_pairs={{0,1},{1,0},{2,3},{3,2},{4,5},{5,4},{6,7},{7,6},{8,9},{9,8},{10,11... | collective-permute-start | bytes 86024 | tf_op jit(solution)/shard_map/ppermute | solution.py:351
  66.6 5.1 %collective-permute-start.1 = (bf16[8,448]{1,0:T(8,128)(2,1)S(1)}, bf16[8,448]{1,0:T(8,128)(2,1)S(1)}, u32[]{:S(2)}, u32[]{:S(2)}) collective-permute-start(bf16[8,448]{1,0:T(8,128)(2,1)S(1)} %get-tuple-element.20), channel_id=1, source_target_pairs={{0,2},{1,3},{2,4},{3,5},{4,6},{5,7},{6,0},{7,1},{8,10},{9,11},{10,... | collective-permute-start | bytes 21512 | tf_op jit(solution)/shard_map/ppermute | solution.py:361
  68.0 4.0 %collective-permute-start.2 = (bf16[8,448]{1,0:T(8,128)(2,1)S(1)}, bf16[8,448]{1,0:T(8,128)(2,1)S(1)}, u32[]{:S(2)}, u32[]{:S(2)}) collective-permute-start(bf16[8,448]{1,0:T(8,128)(2,1)S(1)} %get-tuple-element.21), channel_id=1, source_target_pairs={{0,4},{1,5},{2,6},{3,7},{4,0},{5,1},{6,2},{7,3},{8,12},{9,13},{10,... | collective-permute-start | bytes 21512 | tf_op jit(solution)/shard_map/ppermute | solution.py:361
  70.6 2.8 %collective-permute-start.3 = (bf16[8,448]{1,0:T(8,128)(2,1)S(1)}, bf16[8,448]{1,0:T(8,128)(2,1)S(1)}, u32[]{:S(2)}, u32[]{:S(2)}) collective-permute-start(bf16[8,448]{1,0:T(8,128)(2,1)S(1)} %get-tuple-element.22), channel_id=1, source_target_pairs={{0,6},{1,7},{2,0},{3,1},{4,2},{5,3},{6,4},{7,5},{8,14},{9,15},{10,... | collective-permute-start | bytes 21512 | tf_op jit(solution)/shard_map/ppermute | solution.py:361

commit v4 on v2

--- a/solution.py
+++ b/solution.py
@@ -45,19 +45,35 @@
     return pltpu.roll(x, x.shape[1] - lanes, 1) if lanes else x
 
 
+def stage_kernel(keys, out, sems):
+    copies = []
+    for b in range(sems.shape[0]):
+        rows = pl.ds(b * BLK, BLK)
+        copies.append(pltpu.make_async_copy(keys.at[rows], out.at[rows], sems.at[b]))
+    for copy in copies:
+        copy.start()
+    for copy in copies:
+        copy.wait()
+
+
 def attend_kernel(
-    blocks, hdim, meta, slopes, query, own_stats, keys, values, out, kbuf, vbuf, sems
+    blocks, hdim, meta, slopes, query, own_stats, staged, keys, values, out, kbuf, vbuf, sems
 ):
     width = keys.shape[1]
     per = STEPS * GROUP
     packs = BLK // per
     scale = 1.0 / math.sqrt(hdim)
-    copies = []
-    for i, (src, dst) in enumerate(((keys, kbuf), (values, vbuf))):
-        for b in range(blocks):
-            rows = pl.ds(b * BLK, BLK)
-            copies.append(pltpu.make_async_copy(src.at[rows], dst.at[rows], sems.at[i, b]))
-    for copy in copies:
+    ready = staged.shape[0] // BLK
+    key_copies = {}
+    for b in range(ready, blocks):
+        rows = pl.ds((b - ready) * BLK, BLK)
+        copy = pltpu.make_async_copy(keys.at[pl.ds(b * BLK, BLK)], kbuf.at[rows], sems.at[0, b])
+        key_copies[b] = copy
+    value_copies = []
+    for b in range(blocks):
+        rows = pl.ds(b * BLK, BLK)
+        value_copies.append(pltpu.make_async_copy(values.at[rows], vbuf.at[rows], sems.at[1, b]))
+    for copy in (*key_copies.values(), *value_copies):
         copy.start()
     mask = head_mask(width, hdim)
     lane = iota((STEPS, STATS), 1)
@@ -74,16 +90,23 @@
             q = query[meta[0, b]].astype(jnp.float32)
             for s in range(STEPS):
                 spread.append(jnp.where(mask, q[s : s + 1], 0.0).astype(jnp.bfloat16))
-        for b in range(g * packs, (g + 1) * packs):
-            copies[b].wait()
-        raw.append(
+        spread = jnp.concatenate(spread, axis=0)
+        first, last = g * packs, (g + 1) * packs
+        split = min(max(first, ready), last)
+        pieces = []
+        if split > first:
+            pieces.append(staged[first * BLK : split * BLK])
+        if last > split:
+            for b in range(split, last):
+                key_copies[b].wait()
+            pieces.append(kbuf[(split - ready) * BLK : (last - ready) * BLK])
+        tiles = [
             lax.dot_general(
-                kbuf[g * packs * BLK : (g + 1) * packs * BLK],
-                jnp.concatenate(spread, axis=0),
-                (((1,), (1,)), ((), ())),
-                preferred_element_type=jnp.float32,
+                piece, spread, (((1,), (1,)), ((), ())), preferred_element_type=jnp.float32
             )
-        )
+            for piece in pieces
+        ]
+        raw.append(tiles[0] if len(tiles) == 1 else jnp.concatenate(tiles, axis=0))
 
     pack = iota((BLK, BLK), 1) // per
     when = (iota((BLK, BLK), 1) % per) // GROUP - iota((BLK, BLK), 0)
@@ -135,7 +158,7 @@
     acc = None
     for b in range(blocks):
         k = b % packs
-        copies[blocks + b].wait()
+        value_copies[b].wait()
         full = jnp.dot(
             weights[b // packs][k * per : (k + 1) * per],
             vbuf[b * BLK : (b + 1) * BLK],
@@ -272,6 +295,10 @@
         out[r] = x[...]
 
 
+def in_hbm(x):
+    return pltpu.with_memory_space_constraint(x, pltpu.HBM)
+
+
 def on_device(kernel, out_shape, in_spaces, limit, **more):
     return pl.pallas_call(
         kernel,
@@ -367,24 +394,29 @@
         4,
     )(own_query, new_keys.reshape(STEPS, width), new_values.reshape(STEPS, width), lanes)
 
+    ready = blocks - 1
+    staged = on_device(
+        stage_kernel,
+        pltpu.VMEM((ready * BLK, width), jnp.bfloat16),
+        [pltpu.HBM],
+        2,
+        out_specs=pl.BlockSpec(memory_space=pl.ANY),
+        scratch_shapes=[pltpu.SemaphoreType.DMA((ready,))],
+        cost_estimate=pl.CostEstimate(
+            flops=0, bytes_accessed=4 * ready * BLK * width, transcendentals=0
+        ),
+    )(in_hbm(cache_keys))
     partials = on_device(
         functools.partial(attend_kernel, blocks, hdim),
         jax.ShapeDtypeStruct((peers, STEPS, width + STATS), jnp.bfloat16),
-        [smem, vmem, vmem, pl.ANY, pltpu.HBM, pltpu.HBM],
+        [smem, vmem, vmem, pl.ANY, vmem, pltpu.HBM, pltpu.HBM],
         32,
         scratch_shapes=[
-            pltpu.VMEM(cache_keys.shape, jnp.bfloat16),
+            pltpu.VMEM(((blocks - ready) * BLK, width), jnp.bfloat16),
             pltpu.VMEM(cache_values.shape, jnp.bfloat16),
             pltpu.SemaphoreType.DMA((2, blocks)),
         ],
-    )(
-        table,
-        lanes,
-        everyone,
-        own_stats,
-        pltpu.with_memory_space_constraint(cache_keys, pltpu.HBM),
-        pltpu.with_memory_space_constraint(cache_values, pltpu.HBM),
-    )
+    )(table, lanes, everyone, own_stats, staged, in_hbm(cache_keys), in_hbm(cache_values))
     arrived = lax.all_to_all(partials, "seq", 0, 0, tiled=True)
 
     attended = on_device(

time: 73.7 us -> 73.8 us (level)
    pallas_call x0 -> x1, Pallas kernels: none -> 1.91 us  [body(): on_device(stage_kernel, pltpu.VMEM((ready * BLK, width), jnp.bfloat16), [...]
    pallas_call x1, Pallas kernels: 6.4 us -> 5.02 us  [body(): on_device(functools.partial(attend_kernel, blocks, hdim), jax.ShapeDtypeS...]
  transfers between devices with their start and end apart: 5 -> 5, of which waited for: 4 -> 4; matrix products, arithmetic and copies ran while one was open for 5% -> 4% of each run, Pallas kernels for 1% -> 3%
where the time goes in v4:
time: 73.8 us; the launch traced here: 73.4 us
  blocking collectives  28.7 us (39%)
  starting transfers between devices  21.5 us (29%)
  Pallas kernels  9.79 us (13%)
  waiting for transfers between devices  7.62 us (10%)
  local copies, waits for them, and re-layouts  3.06 us (4%)
  other arithmetic  2.55 us (3%)
    all_to_all x1, blocking collectives, body(): arrived = lax.all_to_all(partials, 'seq', 0, 0, tiled=True)  14.6 us
    all_to_all x1, blocking collectives, body(): lax.all_to_all(attended, 'seq', 0, 0, tiled=True)  14.1 us
    all_to_all x1, starting transfers between devices, body(): everyone = lax.all_to_all(copies, 'seq', 0, 0, tiled=True)  12 us
    all_to_all x1, waiting for transfers between devices, body(): everyone = lax.all_to_all(copies, 'seq', 0, 0, tiled=True)  5.07 us
    ppermute x3, starting transfers between devices, project_and_sum(): lax.ppermute(x, 'head', [(i, (i + 2 * hop) % groups) for i in range(group...  5.06 us
    pallas_call x1, Pallas kernels, body(): on_device(functools.partial(attend_kernel, blocks, hdim), jax.ShapeDtypeS...  5.02 us
    ppermute x1, starting transfers between devices, project_and_sum(): got = lax.ppermute(theirs, 'head', [(i, i ^ 1) for i in range(groups)])  4.41 us
    unnamed x12, local copies, waits for them, and re-layouts  2.13 us
  transfers between devices with their start and end apart: 5, of which 4 were waited for; matrix products, arithmetic and copies ran while one was open for 4% of the time, Pallas kernels for 3%

profile of v4, /device:TPU:1, one launch (start us, length us, event | category | flops | bytes accessed | tf_op | source)
XLA Modules:
  0.0 73.4 jit_solution(12542170243211288448)
XLA Ops:
  0.0 0.7 copy-done.1
  0.7 0.7 shard_map.100
  1.4 12.0 %all-to-all-start = ((bf16[32,2,1792]{2,1,0:T(2,128)(2,1)}), bf16[32,2,1792]{2,1,0:T(2,128)(2,1)S(1)}, u32[]{:S(2)}, u32[]{:S(2)}) async-start(bf16[32,2,1792]{2,1,0:T(2,128)(2,1)} %shard_map.100), calls=%async_computation | async-start | bytes 458752 | tf_op jit(solution)/shard_map/all_to_all | solution.py:383
  13.4 0.8 %select_reduce_fusion = s32[32]{0:T(128)S(1)} fusion(s32[32]{0:T(128)} %param.16), kind=kLoop, calls=%fused_computation | loop fusion | flops 3040 | bytes 256 | tf_op jit(solution)/shard_map/reduce_sum | solution.py:315
  14.2 0.7 add.28
  14.9 0.9 %select_reduce_fusion.2 = (s32[8]{0:T(128)S(1)}, s32[8]{0:T(128)S(1)}) fusion(s32[32]{0:T(128)} %param.17, s32[32]{0:T(128)S(1)} %add.28, s32[32]{0:T(128)S(1)} %select_reduce_fusion, s32[8]{0:T(128)S(1)} %iota_add_fusion), kind=kLoop, calls=%fused_computation.3 | loop fusion | flops 1776 | bytes 480 | tf_op jit(solution)/shard_map/reduce_sum | solution.py:319
  15.7 0.7 pad.4
  16.4 0.1 broadcast_in_dim_tile.3.slopes
  16.5 1.9 %shard_map.102.staged = bf16[896,1792]{1,0:T(8,128)(2,1)S(1)} custom-call(bf16[1024,1792]{1,0:T(8,128)(2,1)} %keys.3), custom_call_target="tpu_custom_call" | custom-call | bytes 6422528 | tf_op jit(solution)/shard_map/pallas_call | solution.py:398
  18.4 0.4 shard_map.101
  18.8 0.2 fusion
  19.1 5.1 %all-to-all-done.query = bf16[32,2,1792]{2,1,0:T(2,128)(2,1)S(1)} async-done(((bf16[32,2,1792]{2,1,0:T(2,128)(2,1)}), bf16[32,2,1792]{2,1,0:T(2,128)(2,1)S(1)}, u32[]{:S(2)}, u32[]{:S(2)}) %all-to-all-start) | async-done | bytes 229408 | tf_op jit(solution)/shard_map/all_to_all | solution.py:383
  24.1 5.0 %shard_map.103 = bf16[32,2,1920]{2,1,0:T(2,128)(2,1)S(1)} custom-call(s32[4,8]{1,0:T(4,128)S(1)} %pad_add_fusion.meta, f32[1,128]{1,0:T(1,128)S(1)} %broadcast_in_dim_tile.3.slopes, bf16[32,2,1792]{2,1,0:T(2,128)(2,1)S(1)} %all-to-all-done.query, f32[2,128]{1,0:T(2,128)S(1)} %get-tuple-element.13.own_stats, bf16[896,1792]{1,0:T(8,128)(2,1)S(1)} %shard_map.102.staged, ...), custom_call_target="tpu_custom_call" | custom-call | tf_op jit(solution)/shard_map/pallas_call | solution.py:409
  29.2 0.0 copy-start.3
  29.2 14.6 %all_to_all.15 = bf16[32,2,1920]{2,1,0:T(2,128)(2,1)S(1)} all-to-all(bf16[32,2,1920]{2,1,0:T(2,128)(2,1)S(1)} %shard_map.103), channel_id=1, replica_groups=mesh['seq'=32,'head'=8] {'seq'}, dimensions={0} | all-to-all | bytes 491520 | tf_op jit(solution)/shard_map/all_to_all | solution.py:420
  43.8 0.1 reshape.72.parts
  43.9 0.6 shard_map.104
  44.5 14.1 %all_to_all.16 = bf16[32,2,1792]{2,1,0:T(2,128)(2,1)S(1)} all-to-all(bf16[32,2,1792]{2,1,0:T(2,128)(2,1)S(1)} %shard_map.104), channel_id=1, replica_groups=mesh['seq'=32,'head'=8] {'seq'}, dimensions={0} | all-to-all | bytes 458752 | tf_op jit(solution)/shard_map/all_to_all | solution.py:428
  58.6 0.1 reshape.73.rows
  58.7 0.0 copy-start
  58.7 1.4 %copy-done = bf16[1792,448]{0,1:T(8,128)(2,1)S(1)} copy-done((bf16[1792,448]{0,1:T(8,128)(2,1)S(1)}, bf16[1792,448]{0,1:T(8,128)(2,1)}, u32[]{:S(2)}) %copy-start) | copy-done | bytes 1605656
  60.1 0.6 shard_map.105
  60.7 4.4 %collective-permute-start = (bf16[4,8,448]{2,1,0:T(8,128)(2,1)S(1)}, bf16[4,8,448]{2,1,0:T(8,128)(2,1)S(1)}, u32[]{:S(2)}, u32[]{:S(2)}) collective-permute-start(bf16[4,8,448]{2,1,0:T(8,128)(2,1)S(1)} %get-tuple-element.16), channel_id=1, source_target_pairs={{0,1},{1,0},{2,3},{3,2},{4,5},{5,4},{6,7},{7,6},{8,9},{9,8},{10,11... | collective-permute-start | bytes 86024 | tf_op jit(solution)/shard_map/ppermute | solution.py:338
  65.1 0.9 %collective-permute-done.got = bf16[4,8,448]{2,1,0:T(8,128)(2,1)S(1)} collective-permute-done((bf16[4,8,448]{2,1,0:T(8,128)(2,1)S(1)}, bf16[4,8,448]{2,1,0:T(8,128)(2,1)S(1)}, u32[]{:S(2)}, u32[]{:S(2)}) %collective-permute-start) | collective-permute-done | bytes 28704 | tf_op jit(solution)/shard_map/ppermute | solution.py:338
  66.0 1.4 %collective-permute-start.1 = (bf16[8,448]{1,0:T(8,128)(2,1)S(1)}, bf16[8,448]{1,0:T(8,128)(2,1)S(1)}, u32[]{:S(2)}, u32[]{:S(2)}) collective-permute-start(bf16[8,448]{1,0:T(8,128)(2,1)S(1)} %get-tuple-element.18), channel_id=1, source_target_pairs={{0,2},{1,3},{2,4},{3,5},{4,6},{5,7},{6,0},{7,1},{8,10},{9,11},{10,... | collective-permute-start | bytes 21512 | tf_op jit(solution)/shard_map/ppermute | solution.py:348
  67.3 2.6 %collective-permute-start.2 = (bf16[8,448]{1,0:T(8,128)(2,1)S(1)}, bf16[8,448]{1,0:T(8,128)(2,1)S(1)}, u32[]{:S(2)}, u32[]{:S(2)}) collective-permute-start(bf16[8,448]{1,0:T(8,128)(2,1)S(1)} %get-tuple-element.19), channel_id=1, source_target_pairs={{0,4},{1,5},{2,6},{3,7},{4,0},{5,1},{6,2},{7,3},{8,12},{9,13},{10,... | collective-permute-start | bytes 21512 | tf_op jit(solution)/shard_map/ppermute | solution.py:348
  70.0 1.1 %collective-permute-start.3 = (bf16[8,448]{1,0:T(8,128)(2,1)S(1)}, bf16[8,448]{1,0:T(8,128)(2,1)S(1)}, u32[]{:S(2)}, u32[]{:S(2)}) collective-permute-start(bf16[8,448]{1,0:T(8,128)(2,1)S(1)} %get-tuple-element.20), channel_id=1, source_target_pairs={{0,6},{1,7},{2,0},{3,1},{4,2},{5,3},{6,4},{7,5},{8,14},{9,15},{10,... | collective-permute-start | bytes 21512 | tf_op jit(solution)/shard_map/ppermute | solution.py:348
  71.0 0.0 collective-permute-done.1.rest_0_
  71.0 0.3 collective-permute-done.2.rest_1_
  71.4 1.4 %collective-permute-done.3.rest_2_ = bf16[8,448]{1,0:T(8,128)(2,1)S(1)} collective-permute-done((bf16[8,448]{1,0:T(8,128)(2,1)S(1)}, bf16[8,448]{1,0:T(8,128)(2,1)S(1)}, u32[]{:S(2)}, u32[]{:S(2)}) %collective-permute-start.3) | collective-permute-done | bytes 7200 | tf_op jit(solution)/shard_map/ppermute | solution.py:348
  72.7 0.0 copy-done.3
  72.7 0.6 shard_map.107
  (14 shorter events, 0.1 us)
Async XLA Ops:
  0.0 0.7 copy-start.1
  1.4 17.0 %copy-start.2 = (bf16[2,1,1792]{2,0,1:T(2,128)(2,1)S(1)}, bf16[2,1,1792]{2,0,1:T(2,128)(2,1)}, u32[]{:S(2)}) copy-start(bf16[2,1,1792]{2,0,1:T(2,128)(2,1)} %param.10) | copy-start | bytes 21508
  1.4 17.0 %copy-start.4 = (bf16[2,1,1792]{2,0,1:T(2,128)(2,1)S(1)}, bf16[2,1,1792]{2,0,1:T(2,128)(2,1)}, u32[]{:S(2)}) copy-start(bf16[2,1,1792]{2,0,1:T(2,128)(2,1)} %param.11) | copy-start | bytes 21508
  1.4 17.0 %copy-start.5 = (bf16[2,1,1792]{2,0,1:T(2,128)(2,1)S(1)}, bf16[2,1,1792]{2,0,1:T(2,128)(2,1)}, u32[]{:S(2)}) copy-start(bf16[2,1,1792]{2,0,1:T(2,128)(2,1)} %param.12) | copy-start | bytes 21508
  1.4 22.7 %all-to-all-start = ((bf16[32,2,1792]{2,1,0:T(2,128)(2,1)}), bf16[32,2,1792]{2,1,0:T(2,128)(2,1)S(1)}, u32[]{:S(2)}, u32[]{:S(2)}) async-start(bf16[32,2,1792]{2,1,0:T(2,128)(2,1)} %shard_map.100), calls=%async_computation | async-start | bytes 458752 | tf_op jit(solution)/shard_map/all_to_all | solution.py:383
  29.2 43.6 %copy-start.3 = (bf16[2,4,448]{2,1,0:T(4,128)(2,1)S(1)}, bf16[2,4,448]{2,1,0:T(4,128)(2,1)}, u32[]{:S(2)}) copy-start(bf16[2,4,448]{2,1,0:T(4,128)(2,1)} %rest_3_.1) | copy-start | bytes 21508
  58.7 1.4 %copy-start = (bf16[1792,448]{0,1:T(8,128)(2,1)S(1)}, bf16[1792,448]{0,1:T(8,128)(2,1)}, u32[]{:S(2)}) copy-start(bf16[1792,448]{0,1:T(8,128)(2,1)} %param.18) | copy-start | bytes 4816900
  60.7 5.3 %collective-permute-start = (bf16[4,8,448]{2,1,0:T(8,128)(2,1)S(1)}, bf16[4,8,448]{2,1,0:T(8,128)(2,1)S(1)}, u32[]{:S(2)}, u32[]{:S(2)}) collective-permute-start(bf16[4,8,448]{2,1,0:T(8,128)(2,1)S(1)} %get-tuple-element.16), channel_id=1, source_target_pairs={{0,1},{1,0},{2,3},{3,2},{4,5},{5,4},{6,7},{7,6},{8,9},{9,8},{10,11... | collective-permute-start | bytes 86024 | tf_op jit(solution)/shard_map/ppermute | solution.py:338
  66.0 5.1 %collective-permute-start.1 = (bf16[8,448]{1,0:T(8,128)(2,1)S(1)}, bf16[8,448]{1,0:T(8,128)(2,1)S(1)}, u32[]{:S(2)}, u32[]{:S(2)}) collective-permute-start(bf16[8,448]{1,0:T(8,128)(2,1)S(1)} %get-tuple-element.18), channel_id=1, source_target_pairs={{0,2},{1,3},{2,4},{3,5},{4,6},{5,7},{6,0},{7,1},{8,10},{9,11},{10,... | collective-permute-start | bytes 21512 | tf_op jit(solution)/shard_map/ppermute | solution.py:348
  67.3 4.0 %collective-permute-start.2 = (bf16[8,448]{1,0:T(8,128)(2,1)S(1)}, bf16[8,448]{1,0:T(8,128)(2,1)S(1)}, u32[]{:S(2)}, u32[]{:S(2)}) collective-permute-start(bf16[8,448]{1,0:T(8,128)(2,1)S(1)} %get-tuple-element.19), channel_id=1, source_target_pairs={{0,4},{1,5},{2,6},{3,7},{4,0},{5,1},{6,2},{7,3},{8,12},{9,13},{10,... | collective-permute-start | bytes 21512 | tf_op jit(solution)/shard_map/ppermute | solution.py:348
  70.0 2.8 %collective-permute-start.3 = (bf16[8,448]{1,0:T(8,128)(2,1)S(1)}, bf16[8,448]{1,0:T(8,128)(2,1)S(1)}, u32[]{:S(2)}, u32[]{:S(2)}) collective-permute-start(bf16[8,448]{1,0:T(8,128)(2,1)S(1)} %get-tuple-element.20), channel_id=1, source_target_pairs={{0,6},{1,7},{2,0},{3,1},{4,2},{5,3},{6,4},{7,5},{8,14},{9,15},{10,... | collective-permute-start | bytes 21512 | tf_op jit(solution)/shard_map/ppermute | solution.py:348

commit v5 on v4

--- a/solution.py
+++ b/solution.py
@@ -57,7 +57,22 @@
 
 
 def attend_kernel(
-    blocks, hdim, meta, slopes, query, own_stats, staged, keys, values, out, kbuf, vbuf, sems
+    blocks,
+    hdim,
+    meta,
+    slopes,
+    query,
+    own_stats,
+    staged,
+    keys,
+    values,
+    weight,
+    out,
+    weight_out,
+    kbuf,
+    vbuf,
+    sems,
+    weight_sem,
 ):
     width = keys.shape[1]
     per = STEPS * GROUP
@@ -73,7 +88,8 @@
     for b in range(blocks):
         rows = pl.ds(b * BLK, BLK)
         value_copies.append(pltpu.make_async_copy(values.at[rows], vbuf.at[rows], sems.at[1, b]))
-    for copy in (*key_copies.values(), *value_copies):
+    weight_copy = pltpu.make_async_copy(weight, weight_out, weight_sem)
+    for copy in (*key_copies.values(), *value_copies, weight_copy):
         copy.start()
     mask = head_mask(width, hdim)
     lane = iota((STEPS, STATS), 1)
@@ -171,6 +187,7 @@
         rows.append(jnp.where(meta[2, b] == 1, row, empty))
     for b in range(blocks):
         out[meta[0, b]] = rows[b]
+    weight_copy.wait()
 
 
 def own_kernel(heads, hdim, query, key, value, slopes, stats, acc):
@@ -325,16 +342,16 @@
     return jnp.stack([row, base, live.astype(jnp.int32), joined.astype(jnp.int32)])
 
 
-def project_and_sum(rows, out_weight, residual, groups):
+def project_and_sum(rows, weight, residual, groups):
     chips = groups // 2
-    size, columns = rows.shape[0] // groups, out_weight.shape[1]
+    size, columns = rows.shape[0] // groups, weight.shape[0]
     each = (chips, size, columns)
     mine, theirs = on_device(
         project_kernel,
         (jax.ShapeDtypeStruct(each, jnp.float32), jax.ShapeDtypeStruct(each, jnp.bfloat16)),
         [pltpu.VMEM] * 2,
         16,
-    )(rows, out_weight.T)
+    )(rows, weight)
     got = lax.ppermute(theirs, "head", [(i, i ^ 1) for i in range(groups)])
     share = jax.ShapeDtypeStruct((size, columns), jnp.bfloat16)
     total, *shares = on_device(
@@ -406,17 +423,31 @@
             flops=0, bytes_accessed=4 * ready * BLK * width, transcendentals=0
         ),
     )(in_hbm(cache_keys))
-    partials = on_device(
+    partials, weight = on_device(
         functools.partial(attend_kernel, blocks, hdim),
-        jax.ShapeDtypeStruct((peers, STEPS, width + STATS), jnp.bfloat16),
-        [smem, vmem, vmem, pl.ANY, vmem, pltpu.HBM, pltpu.HBM],
+        (
+            jax.ShapeDtypeStruct((peers, STEPS, width + STATS), jnp.bfloat16),
+            pltpu.HBM(out_weight.shape[::-1], jnp.bfloat16),
+        ),
+        [smem, vmem, vmem, pl.ANY, vmem] + [pltpu.HBM] * 3,
         32,
+        out_specs=(pl.BlockSpec(memory_space=vmem), pl.BlockSpec(memory_space=pl.ANY)),
         scratch_shapes=[
             pltpu.VMEM(((blocks - ready) * BLK, width), jnp.bfloat16),
             pltpu.VMEM(cache_values.shape, jnp.bfloat16),
             pltpu.SemaphoreType.DMA((2, blocks)),
+            pltpu.SemaphoreType.DMA,
         ],
-    )(table, lanes, everyone, own_stats, staged, in_hbm(cache_keys), in_hbm(cache_values))
+    )(
+        table,
+        lanes,
+        everyone,
+        own_stats,
+        staged,
+        in_hbm(cache_keys),
+        in_hbm(cache_values),
+        in_hbm(out_weight.T),
+    )
     arrived = lax.all_to_all(partials, "seq", 0, 0, tiled=True)
 
     attended = on_device(
@@ -427,7 +458,7 @@
     )(arrived.reshape(peers * STEPS, width + STATS), own_stats, own_acc)
     rows = lax.all_to_all(attended, "seq", 0, 0, tiled=True).reshape(peers * STEPS, width)
 
-    return project_and_sum(rows, out_weight, residual, groups)
+    return project_and_sum(rows, weight, residual, groups)
 
 
 def solution(mesh):

time: 73.8 us -> 118 us (1.60)
  Pallas kernels: 9.79 us -> 55.3 us
  local copies, waits for them, and re-layouts: 3.06 us -> 1.65 us
    pallas_call x1, Pallas kernels: 5.02 us -> 50.5 us  [body(): on_device(functools.partial(attend_kernel, blocks, hdim), (jax.ShapeDtype...]
    unnamed x12, local copies, waits for them, and re-layouts: 2.13 us -> 0.72 us
  transfers between devices with their start and end apart: 5 -> 5, of which waited for: 4 -> 4; matrix products, arithmetic and copies ran while one was open for 4% -> 3% of each run, Pallas kernels for 3% -> 2%
where the time goes in v5:
time: 118 us; the launch traced here: 117 us
  Pallas kernels  55.3 us (47%)
  blocking collectives  28.9 us (24%)
  starting transfers between devices  21.3 us (18%)
  waiting for transfers between devices  7.58 us (6%)
  other arithmetic  2.55 us (2%)
  local copies, waits for them, and re-layouts  1.65 us (1%)
    pallas_call x1, Pallas kernels, body(): on_device(functools.partial(attend_kernel, blocks, hdim), (jax.ShapeDtype...  50.5 us
    all_to_all x1, blocking collectives, body(): arrived = lax.all_to_all(partials, 'seq', 0, 0, tiled=True)  14.7 us
    all_to_all x1, blocking collectives, body(): lax.all_to_all(attended, 'seq', 0, 0, tiled=True)  14.1 us
    all_to_all x1, starting transfers between devices, body(): everyone = lax.all_to_all(copies, 'seq', 0, 0, tiled=True)  11.9 us
    ppermute x3, starting transfers between devices, project_and_sum(): lax.ppermute(x, 'head', [(i, (i + 2 * hop) % groups) for i in range(group...  5.06 us
    all_to_all x1, waiting for transfers between devices, body(): everyone = lax.all_to_all(copies, 'seq', 0, 0, tiled=True)  5.02 us
    ppermute x1, starting transfers between devices, project_and_sum(): got = lax.ppermute(theirs, 'head', [(i, i ^ 1) for i in range(groups)])  4.41 us
  transfers between devices with their start and end apart: 5, of which 4 were waited for; matrix products, arithmetic and copies ran while one was open for 3% of the time, Pallas kernels for 2%

profile of v5, /device:TPU:1, one launch (start us, length us, event | category | flops | bytes accessed | tf_op | source)
XLA Modules:
  0.0 117.4 jit_solution(1377739089013334010)
XLA Ops:
  0.0 0.7 copy-done.1
  0.7 0.7 shard_map.100
  1.4 11.9 %all-to-all-start = ((bf16[32,2,1792]{2,1,0:T(2,128)(2,1)}), bf16[32,2,1792]{2,1,0:T(2,128)(2,1)S(1)}, u32[]{:S(2)}, u32[]{:S(2)}) async-start(bf16[32,2,1792]{2,1,0:T(2,128)(2,1)} %shard_map.100), calls=%async_computation | async-start | bytes 458752 | tf_op jit(solution)/shard_map/all_to_all | solution.py:400
  13.3 0.8 select_reduce_fusion
  14.1 0.7 add.28
  14.7 0.9 select_reduce_fusion.2
  15.6 0.7 pad.4
  16.3 0.1 broadcast_in_dim_tile.3.slopes
  16.4 0.0 copy-start.5
  16.4 1.9 %shard_map.102.staged = bf16[896,1792]{1,0:T(8,128)(2,1)S(1)} custom-call(bf16[1024,1792]{1,0:T(8,128)(2,1)} %keys.3), custom_call_target="tpu_custom_call" | custom-call | bytes 6422528 | tf_op jit(solution)/shard_map/pallas_call | solution.py:415
  18.3 0.0 copy-done.2
  18.3 0.0 copy-done.4
  18.3 0.4 shard_map.101
  18.7 0.2 fusion
  19.0 5.0 %all-to-all-done.query = bf16[32,2,1792]{2,1,0:T(2,128)(2,1)S(1)} async-done(((bf16[32,2,1792]{2,1,0:T(2,128)(2,1)}), bf16[32,2,1792]{2,1,0:T(2,128)(2,1)S(1)}, u32[]{:S(2)}, u32[]{:S(2)}) %all-to-all-start) | async-done | bytes 229408 | tf_op jit(solution)/shard_map/all_to_all | solution.py:400
  24.0 50.5 %shard_map.103 = (bf16[32,2,1920]{2,1,0:T(2,128)(2,1)S(1)}, bf16[448,1792]{1,0:T(8,128)(2,1)}) custom-call(s32[4,8]{1,0:T(4,128)S(1)} %pad_add_fusion.meta, f32[1,128]{1,0:T(1,128)S(1)} %broadcast_in_dim_tile.3.slopes, bf16[32,2,1792]{2,1,0:T(2,128)(2,1)S(1)} %all-to-all-done.query, f32[2,128]{1,0:T(2,128)S(1)} %get-tuple-element.15.own_stats, ...), custom_call_target="tpu_custom_call" | custom-call | tf_op jit(solution)/shard_map/pallas_call | solution.py:426
  74.5 0.0 copy-start.3
  74.5 14.7 %all_to_all.15 = bf16[32,2,1920]{2,1,0:T(2,128)(2,1)S(1)} all-to-all(bf16[32,2,1920]{2,1,0:T(2,128)(2,1)S(1)} %get-tuple-element.16), channel_id=1, replica_groups=mesh['seq'=32,'head'=8] {'seq'}, dimensions={0} | all-to-all | bytes 491520 | tf_op jit(solution)/shard_map/all_to_all | solution.py:451
  89.2 0.1 reshape.72.parts
  89.3 0.6 shard_map.104
  89.9 14.1 %all_to_all.16 = bf16[32,2,1792]{2,1,0:T(2,128)(2,1)S(1)} all-to-all(bf16[32,2,1792]{2,1,0:T(2,128)(2,1)S(1)} %shard_map.104), channel_id=1, replica_groups=mesh['seq'=32,'head'=8] {'seq'}, dimensions={0} | all-to-all | bytes 458752 | tf_op jit(solution)/shard_map/all_to_all | solution.py:459
  104.0 0.1 reshape.73.rows
  104.1 0.6 shard_map.105
  104.7 4.4 %collective-permute-start = (bf16[4,8,448]{2,1,0:T(8,128)(2,1)S(1)}, bf16[4,8,448]{2,1,0:T(8,128)(2,1)S(1)}, u32[]{:S(2)}, u32[]{:S(2)}) collective-permute-start(bf16[4,8,448]{2,1,0:T(8,128)(2,1)S(1)} %get-tuple-element.20), channel_id=1, source_target_pairs={{0,1},{1,0},{2,3},{3,2},{4,5},{5,4},{6,7},{7,6},{8,9},{9,8},{10,11... | collective-permute-start | bytes 86024 | tf_op jit(solution)/shard_map/ppermute | solution.py:355
  109.1 0.9 collective-permute-done.got
  110.0 1.4 %collective-permute-start.1 = (bf16[8,448]{1,0:T(8,128)(2,1)S(1)}, bf16[8,448]{1,0:T(8,128)(2,1)S(1)}, u32[]{:S(2)}, u32[]{:S(2)}) collective-permute-start(bf16[8,448]{1,0:T(8,128)(2,1)S(1)} %get-tuple-element.22), channel_id=1, source_target_pairs={{0,2},{1,3},{2,4},{3,5},{4,6},{5,7},{6,0},{7,1},{8,10},{9,11},{10,... | collective-permute-start | bytes 21512 | tf_op jit(solution)/shard_map/ppermute | solution.py:365
  111.4 2.6 %collective-permute-start.2 = (bf16[8,448]{1,0:T(8,128)(2,1)S(1)}, bf16[8,448]{1,0:T(8,128)(2,1)S(1)}, u32[]{:S(2)}, u32[]{:S(2)}) collective-permute-start(bf16[8,448]{1,0:T(8,128)(2,1)S(1)} %get-tuple-element.23), channel_id=1, source_target_pairs={{0,4},{1,5},{2,6},{3,7},{4,0},{5,1},{6,2},{7,3},{8,12},{9,13},{10,... | collective-permute-start | bytes 21512 | tf_op jit(solution)/shard_map/ppermute | solution.py:365
  114.0 1.1 collective-permute-start.3
  115.1 0.0 collective-permute-done.1.rest_0_
  115.1 0.3 collective-permute-done.2.rest_1_
  115.4 1.4 %collective-permute-done.3.rest_2_ = bf16[8,448]{1,0:T(8,128)(2,1)S(1)} collective-permute-done((bf16[8,448]{1,0:T(8,128)(2,1)S(1)}, bf16[8,448]{1,0:T(8,128)(2,1)S(1)}, u32[]{:S(2)}, u32[]{:S(2)}) %collective-permute-start.3) | collective-permute-done | bytes 7200 | tf_op jit(solution)/shard_map/ppermute | solution.py:365
  116.8 0.6 shard_map.107
  (14 shorter events, 0.1 us)
Async XLA Ops:
  0.0 0.7 copy-start.1
  1.4 22.6 %all-to-all-start = ((bf16[32,2,1792]{2,1,0:T(2,128)(2,1)}), bf16[32,2,1792]{2,1,0:T(2,128)(2,1)S(1)}, u32[]{:S(2)}, u32[]{:S(2)}) async-start(bf16[32,2,1792]{2,1,0:T(2,128)(2,1)} %shard_map.100), calls=%async_computation | async-start | bytes 458752 | tf_op jit(solution)/shard_map/all_to_all | solution.py:400
  16.4 2.0 %copy-start.2 = (bf16[2,1,1792]{2,0,1:T(2,128)(2,1)S(1)}, bf16[2,1,1792]{2,0,1:T(2,128)(2,1)}, u32[]{:S(2)}) copy-start(bf16[2,1,1792]{2,0,1:T(2,128)(2,1)} %param.10) | copy-start | bytes 21508
  16.4 2.0 %copy-start.4 = (bf16[2,1,1792]{2,0,1:T(2,128)(2,1)S(1)}, bf16[2,1,1792]{2,0,1:T(2,128)(2,1)}, u32[]{:S(2)}) copy-start(bf16[2,1,1792]{2,0,1:T(2,128)(2,1)} %param.11) | copy-start | bytes 21508
  16.4 2.0 %copy-start.5 = (bf16[2,1,1792]{2,0,1:T(2,128)(2,1)S(1)}, bf16[2,1,1792]{2,0,1:T(2,128)(2,1)}, u32[]{:S(2)}) copy-start(bf16[2,1,1792]{2,0,1:T(2,128)(2,1)} %param.12) | copy-start | bytes 21508
  74.5 29.6 %copy-start = (bf16[448,1792]{1,0:T(8,128)(2,1)S(1)}, bf16[448,1792]{1,0:T(8,128)(2,1)}, u32[]{:S(2)}) copy-start(bf16[448,1792]{1,0:T(8,128)(2,1)} %get-tuple-element.18.weight) | copy-start | bytes 4816900
  74.5 42.3 %copy-start.3 = (bf16[2,4,448]{2,1,0:T(4,128)(2,1)S(1)}, bf16[2,4,448]{2,1,0:T(4,128)(2,1)}, u32[]{:S(2)}) copy-start(bf16[2,4,448]{2,1,0:T(4,128)(2,1)} %rest_3_.1) | copy-start | bytes 21508
  104.7 5.3 %collective-permute-start = (bf16[4,8,448]{2,1,0:T(8,128)(2,1)S(1)}, bf16[4,8,448]{2,1,0:T(8,128)(2,1)S(1)}, u32[]{:S(2)}, u32[]{:S(2)}) collective-permute-start(bf16[4,8,448]{2,1,0:T(8,128)(2,1)S(1)} %get-tuple-element.20), channel_id=1, source_target_pairs={{0,1},{1,0},{2,3},{3,2},{4,5},{5,4},{6,7},{7,6},{8,9},{9,8},{10,11... | collective-permute-start | bytes 86024 | tf_op jit(solution)/shard_map/ppermute | solution.py:355
  110.0 5.1 %collective-permute-start.1 = (bf16[8,448]{1,0:T(8,128)(2,1)S(1)}, bf16[8,448]{1,0:T(8,128)(2,1)S(1)}, u32[]{:S(2)}, u32[]{:S(2)}) collective-permute-start(bf16[8,448]{1,0:T(8,128)(2,1)S(1)} %get-tuple-element.22), channel_id=1, source_target_pairs={{0,2},{1,3},{2,4},{3,5},{4,6},{5,7},{6,0},{7,1},{8,10},{9,11},{10,... | collective-permute-start | bytes 21512 | tf_op jit(solution)/shard_map/ppermute | solution.py:365
  111.4 4.0 %collective-permute-start.2 = (bf16[8,448]{1,0:T(8,128)(2,1)S(1)}, bf16[8,448]{1,0:T(8,128)(2,1)S(1)}, u32[]{:S(2)}, u32[]{:S(2)}) collective-permute-start(bf16[8,448]{1,0:T(8,128)(2,1)S(1)} %get-tuple-element.23), channel_id=1, source_target_pairs={{0,4},{1,5},{2,6},{3,7},{4,0},{5,1},{6,2},{7,3},{8,12},{9,13},{10,... | collective-permute-start | bytes 21512 | tf_op jit(solution)/shard_map/ppermute | solution.py:365
  114.0 2.8 %collective-permute-start.3 = (bf16[8,448]{1,0:T(8,128)(2,1)S(1)}, bf16[8,448]{1,0:T(8,128)(2,1)S(1)}, u32[]{:S(2)}, u32[]{:S(2)}) collective-permute-start(bf16[8,448]{1,0:T(8,128)(2,1)S(1)} %get-tuple-element.24), channel_id=1, source_target_pairs={{0,6},{1,7},{2,0},{3,1},{4,2},{5,3},{6,4},{7,5},{8,14},{9,15},{10,... | collective-permute-start | bytes 21512 | tf_op jit(solution)/shard_map/ppermute | solution.py:365

commit v6 on v5

--- a/solution.py
+++ b/solution.py
@@ -71,8 +71,9 @@
     weight_out,
     kbuf,
     vbuf,
+    wbuf,
     sems,
-    weight_sem,
+    weight_sems,
 ):
     width = keys.shape[1]
     per = STEPS * GROUP
@@ -88,8 +89,9 @@
     for b in range(blocks):
         rows = pl.ds(b * BLK, BLK)
         value_copies.append(pltpu.make_async_copy(values.at[rows], vbuf.at[rows], sems.at[1, b]))
-    weight_copy = pltpu.make_async_copy(weight, weight_out, weight_sem)
-    for copy in (*key_copies.values(), *value_copies, weight_copy):
+    weight_in = pltpu.make_async_copy(weight, wbuf, weight_sems.at[0])
+    weight_back = pltpu.make_async_copy(wbuf, weight_out, weight_sems.at[1])
+    for copy in (*key_copies.values(), *value_copies, weight_in):
         copy.start()
     mask = head_mask(width, hdim)
     lane = iota((STEPS, STATS), 1)
@@ -185,9 +187,12 @@
         tail = jnp.concatenate([x[b : b + 1] for x in stats], axis=0)
         row = jnp.concatenate([acc, tail], axis=1).astype(out.dtype)
         rows.append(jnp.where(meta[2, b] == 1, row, empty))
+        if b == blocks // 2:
+            weight_in.wait()
+            weight_back.start()
     for b in range(blocks):
         out[meta[0, b]] = rows[b]
-    weight_copy.wait()
+    weight_back.wait()
 
 
 def own_kernel(heads, hdim, query, key, value, slopes, stats, acc):
@@ -435,8 +440,9 @@
         scratch_shapes=[
             pltpu.VMEM(((blocks - ready) * BLK, width), jnp.bfloat16),
             pltpu.VMEM(cache_values.shape, jnp.bfloat16),
+            pltpu.VMEM(out_weight.shape[::-1], jnp.bfloat16),
             pltpu.SemaphoreType.DMA((2, blocks)),
-            pltpu.SemaphoreType.DMA,
+            pltpu.SemaphoreType.DMA((2,)),
         ],
     )(
         table,

time: 118 us -> 72.8 us (0.62)
  Pallas kernels: 55.3 us -> 10.4 us
    pallas_call x1, Pallas kernels: 50.5 us -> 5.56 us  [body(): on_device(functools.partial(attend_kernel, blocks, hdim), (jax.ShapeDtype...]
  transfers between devices with their start and end apart: 5 -> 5, of which waited for: 4 -> 4; matrix products, arithmetic and copies ran while one was open for 3% -> 5% of each run, Pallas kernels for 2% -> 3%
where the time goes in v6:
time: 72.8 us; the launch traced here: 72.5 us
  blocking collectives  28.9 us (40%)
  starting transfers between devices  21.3 us (29%)
  Pallas kernels  10.4 us (14%)
  waiting for transfers between devices  7.58 us (10%)
  other arithmetic  2.55 us (4%)
  local copies, waits for them, and re-layouts  1.65 us (2%)
    all_to_all x1, blocking collectives, body(): arrived = lax.all_to_all(partials, 'seq', 0, 0, tiled=True)  14.7 us
    all_to_all x1, blocking collectives, body(): lax.all_to_all(attended, 'seq', 0, 0, tiled=True)  14.1 us
    all_to_all x1, starting transfers between devices, body(): everyone = lax.all_to_all(copies, 'seq', 0, 0, tiled=True)  11.9 us
    pallas_call x1, Pallas kernels, body(): on_device(functools.partial(attend_kernel, blocks, hdim), (jax.ShapeDtype...  5.56 us
    ppermute x3, starting transfers between devices, project_and_sum(): lax.ppermute(x, 'head', [(i, (i + 2 * hop) % groups) for i in range(group...  5.07 us
    all_to_all x1, waiting for transfers between devices, body(): everyone = lax.all_to_all(copies, 'seq', 0, 0, tiled=True)  5.02 us
    ppermute x1, starting transfers between devices, project_and_sum(): got = lax.ppermute(theirs, 'head', [(i, i ^ 1) for i in range(groups)])  4.41 us
    pallas_call x1, Pallas kernels, body(): on_device(stage_kernel, pltpu.VMEM((ready * BLK, width), jnp.bfloat16), [...  1.94 us
  transfers between devices with their start and end apart: 5, of which 4 were waited for; matrix products, arithmetic and copies ran while one was open for 5% of the time, Pallas kernels for 3%

profile of v6, /device:TPU:1, one launch (start us, length us, event | category | flops | bytes accessed | tf_op | source)
XLA Modules:
  0.0 72.5 jit_solution(9795524393030912644)
XLA Ops:
  0.0 0.7 copy-done.1
  0.7 0.7 shard_map.100
  1.4 11.9 %all-to-all-start = ((bf16[32,2,1792]{2,1,0:T(2,128)(2,1)}), bf16[32,2,1792]{2,1,0:T(2,128)(2,1)S(1)}, u32[]{:S(2)}, u32[]{:S(2)}) async-start(bf16[32,2,1792]{2,1,0:T(2,128)(2,1)} %shard_map.100), calls=%async_computation | async-start | bytes 458752 | tf_op jit(solution)/shard_map/all_to_all | solution.py:405
  13.3 0.8 %select_reduce_fusion = s32[32]{0:T(128)S(1)} fusion(s32[32]{0:T(128)} %param.16), kind=kLoop, calls=%fused_computation | loop fusion | flops 3040 | bytes 256 | tf_op jit(solution)/shard_map/reduce_sum | solution.py:337
  14.1 0.7 add.28
  14.7 0.9 %select_reduce_fusion.2 = (s32[8]{0:T(128)S(1)}, s32[8]{0:T(128)S(1)}) fusion(s32[32]{0:T(128)} %param.17, s32[32]{0:T(128)S(1)} %add.28, s32[32]{0:T(128)S(1)} %select_reduce_fusion, s32[8]{0:T(128)S(1)} %iota_add_fusion), kind=kLoop, calls=%fused_computation.3 | loop fusion | flops 1776 | bytes 480 | tf_op jit(solution)/shard_map/reduce_sum | solution.py:341
  15.6 0.7 pad.4
  16.3 0.1 broadcast_in_dim_tile.3.slopes
  16.4 0.0 copy-start.5
  16.4 1.9 %shard_map.102.staged = bf16[896,1792]{1,0:T(8,128)(2,1)S(1)} custom-call(bf16[1024,1792]{1,0:T(8,128)(2,1)} %keys.3), custom_call_target="tpu_custom_call" | custom-call | bytes 6422528 | tf_op jit(solution)/shard_map/pallas_call | solution.py:420
  18.3 0.0 copy-done.2
  18.3 0.0 copy-done.4
  18.3 0.4 shard_map.101
  18.7 0.2 fusion
  19.0 5.0 %all-to-all-done.query = bf16[32,2,1792]{2,1,0:T(2,128)(2,1)S(1)} async-done(((bf16[32,2,1792]{2,1,0:T(2,128)(2,1)}), bf16[32,2,1792]{2,1,0:T(2,128)(2,1)S(1)}, u32[]{:S(2)}, u32[]{:S(2)}) %all-to-all-start) | async-done | bytes 229408 | tf_op jit(solution)/shard_map/all_to_all | solution.py:405
  24.0 5.6 %shard_map.103 = (bf16[32,2,1920]{2,1,0:T(2,128)(2,1)S(1)}, bf16[448,1792]{1,0:T(8,128)(2,1)}) custom-call(s32[4,8]{1,0:T(4,128)S(1)} %pad_add_fusion.meta, f32[1,128]{1,0:T(1,128)S(1)} %broadcast_in_dim_tile.3.slopes, bf16[32,2,1792]{2,1,0:T(2,128)(2,1)S(1)} %all-to-all-done.query, f32[2,128]{1,0:T(2,128)S(1)} %get-tuple-element.15.own_stats, ...), custom_call_target="tpu_custom_call" | custom-call | tf_op jit(solution)/shard_map/pallas_call | solution.py:431
  29.6 0.0 copy-start.3
  29.6 14.7 %all_to_all.15 = bf16[32,2,1920]{2,1,0:T(2,128)(2,1)S(1)} all-to-all(bf16[32,2,1920]{2,1,0:T(2,128)(2,1)S(1)} %get-tuple-element.16), channel_id=1, replica_groups=mesh['seq'=32,'head'=8] {'seq'}, dimensions={0} | all-to-all | bytes 491520 | tf_op jit(solution)/shard_map/all_to_all | solution.py:457
  44.3 0.1 reshape.72.parts
  44.4 0.6 shard_map.104
  45.0 14.1 %all_to_all.16 = bf16[32,2,1792]{2,1,0:T(2,128)(2,1)S(1)} all-to-all(bf16[32,2,1792]{2,1,0:T(2,128)(2,1)S(1)} %shard_map.104), channel_id=1, replica_groups=mesh['seq'=32,'head'=8] {'seq'}, dimensions={0} | all-to-all | bytes 458752 | tf_op jit(solution)/shard_map/all_to_all | solution.py:465
  59.1 0.1 reshape.73.rows
  59.2 0.6 shard_map.105
  59.8 4.4 %collective-permute-start = (bf16[4,8,448]{2,1,0:T(8,128)(2,1)S(1)}, bf16[4,8,448]{2,1,0:T(8,128)(2,1)S(1)}, u32[]{:S(2)}, u32[]{:S(2)}) collective-permute-start(bf16[4,8,448]{2,1,0:T(8,128)(2,1)S(1)} %get-tuple-element.20), channel_id=1, source_target_pairs={{0,1},{1,0},{2,3},{3,2},{4,5},{5,4},{6,7},{7,6},{8,9},{9,8},{10,11... | collective-permute-start | bytes 86024 | tf_op jit(solution)/shard_map/ppermute | solution.py:360
  64.2 0.9 %collective-permute-done.got = bf16[4,8,448]{2,1,0:T(8,128)(2,1)S(1)} collective-permute-done((bf16[4,8,448]{2,1,0:T(8,128)(2,1)S(1)}, bf16[4,8,448]{2,1,0:T(8,128)(2,1)S(1)}, u32[]{:S(2)}, u32[]{:S(2)}) %collective-permute-start) | collective-permute-done | bytes 28704 | tf_op jit(solution)/shard_map/ppermute | solution.py:360
  65.1 1.4 %collective-permute-start.1 = (bf16[8,448]{1,0:T(8,128)(2,1)S(1)}, bf16[8,448]{1,0:T(8,128)(2,1)S(1)}, u32[]{:S(2)}, u32[]{:S(2)}) collective-permute-start(bf16[8,448]{1,0:T(8,128)(2,1)S(1)} %get-tuple-element.22), channel_id=1, source_target_pairs={{0,2},{1,3},{2,4},{3,5},{4,6},{5,7},{6,0},{7,1},{8,10},{9,11},{10,... | collective-permute-start | bytes 21512 | tf_op jit(solution)/shard_map/ppermute | solution.py:370
  66.5 2.6 %collective-permute-start.2 = (bf16[8,448]{1,0:T(8,128)(2,1)S(1)}, bf16[8,448]{1,0:T(8,128)(2,1)S(1)}, u32[]{:S(2)}, u32[]{:S(2)}) collective-permute-start(bf16[8,448]{1,0:T(8,128)(2,1)S(1)} %get-tuple-element.23), channel_id=1, source_target_pairs={{0,4},{1,5},{2,6},{3,7},{4,0},{5,1},{6,2},{7,3},{8,12},{9,13},{10,... | collective-permute-start | bytes 21512 | tf_op jit(solution)/shard_map/ppermute | solution.py:370
  69.1 1.1 %collective-permute-start.3 = (bf16[8,448]{1,0:T(8,128)(2,1)S(1)}, bf16[8,448]{1,0:T(8,128)(2,1)S(1)}, u32[]{:S(2)}, u32[]{:S(2)}) collective-permute-start(bf16[8,448]{1,0:T(8,128)(2,1)S(1)} %get-tuple-element.24), channel_id=1, source_target_pairs={{0,6},{1,7},{2,0},{3,1},{4,2},{5,3},{6,4},{7,5},{8,14},{9,15},{10,... | collective-permute-start | bytes 21512 | tf_op jit(solution)/shard_map/ppermute | solution.py:370
  70.2 0.0 collective-permute-done.1.rest_0_
  70.2 0.3 collective-permute-done.2.rest_1_
  70.5 1.4 %collective-permute-done.3.rest_2_ = bf16[8,448]{1,0:T(8,128)(2,1)S(1)} collective-permute-done((bf16[8,448]{1,0:T(8,128)(2,1)S(1)}, bf16[8,448]{1,0:T(8,128)(2,1)S(1)}, u32[]{:S(2)}, u32[]{:S(2)}) %collective-permute-start.3) | collective-permute-done | bytes 7200 | tf_op jit(solution)/shard_map/ppermute | solution.py:370
  71.9 0.6 shard_map.107
  (14 shorter events, 0.1 us)
Async XLA Ops:
  0.0 0.7 copy-start.1
  1.4 22.6 %all-to-all-start = ((bf16[32,2,1792]{2,1,0:T(2,128)(2,1)}), bf16[32,2,1792]{2,1,0:T(2,128)(2,1)S(1)}, u32[]{:S(2)}, u32[]{:S(2)}) async-start(bf16[32,2,1792]{2,1,0:T(2,128)(2,1)} %shard_map.100), calls=%async_computation | async-start | bytes 458752 | tf_op jit(solution)/shard_map/all_to_all | solution.py:405
  16.4 2.0 %copy-start.2 = (bf16[2,1,1792]{2,0,1:T(2,128)(2,1)S(1)}, bf16[2,1,1792]{2,0,1:T(2,128)(2,1)}, u32[]{:S(2)}) copy-start(bf16[2,1,1792]{2,0,1:T(2,128)(2,1)} %param.10) | copy-start | bytes 21508
  16.4 2.0 %copy-start.4 = (bf16[2,1,1792]{2,0,1:T(2,128)(2,1)S(1)}, bf16[2,1,1792]{2,0,1:T(2,128)(2,1)}, u32[]{:S(2)}) copy-start(bf16[2,1,1792]{2,0,1:T(2,128)(2,1)} %param.11) | copy-start | bytes 21508
  16.4 2.0 %copy-start.5 = (bf16[2,1,1792]{2,0,1:T(2,128)(2,1)S(1)}, bf16[2,1,1792]{2,0,1:T(2,128)(2,1)}, u32[]{:S(2)}) copy-start(bf16[2,1,1792]{2,0,1:T(2,128)(2,1)} %param.12) | copy-start | bytes 21508
  29.6 29.6 %copy-start = (bf16[448,1792]{1,0:T(8,128)(2,1)S(1)}, bf16[448,1792]{1,0:T(8,128)(2,1)}, u32[]{:S(2)}) copy-start(bf16[448,1792]{1,0:T(8,128)(2,1)} %get-tuple-element.18.weight) | copy-start | bytes 4816900
  29.6 42.3 %copy-start.3 = (bf16[2,4,448]{2,1,0:T(4,128)(2,1)S(1)}, bf16[2,4,448]{2,1,0:T(4,128)(2,1)}, u32[]{:S(2)}) copy-start(bf16[2,4,448]{2,1,0:T(4,128)(2,1)} %rest_3_.1) | copy-start | bytes 21508
  59.8 5.3 %collective-permute-start = (bf16[4,8,448]{2,1,0:T(8,128)(2,1)S(1)}, bf16[4,8,448]{2,1,0:T(8,128)(2,1)S(1)}, u32[]{:S(2)}, u32[]{:S(2)}) collective-permute-start(bf16[4,8,448]{2,1,0:T(8,128)(2,1)S(1)} %get-tuple-element.20), channel_id=1, source_target_pairs={{0,1},{1,0},{2,3},{3,2},{4,5},{5,4},{6,7},{7,6},{8,9},{9,8},{10,11... | collective-permute-start | bytes 86024 | tf_op jit(solution)/shard_map/ppermute | solution.py:360
  65.1 5.1 %collective-permute-start.1 = (bf16[8,448]{1,0:T(8,128)(2,1)S(1)}, bf16[8,448]{1,0:T(8,128)(2,1)S(1)}, u32[]{:S(2)}, u32[]{:S(2)}) collective-permute-start(bf16[8,448]{1,0:T(8,128)(2,1)S(1)} %get-tuple-element.22), channel_id=1, source_target_pairs={{0,2},{1,3},{2,4},{3,5},{4,6},{5,7},{6,0},{7,1},{8,10},{9,11},{10,... | collective-permute-start | bytes 21512 | tf_op jit(solution)/shard_map/ppermute | solution.py:370
  66.5 4.0 %collective-permute-start.2 = (bf16[8,448]{1,0:T(8,128)(2,1)S(1)}, bf16[8,448]{1,0:T(8,128)(2,1)S(1)}, u32[]{:S(2)}, u32[]{:S(2)}) collective-permute-start(bf16[8,448]{1,0:T(8,128)(2,1)S(1)} %get-tuple-element.23), channel_id=1, source_target_pairs={{0,4},{1,5},{2,6},{3,7},{4,0},{5,1},{6,2},{7,3},{8,12},{9,13},{10,... | collective-permute-start | bytes 21512 | tf_op jit(solution)/shard_map/ppermute | solution.py:370
  69.1 2.8 %collective-permute-start.3 = (bf16[8,448]{1,0:T(8,128)(2,1)S(1)}, bf16[8,448]{1,0:T(8,128)(2,1)S(1)}, u32[]{:S(2)}, u32[]{:S(2)}) collective-permute-start(bf16[8,448]{1,0:T(8,128)(2,1)S(1)} %get-tuple-element.24), channel_id=1, source_target_pairs={{0,6},{1,7},{2,0},{3,1},{4,2},{5,3},{6,4},{7,5},{8,14},{9,15},{10,... | collective-permute-start | bytes 21512 | tf_op jit(solution)/shard_map/ppermute | solution.py:370

commit v7 on v6

--- a/solution.py
+++ b/solution.py
@@ -277,35 +277,17 @@
         out[r] = attended
 
 
-def project_kernel(rows, weight, mine, theirs):
+def project_kernel(rows, weight, out):
     full = lax.dot_general(
         rows[...], weight[...], (((1,), (1,)), ((), ())), preferred_element_type=jnp.float32
     )
-    first = lax.axis_index("head") % 2 == 0
-    chips, size = mine.shape[0], mine.shape[1]
-    for c in range(chips):
-        a = full[2 * c * size : (2 * c + 1) * size]
-        b = full[(2 * c + 1) * size : (2 * c + 2) * size]
-        mine[c] = jnp.where(first, a, b)
-        theirs[c] = jnp.where(first, b, a).astype(theirs.dtype)
-
-
-def pair_kernel(mine, got, total, *rest):
-    shares, both = rest[:-1], rest[-1]
-    chips = mine.shape[0]
-    chip = lax.axis_index("head") // 2
-    for c in range(chips):
-        both[c] = mine[c] + got[c].astype(jnp.float32)
-    total[...] = both[chip]
-    for hop, share in enumerate(shares, 1):
-        share[...] = both[lax.rem(chip + hop, chips)].astype(share.dtype)
-
-
-def finish_kernel(total, *rest):
-    shares, residual, out = rest[:-2], rest[-2], rest[-1]
-    x = total[...]
-    for share in shares:
-        x = x + share[...].astype(jnp.float32)
+    size = out.shape[1]
+    for i in range(out.shape[0]):
+        out[i] = full[i * size : (i + 1) * size].astype(out.dtype)
+
+
+def finish_kernel(shares, residual, out):
+    x = jnp.sum(shares[...].astype(jnp.float32), axis=0)
     for s in range(STEPS):
         rows = [x[r : r + 1] for r in range(s, x.shape[0], STEPS)]
         y = residual[s].astype(jnp.float32) + jnp.concatenate(rows, axis=0)
@@ -348,34 +330,17 @@
 
 
 def project_and_sum(rows, weight, residual, groups):
-    chips = groups // 2
-    size, columns = rows.shape[0] // groups, weight.shape[0]
-    each = (chips, size, columns)
-    mine, theirs = on_device(
-        project_kernel,
-        (jax.ShapeDtypeStruct(each, jnp.float32), jax.ShapeDtypeStruct(each, jnp.bfloat16)),
-        [pltpu.VMEM] * 2,
-        16,
+    each = (groups, rows.shape[0] // groups, weight.shape[0])
+    projected = on_device(
+        project_kernel, jax.ShapeDtypeStruct(each, jnp.bfloat16), [pltpu.VMEM] * 2, 16
     )(rows, weight)
-    got = lax.ppermute(theirs, "head", [(i, i ^ 1) for i in range(groups)])
-    share = jax.ShapeDtypeStruct((size, columns), jnp.bfloat16)
-    total, *shares = on_device(
-        pair_kernel,
-        (jax.ShapeDtypeStruct((size, columns), jnp.float32), *[share] * (chips - 1)),
-        [pltpu.VMEM] * 2,
-        16,
-        scratch_shapes=[pltpu.VMEM(each, jnp.float32)],
-    )(mine, got)
-    arrived = [
-        lax.ppermute(x, "head", [(i, (i + 2 * hop) % groups) for i in range(groups)])
-        for hop, x in enumerate(shares, 1)
-    ]
+    shares = lax.all_to_all(projected, "head", 0, 0, tiled=True)
     return on_device(
         finish_kernel,
         jax.ShapeDtypeStruct(residual.shape, residual.dtype),
-        [pltpu.VMEM] * (chips + 1),
+        [pltpu.VMEM] * 2,
         16,
-    )(total, *arrived, residual)
+    )(shares, residual)
 
 
 def body(
@@ -401,7 +366,7 @@
 
     copies = on_device(
         copies_kernel, jax.ShapeDtypeStruct((peers, STEPS, width), jnp.bfloat16), [vmem], 4
-    )(own_query)
+    )(in_hbm(own_query))
     everyone = lax.all_to_all(copies, "seq", 0, 0, tiled=True)
 
     table = block_table(seg_blocks, request_row, blocks)

time: 72.8 us -> 74.2 us (1.019)
  blocking collectives: 28.9 us -> 42.3 us
  starting transfers between devices: 21.3 us -> 11.9 us
  waiting for transfers between devices: 7.58 us -> 5.02 us
    all_to_all x0 -> x1, blocking collectives: none -> 13.4 us  [project_and_sum(): shares = lax.all_to_all(projected, 'head', 0, 0, tiled=True)]
    ppermute x4 -> x0, starting transfers between devices: 9.48 us -> none  [the longest x3 5.07 us: project_and_sum(): lax.ppermute(x, 'head', [(i, (i + 2 * hop) % groups) for i in range(group...]
    ppermute x4 -> x0, waiting for transfers between devices: 2.56 us -> none  [the longest x3 1.7 us: project_and_sum(): lax.ppermute(x, 'head', [(i, (i + 2 * hop) % groups) for i in range(group...]
  transfers between devices with their start and end apart: 5 -> 1, of which waited for: 4 -> 1; matrix products, arithmetic and copies ran while one was open for 5% -> 4% of each run, Pallas kernels for 3% -> 3%
where the time goes in v7:
time: 74.2 us; the launch traced here: 73.9 us
  blocking collectives  42.3 us (57%)
  starting transfers between devices  11.9 us (16%)
  Pallas kernels  11 us (15%)
  waiting for transfers between devices  5.02 us (7%)
  other arithmetic  2.55 us (3%)
  local copies, waits for them, and re-layouts  0.95 us (1%)
    all_to_all x1, blocking collectives, body(): arrived = lax.all_to_all(partials, 'seq', 0, 0, tiled=True)  14.7 us
    all_to_all x1, blocking collectives, body(): lax.all_to_all(attended, 'seq', 0, 0, tiled=True)  14.1 us
    all_to_all x1, blocking collectives, project_and_sum(): shares = lax.all_to_all(projected, 'head', 0, 0, tiled=True)  13.4 us
    all_to_all x1, starting transfers between devices, body(): everyone = lax.all_to_all(copies, 'seq', 0, 0, tiled=True)  11.9 us
    pallas_call x1, Pallas kernels, body(): on_device(functools.partial(attend_kernel, blocks, hdim), (jax.ShapeDtype...  5.57 us
    all_to_all x1, waiting for transfers between devices, body(): everyone = lax.all_to_all(copies, 'seq', 0, 0, tiled=True)  5.02 us
    pallas_call x1, Pallas kernels, body(): on_device(stage_kernel, pltpu.VMEM((ready * BLK, width), jnp.bfloat16), [...  1.94 us
  transfers between devices with their start and end apart: 1, of which 1 were waited for; matrix products, arithmetic and copies ran while one was open for 4% of the time, Pallas kernels for 3%

profile of v7, /device:TPU:1, one launch (start us, length us, event | category | flops | bytes accessed | tf_op | source)
XLA Modules:
  0.0 73.9 jit_solution(11321209875783691642)
XLA Ops:
  0.0 1.4 %shard_map.100 = bf16[32,2,1792]{2,1,0:T(2,128)(2,1)} custom-call(bf16[2,1792]{1,0:T(2,128)(2,1)} %bitcast.11), custom_call_target="tpu_custom_call" | custom-call | tf_op jit(solution)/shard_map/pallas_call | solution.py:367
  1.4 11.9 %all-to-all-start = ((bf16[32,2,1792]{2,1,0:T(2,128)(2,1)}), bf16[32,2,1792]{2,1,0:T(2,128)(2,1)S(1)}, u32[]{:S(2)}, u32[]{:S(2)}) async-start(bf16[32,2,1792]{2,1,0:T(2,128)(2,1)} %shard_map.100), calls=%async_computation | async-start | bytes 458752 | tf_op jit(solution)/shard_map/all_to_all | solution.py:370
  13.3 0.8 %select_reduce_fusion = s32[32]{0:T(128)S(1)} fusion(s32[32]{0:T(128)} %param.16), kind=kLoop, calls=%fused_computation | loop fusion | flops 3040 | bytes 256 | tf_op jit(solution)/shard_map/reduce_sum | solution.py:319
  14.0 0.7 add.28
  14.7 0.9 %select_reduce_fusion.2 = (s32[8]{0:T(128)S(1)}, s32[8]{0:T(128)S(1)}) fusion(s32[32]{0:T(128)} %param.17, s32[32]{0:T(128)S(1)} %add.28, s32[32]{0:T(128)S(1)} %select_reduce_fusion, s32[8]{0:T(128)S(1)} %iota_add_fusion), kind=kLoop, calls=%fused_computation.3 | loop fusion | flops 1776 | bytes 480 | tf_op jit(solution)/shard_map/reduce_sum | solution.py:323
  15.6 0.7 pad.4
  16.3 0.1 broadcast_in_dim_tile.3.slopes
  16.3 0.0 copy-start.1
  16.3 0.0 copy-start.3
  16.4 0.0 copy-start.4
  16.4 1.9 %shard_map.102.staged = bf16[896,1792]{1,0:T(8,128)(2,1)S(1)} custom-call(bf16[1024,1792]{1,0:T(8,128)(2,1)} %keys.3), custom_call_target="tpu_custom_call" | custom-call | bytes 6422528 | tf_op jit(solution)/shard_map/pallas_call | solution.py:385
  18.3 0.0 copy-done.1
  18.3 0.0 copy-done.3
  18.3 0.0 copy-done.4
  18.3 0.4 shard_map.101
  18.7 0.2 fusion
  19.0 5.0 %all-to-all-done.query = bf16[32,2,1792]{2,1,0:T(2,128)(2,1)S(1)} async-done(((bf16[32,2,1792]{2,1,0:T(2,128)(2,1)}), bf16[32,2,1792]{2,1,0:T(2,128)(2,1)S(1)}, u32[]{:S(2)}, u32[]{:S(2)}) %all-to-all-start) | async-done | bytes 229408 | tf_op jit(solution)/shard_map/all_to_all | solution.py:370
  24.0 5.6 %shard_map.103 = (bf16[32,2,1920]{2,1,0:T(2,128)(2,1)S(1)}, bf16[448,1792]{1,0:T(8,128)(2,1)}) custom-call(s32[4,8]{1,0:T(4,128)S(1)} %pad_add_fusion.meta, f32[1,128]{1,0:T(1,128)S(1)} %broadcast_in_dim_tile.3.slopes, bf16[32,2,1792]{2,1,0:T(2,128)(2,1)S(1)} %all-to-all-done.query, f32[2,128]{1,0:T(2,128)S(1)} %get-tuple-element.9.own_stats, ...), custom_call_target="tpu_custom_call" | custom-call | tf_op jit(solution)/shard_map/pallas_call | solution.py:396
  29.6 0.0 copy-start
  29.6 0.0 copy-start.2
  29.6 14.7 %all_to_all.20 = bf16[32,2,1920]{2,1,0:T(2,128)(2,1)S(1)} all-to-all(bf16[32,2,1920]{2,1,0:T(2,128)(2,1)S(1)} %get-tuple-element.10), channel_id=1, replica_groups=mesh['seq'=32,'head'=8] {'seq'}, dimensions={0} | all-to-all | bytes 491520 | tf_op jit(solution)/shard_map/all_to_all | solution.py:422
  44.3 0.1 reshape.72.parts
  44.4 0.6 shard_map.104
  45.0 14.1 %all_to_all.21 = bf16[32,2,1792]{2,1,0:T(2,128)(2,1)S(1)} all-to-all(bf16[32,2,1792]{2,1,0:T(2,128)(2,1)S(1)} %shard_map.104), channel_id=1, replica_groups=mesh['seq'=32,'head'=8] {'seq'}, dimensions={0} | all-to-all | bytes 458752 | tf_op jit(solution)/shard_map/all_to_all | solution.py:430
  59.1 0.1 reshape.73.rows
  59.2 0.0 copy-done
  59.2 0.6 shard_map.105
  59.8 13.4 %all_to_all.22.shares = bf16[8,8,448]{2,1,0:T(8,128)(2,1)S(1)} all-to-all(bf16[8,8,448]{2,1,0:T(8,128)(2,1)S(1)} %shard_map.105), channel_id=1, replica_groups=mesh['seq'=32,'head'=8] {'head'}, dimensions={0} | all-to-all | bytes 114688 | tf_op jit(solution)/shard_map/all_to_all | solution.py:337
  73.2 0.0 copy-done.2
  73.2 0.6 shard_map.106
  (6 shorter events, 0.0 us)
Async XLA Ops:
  1.4 22.6 %all-to-all-start = ((bf16[32,2,1792]{2,1,0:T(2,128)(2,1)}), bf16[32,2,1792]{2,1,0:T(2,128)(2,1)S(1)}, u32[]{:S(2)}, u32[]{:S(2)}) async-start(bf16[32,2,1792]{2,1,0:T(2,128)(2,1)} %shard_map.100), calls=%async_computation | async-start | bytes 458752 | tf_op jit(solution)/shard_map/all_to_all | solution.py:370
  16.3 2.0 %copy-start.1 = (bf16[2,1,1792]{2,0,1:T(2,128)(2,1)S(1)}, bf16[2,1,1792]{2,0,1:T(2,128)(2,1)}, u32[]{:S(2)}) copy-start(bf16[2,1,1792]{2,0,1:T(2,128)(2,1)} %param.10) | copy-start | bytes 21508
  16.3 2.0 %copy-start.3 = (bf16[2,1,1792]{2,0,1:T(2,128)(2,1)S(1)}, bf16[2,1,1792]{2,0,1:T(2,128)(2,1)}, u32[]{:S(2)}) copy-start(bf16[2,1,1792]{2,0,1:T(2,128)(2,1)} %param.11) | copy-start | bytes 21508
  16.4 2.0 %copy-start.4 = (bf16[2,1,1792]{2,0,1:T(2,128)(2,1)S(1)}, bf16[2,1,1792]{2,0,1:T(2,128)(2,1)}, u32[]{:S(2)}) copy-start(bf16[2,1,1792]{2,0,1:T(2,128)(2,1)} %param.12) | copy-start | bytes 21508
  29.6 29.6 %copy-start = (bf16[448,1792]{1,0:T(8,128)(2,1)S(1)}, bf16[448,1792]{1,0:T(8,128)(2,1)}, u32[]{:S(2)}) copy-start(bf16[448,1792]{1,0:T(8,128)(2,1)} %get-tuple-element.12.weight) | copy-start | bytes 4816900
  29.6 43.7 %copy-start.2 = (bf16[2,4,448]{2,1,0:T(4,128)(2,1)S(1)}, bf16[2,4,448]{2,1,0:T(4,128)(2,1)}, u32[]{:S(2)}) copy-start(bf16[2,4,448]{2,1,0:T(4,128)(2,1)} %residual.1) | copy-start | bytes 21508

commit v8 on v5

--- a/solution.py
+++ b/solution.py
@@ -12,6 +12,7 @@
 NEG = -1e30
 STEPS = 2
 GROUP = 16
+ROWS = 8
 STATS = 128
 MIB = 1024 * 1024
 
@@ -45,14 +46,19 @@
     return pltpu.roll(x, x.shape[1] - lanes, 1) if lanes else x
 
 
-def stage_kernel(keys, out, sems):
+def stage_kernel(keys, weight, out, weight_out, wbuf, sems, weight_sems):
+    weight_in = pltpu.make_async_copy(weight, wbuf, weight_sems.at[0])
+    weight_back = pltpu.make_async_copy(wbuf, weight_out, weight_sems.at[1])
+    weight_in.start()
     copies = []
     for b in range(sems.shape[0]):
         rows = pl.ds(b * BLK, BLK)
         copies.append(pltpu.make_async_copy(keys.at[rows], out.at[rows], sems.at[b]))
     for copy in copies:
         copy.start()
-    for copy in copies:
+    weight_in.wait()
+    weight_back.start()
+    for copy in (*copies, weight_back):
         copy.wait()
 
 
@@ -72,7 +78,6 @@
     kbuf,
     vbuf,
     sems,
-    weight_sem,
 ):
     width = keys.shape[1]
     per = STEPS * GROUP
@@ -88,8 +93,7 @@
     for b in range(blocks):
         rows = pl.ds(b * BLK, BLK)
         value_copies.append(pltpu.make_async_copy(values.at[rows], vbuf.at[rows], sems.at[1, b]))
-    weight_copy = pltpu.make_async_copy(weight, weight_out, weight_sem)
-    for copy in (*key_copies.values(), *value_copies, weight_copy):
+    for copy in (*key_copies.values(), *value_copies):
         copy.start()
     mask = head_mask(width, hdim)
     lane = iota((STEPS, STATS), 1)
@@ -146,6 +150,9 @@
     for b in range(blocks - 2, -1, -1):
         tops[b] = jnp.where(joined[b + 1], tops[b + 1], tops[b])
 
+    row = iota((BLK, BLK), 0)
+    source = row // per * per + row % STEPS * GROUP + row % per // STEPS
+    swap = (source == iota((BLK, BLK), 1)).astype(jnp.bfloat16)
     place = iota((1, BLK), 1) // per
     totals = []
     weights = []
@@ -156,7 +163,14 @@
         probs = jnp.exp(scores[g] - top)
         total = jnp.sum(probs, axis=0, keepdims=True)
         totals += [left(total, k * per) for k in range(packs)]
-        weights.append(probs.T.astype(jnp.bfloat16))
+        weights.append(
+            lax.dot_general(
+                swap,
+                probs.astype(jnp.bfloat16),
+                (((1,), (1,)), ((), ())),
+                preferred_element_type=jnp.float32,
+            )
+        )
     for b in range(1, blocks):
         totals[b] = totals[b] + jnp.where(joined[b], totals[b - 1], 0.0)
 
@@ -175,19 +189,23 @@
     for b in range(blocks):
         k = b % packs
         value_copies[b].wait()
-        full = jnp.dot(
-            weights[b // packs][k * per : (k + 1) * per],
-            vbuf[b * BLK : (b + 1) * BLK],
-            preferred_element_type=jnp.float32,
-        )
-        mine = by_step(full, mask)
+        mine = []
+        for h in range(0, width // hdim, ROWS // STEPS):
+            lanes = slice(h * hdim, min(h + ROWS // STEPS, width // hdim) * hdim)
+            some = jnp.dot(
+                weights[b // packs][k * per + STEPS * h :][:ROWS].astype(jnp.bfloat16),
+                vbuf[b * BLK : (b + 1) * BLK, lanes],
+                preferred_element_type=jnp.float32,
+            )
+            for i in range(some.shape[1] // hdim):
+                mine.append(some[STEPS * i : STEPS * (i + 1), i * hdim : (i + 1) * hdim])
+        mine = jnp.concatenate(mine, axis=1)
         acc = mine if acc is None else mine + jnp.where(joined[b], acc, 0.0)
         tail = jnp.concatenate([x[b : b + 1] for x in stats], axis=0)
         row = jnp.concatenate([acc, tail], axis=1).astype(out.dtype)
         rows.append(jnp.where(meta[2, b] == 1, row, empty))
     for b in range(blocks):
         out[meta[0, b]] = rows[b]
-    weight_copy.wait()
 
 
 def own_kernel(heads, hdim, query, key, value, slopes, stats, acc):
@@ -412,31 +430,36 @@
     )(own_query, new_keys.reshape(STEPS, width), new_values.reshape(STEPS, width), lanes)
 
     ready = blocks - 1
-    staged = on_device(
+    turned = out_weight.shape[::-1]
+    staged, weight = on_device(
         stage_kernel,
-        pltpu.VMEM((ready * BLK, width), jnp.bfloat16),
-        [pltpu.HBM],
-        2,
-        out_specs=pl.BlockSpec(memory_space=pl.ANY),
-        scratch_shapes=[pltpu.SemaphoreType.DMA((ready,))],
+        (pltpu.VMEM((ready * BLK, width), jnp.bfloat16), pltpu.HBM(turned, jnp.bfloat16)),
+        [pltpu.HBM] * 2,
+        4,
+        out_specs=[pl.BlockSpec(memory_space=pl.ANY)] * 2,
+        scratch_shapes=[
+            pltpu.VMEM(turned, jnp.bfloat16),
+            pltpu.SemaphoreType.DMA((ready,)),
+            pltpu.SemaphoreType.DMA((2,)),
+        ],
         cost_estimate=pl.CostEstimate(
             flops=0, bytes_accessed=4 * ready * BLK * width, transcendentals=0
         ),
-    )(in_hbm(cache_keys))
+    )(in_hbm(cache_keys), in_hbm(out_weight.T))
     partials, weight = on_device(
         functools.partial(attend_kernel, blocks, hdim),
         (
             jax.ShapeDtypeStruct((peers, STEPS, width + STATS), jnp.bfloat16),
-            pltpu.HBM(out_weight.shape[::-1], jnp.bfloat16),
+            pltpu.HBM(turned, jnp.bfloat16),
         ),
         [smem, vmem, vmem, pl.ANY, vmem] + [pltpu.HBM] * 3,
         32,
         out_specs=(pl.BlockSpec(memory_space=vmem), pl.BlockSpec(memory_space=pl.ANY)),
+        input_output_aliases={7: 1},
         scratch_shapes=[
             pltpu.VMEM(((blocks - ready) * BLK, width), jnp.bfloat16),
             pltpu.VMEM(cache_values.shape, jnp.bfloat16),
             pltpu.SemaphoreType.DMA((2, blocks)),
-            pltpu.SemaphoreType.DMA,
         ],
     )(
         table,
@@ -446,7 +469,7 @@
         staged,
         in_hbm(cache_keys),
         in_hbm(cache_values),
-        in_hbm(out_weight.T),
+        weight,
     )
     arrived = lax.all_to_all(partials, "seq", 0, 0, tiled=True)
 

time: 118 us -> 73.2 us (0.62)
  Pallas kernels: 55.3 us -> 11.2 us
  blocking collectives: 28.9 us -> 30.9 us
  waiting for transfers between devices: 7.58 us -> 6.04 us
    pallas_call x1, Pallas kernels: 50.5 us -> 4.8 us  [body(): on_device(functools.partial(attend_kernel, blocks, hdim), (jax.ShapeDtype...]
    pallas_call x1, Pallas kernels: 1.94 us -> 3.5 us  [body(): on_device(stage_kernel, (pltpu.VMEM((ready * BLK, width), jnp.bfloat16),...]
    all_to_all x1, waiting for transfers between devices: 5.02 us -> 3.48 us  [body(): everyone = lax.all_to_all(copies, 'seq', 0, 0, tiled=True)]
    all_to_all x1, blocking collectives: 14.7 us -> 16 us  [body(): arrived = lax.all_to_all(partials, 'seq', 0, 0, tiled=True)]
  transfers between devices with their start and end apart: 5 -> 5, of which waited for: 4 -> 4; matrix products, arithmetic and copies ran while one was open for 3% -> 5% of each run, Pallas kernels for 2% -> 5%
where the time goes in v8:
time: 73.2 us; the launch traced here: 72.9 us
  blocking collectives  30.9 us (42%)
  starting transfers between devices  20.4 us (28%)
  Pallas kernels  11.2 us (15%)
  waiting for transfers between devices  6.04 us (8%)
  other arithmetic  2.55 us (3%)
  local copies, waits for them, and re-layouts  1.65 us (2%)
    all_to_all x1, blocking collectives, body(): arrived = lax.all_to_all(partials, 'seq', 0, 0, tiled=True)  16 us
    all_to_all x1, blocking collectives, body(): lax.all_to_all(attended, 'seq', 0, 0, tiled=True)  14.9 us
    all_to_all x1, starting transfers between devices, body(): everyone = lax.all_to_all(copies, 'seq', 0, 0, tiled=True)  11.9 us
    ppermute x3, starting transfers between devices, project_and_sum(): lax.ppermute(x, 'head', [(i, (i + 2 * hop) % groups) for i in range(group...  5.06 us
    pallas_call x1, Pallas kernels, body(): on_device(functools.partial(attend_kernel, blocks, hdim), (jax.ShapeDtype...  4.8 us
    pallas_call x1, Pallas kernels, body(): on_device(stage_kernel, (pltpu.VMEM((ready * BLK, width), jnp.bfloat16),...  3.5 us
    ppermute x1, starting transfers between devices, project_and_sum(): got = lax.ppermute(theirs, 'head', [(i, i ^ 1) for i in range(groups)])  3.49 us
    all_to_all x1, waiting for transfers between devices, body(): everyone = lax.all_to_all(copies, 'seq', 0, 0, tiled=True)  3.48 us
  transfers between devices with their start and end apart: 5, of which 4 were waited for; matrix products, arithmetic and copies ran while one was open for 5% of the time, Pallas kernels for 5%

profile of v8, /device:TPU:1, one launch (start us, length us, event | category | flops | bytes accessed | tf_op | source)
XLA Modules:
  0.0 72.9 jit_solution(4432838141268780944)
XLA Ops:
  0.0 0.7 copy-done.1
  0.7 0.7 shard_map.100
  1.4 11.9 %all-to-all-start = ((bf16[32,2,1792]{2,1,0:T(2,128)(2,1)}), bf16[32,2,1792]{2,1,0:T(2,128)(2,1)S(1)}, u32[]{:S(2)}, u32[]{:S(2)}) async-start(bf16[32,2,1792]{2,1,0:T(2,128)(2,1)} %shard_map.100), calls=%async_computation | async-start | bytes 458752 | tf_op jit(solution)/shard_map/all_to_all | solution.py:418
  13.3 0.8 %select_reduce_fusion = s32[32]{0:T(128)S(1)} fusion(s32[32]{0:T(128)} %param.16), kind=kLoop, calls=%fused_computation | loop fusion | flops 3040 | bytes 256 | tf_op jit(solution)/shard_map/reduce_sum | solution.py:350
  14.1 0.7 add.28
  14.7 0.9 %select_reduce_fusion.2 = (s32[8]{0:T(128)S(1)}, s32[8]{0:T(128)S(1)}) fusion(s32[32]{0:T(128)} %param.17, s32[32]{0:T(128)S(1)} %add.28, s32[32]{0:T(128)S(1)} %select_reduce_fusion, s32[8]{0:T(128)S(1)} %iota_add_fusion), kind=kLoop, calls=%fused_computation.3 | loop fusion | flops 1776 | bytes 480 | tf_op jit(solution)/shard_map/reduce_sum | solution.py:354
  15.6 0.7 pad.4
  16.3 0.1 broadcast_in_dim_tile.3.slopes
  16.4 3.5 %shard_map.102 = (bf16[896,1792]{1,0:T(8,128)(2,1)S(1)}, bf16[448,1792]{1,0:T(8,128)(2,1)}) custom-call(bf16[1024,1792]{1,0:T(8,128)(2,1)} %keys.3, bf16[448,1792]{1,0:T(8,128)(2,1)} %bitcast.15), custom_call_target="tpu_custom_call" | custom-call | bytes 6422528 | tf_op jit(solution)/shard_map/pallas_call | solution.py:434
  19.9 0.0 copy-done.2
  19.9 0.0 copy-done.4
  19.9 0.0 copy-done.5
  19.9 0.4 shard_map.101
  20.3 0.2 fusion
  20.5 3.5 %all-to-all-done.query = bf16[32,2,1792]{2,1,0:T(2,128)(2,1)S(1)} async-done(((bf16[32,2,1792]{2,1,0:T(2,128)(2,1)}), bf16[32,2,1792]{2,1,0:T(2,128)(2,1)S(1)}, u32[]{:S(2)}, u32[]{:S(2)}) %all-to-all-start) | async-done | bytes 229408 | tf_op jit(solution)/shard_map/all_to_all | solution.py:418
  24.0 4.8 %shard_map.103 = (bf16[32,2,1920]{2,1,0:T(2,128)(2,1)S(1)}, bf16[448,1792]{1,0:T(8,128)(2,1)}) custom-call(s32[4,8]{1,0:T(4,128)S(1)} %pad_add_fusion.meta, f32[1,128]{1,0:T(1,128)S(1)} %broadcast_in_dim_tile.3.slopes, bf16[32,2,1792]{2,1,0:T(2,128)(2,1)S(1)} %all-to-all-done.query, ...), custom_call_target="tpu_custom_call", output_to_operand_aliasing={{1}: (7, {})} | custom-call | tf_op jit(solution)/shard_map/pallas_call | solution.py:449
  28.8 0.0 copy-start.3
  28.8 16.0 %all_to_all.15 = bf16[32,2,1920]{2,1,0:T(2,128)(2,1)S(1)} all-to-all(bf16[32,2,1920]{2,1,0:T(2,128)(2,1)S(1)} %get-tuple-element.20), channel_id=1, replica_groups=mesh['seq'=32,'head'=8] {'seq'}, dimensions={0} | all-to-all | bytes 491520 | tf_op jit(solution)/shard_map/all_to_all | solution.py:474
  44.8 0.1 reshape.72.parts
  44.9 0.6 shard_map.104
  45.5 14.9 %all_to_all.16 = bf16[32,2,1792]{2,1,0:T(2,128)(2,1)S(1)} all-to-all(bf16[32,2,1792]{2,1,0:T(2,128)(2,1)S(1)} %shard_map.104), channel_id=1, replica_groups=mesh['seq'=32,'head'=8] {'seq'}, dimensions={0} | all-to-all | bytes 458752 | tf_op jit(solution)/shard_map/all_to_all | solution.py:482
  60.4 0.1 reshape.73.rows
  60.5 0.6 shard_map.105
  61.1 3.5 %collective-permute-start = (bf16[4,8,448]{2,1,0:T(8,128)(2,1)S(1)}, bf16[4,8,448]{2,1,0:T(8,128)(2,1)S(1)}, u32[]{:S(2)}, u32[]{:S(2)}) collective-permute-start(bf16[4,8,448]{2,1,0:T(8,128)(2,1)S(1)} %get-tuple-element.24), channel_id=1, source_target_pairs={{0,1},{1,0},{2,3},{3,2},{4,5},{5,4},{6,7},{7,6},{8,9},{9,8},{10,11... | collective-permute-start | bytes 86024 | tf_op jit(solution)/shard_map/ppermute | solution.py:373
  64.6 0.9 %collective-permute-done.got = bf16[4,8,448]{2,1,0:T(8,128)(2,1)S(1)} collective-permute-done((bf16[4,8,448]{2,1,0:T(8,128)(2,1)S(1)}, bf16[4,8,448]{2,1,0:T(8,128)(2,1)S(1)}, u32[]{:S(2)}, u32[]{:S(2)}) %collective-permute-start) | collective-permute-done | bytes 28704 | tf_op jit(solution)/shard_map/ppermute | solution.py:373
  65.5 1.4 %collective-permute-start.1 = (bf16[8,448]{1,0:T(8,128)(2,1)S(1)}, bf16[8,448]{1,0:T(8,128)(2,1)S(1)}, u32[]{:S(2)}, u32[]{:S(2)}) collective-permute-start(bf16[8,448]{1,0:T(8,128)(2,1)S(1)} %get-tuple-element.26), channel_id=1, source_target_pairs={{0,2},{1,3},{2,4},{3,5},{4,6},{5,7},{6,0},{7,1},{8,10},{9,11},{10,... | collective-permute-start | bytes 21512 | tf_op jit(solution)/shard_map/ppermute | solution.py:383
  66.9 2.6 %collective-permute-start.2 = (bf16[8,448]{1,0:T(8,128)(2,1)S(1)}, bf16[8,448]{1,0:T(8,128)(2,1)S(1)}, u32[]{:S(2)}, u32[]{:S(2)}) collective-permute-start(bf16[8,448]{1,0:T(8,128)(2,1)S(1)} %get-tuple-element.27), channel_id=1, source_target_pairs={{0,4},{1,5},{2,6},{3,7},{4,0},{5,1},{6,2},{7,3},{8,12},{9,13},{10,... | collective-permute-start | bytes 21512 | tf_op jit(solution)/shard_map/ppermute | solution.py:383
  69.5 1.1 %collective-permute-start.3 = (bf16[8,448]{1,0:T(8,128)(2,1)S(1)}, bf16[8,448]{1,0:T(8,128)(2,1)S(1)}, u32[]{:S(2)}, u32[]{:S(2)}) collective-permute-start(bf16[8,448]{1,0:T(8,128)(2,1)S(1)} %get-tuple-element.28), channel_id=1, source_target_pairs={{0,6},{1,7},{2,0},{3,1},{4,2},{5,3},{6,4},{7,5},{8,14},{9,15},{10,... | collective-permute-start | bytes 21512 | tf_op jit(solution)/shard_map/ppermute | solution.py:383
  70.5 0.0 collective-permute-done.1.rest_0_
  70.5 0.3 collective-permute-done.2.rest_1_
  70.9 1.4 %collective-permute-done.3.rest_2_ = bf16[8,448]{1,0:T(8,128)(2,1)S(1)} collective-permute-done((bf16[8,448]{1,0:T(8,128)(2,1)S(1)}, bf16[8,448]{1,0:T(8,128)(2,1)S(1)}, u32[]{:S(2)}, u32[]{:S(2)}) %collective-permute-start.3) | collective-permute-done | bytes 7200 | tf_op jit(solution)/shard_map/ppermute | solution.py:383
  72.3 0.6 shard_map.107
  (14 shorter events, 0.1 us)
Async XLA Ops:
  0.0 0.7 copy-start.1
  0.7 19.2 %copy-start.2 = (bf16[2,1,1792]{2,0,1:T(2,128)(2,1)S(1)}, bf16[2,1,1792]{2,0,1:T(2,128)(2,1)}, u32[]{:S(2)}) copy-start(bf16[2,1,1792]{2,0,1:T(2,128)(2,1)} %param.10) | copy-start | bytes 21508
  0.7 19.2 %copy-start.4 = (bf16[2,1,1792]{2,0,1:T(2,128)(2,1)S(1)}, bf16[2,1,1792]{2,0,1:T(2,128)(2,1)}, u32[]{:S(2)}) copy-start(bf16[2,1,1792]{2,0,1:T(2,128)(2,1)} %param.11) | copy-start | bytes 21508
  0.7 19.2 %copy-start.5 = (bf16[2,1,1792]{2,0,1:T(2,128)(2,1)S(1)}, bf16[2,1,1792]{2,0,1:T(2,128)(2,1)}, u32[]{:S(2)}) copy-start(bf16[2,1,1792]{2,0,1:T(2,128)(2,1)} %param.12) | copy-start | bytes 21508
  1.4 22.6 %all-to-all-start = ((bf16[32,2,1792]{2,1,0:T(2,128)(2,1)}), bf16[32,2,1792]{2,1,0:T(2,128)(2,1)S(1)}, u32[]{:S(2)}, u32[]{:S(2)}) async-start(bf16[32,2,1792]{2,1,0:T(2,128)(2,1)} %shard_map.100), calls=%async_computation | async-start | bytes 458752 | tf_op jit(solution)/shard_map/all_to_all | solution.py:418
  28.8 31.7 %copy-start = (bf16[448,1792]{1,0:T(8,128)(2,1)S(1)}, bf16[448,1792]{1,0:T(8,128)(2,1)}, u32[]{:S(2)}) copy-start(bf16[448,1792]{1,0:T(8,128)(2,1)} %get-tuple-element.22.weight) | copy-start | bytes 4816900
  28.8 43.4 %copy-start.3 = (bf16[2,4,448]{2,1,0:T(4,128)(2,1)S(1)}, bf16[2,4,448]{2,1,0:T(4,128)(2,1)}, u32[]{:S(2)}) copy-start(bf16[2,4,448]{2,1,0:T(4,128)(2,1)} %rest_3_.1) | copy-start | bytes 21508
  61.1 4.3 %collective-permute-start = (bf16[4,8,448]{2,1,0:T(8,128)(2,1)S(1)}, bf16[4,8,448]{2,1,0:T(8,128)(2,1)S(1)}, u32[]{:S(2)}, u32[]{:S(2)}) collective-permute-start(bf16[4,8,448]{2,1,0:T(8,128)(2,1)S(1)} %get-tuple-element.24), channel_id=1, source_target_pairs={{0,1},{1,0},{2,3},{3,2},{4,5},{5,4},{6,7},{7,6},{8,9},{9,8},{10,11... | collective-permute-start | bytes 86024 | tf_op jit(solution)/shard_map/ppermute | solution.py:373
  65.5 5.1 %collective-permute-start.1 = (bf16[8,448]{1,0:T(8,128)(2,1)S(1)}, bf16[8,448]{1,0:T(8,128)(2,1)S(1)}, u32[]{:S(2)}, u32[]{:S(2)}) collective-permute-start(bf16[8,448]{1,0:T(8,128)(2,1)S(1)} %get-tuple-element.26), channel_id=1, source_target_pairs={{0,2},{1,3},{2,4},{3,5},{4,6},{5,7},{6,0},{7,1},{8,10},{9,11},{10,... | collective-permute-start | bytes 21512 | tf_op jit(solution)/shard_map/ppermute | solution.py:383
  66.9 4.0 %collective-permute-start.2 = (bf16[8,448]{1,0:T(8,128)(2,1)S(1)}, bf16[8,448]{1,0:T(8,128)(2,1)S(1)}, u32[]{:S(2)}, u32[]{:S(2)}) collective-permute-start(bf16[8,448]{1,0:T(8,128)(2,1)S(1)} %get-tuple-element.27), channel_id=1, source_target_pairs={{0,4},{1,5},{2,6},{3,7},{4,0},{5,1},{6,2},{7,3},{8,12},{9,13},{10,... | collective-permute-start | bytes 21512 | tf_op jit(solution)/shard_map/ppermute | solution.py:383
  69.5 2.8 %collective-permute-start.3 = (bf16[8,448]{1,0:T(8,128)(2,1)S(1)}, bf16[8,448]{1,0:T(8,128)(2,1)S(1)}, u32[]{:S(2)}, u32[]{:S(2)}) collective-permute-start(bf16[8,448]{1,0:T(8,128)(2,1)S(1)} %get-tuple-element.28), channel_id=1, source_target_pairs={{0,6},{1,7},{2,0},{3,1},{4,2},{5,3},{6,4},{7,5},{8,14},{9,15},{10,... | collective-permute-start | bytes 21512 | tf_op jit(solution)/shard_map/ppermute | solution.py:383

commit v9 on v8

--- a/solution.py
+++ b/solution.py
@@ -208,7 +208,7 @@
         out[meta[0, b]] = rows[b]
 
 
-def own_kernel(heads, hdim, query, key, value, slopes, stats, acc):
+def own_terms(heads, hdim, query, key, value, slopes):
     scale = 1.0 / math.sqrt(hdim)
     q = query[...].astype(jnp.float32)
     k = key[...].astype(jnp.float32)
@@ -225,7 +225,7 @@
         at = slice(h * hdim, (h + 1) * hdim)
         dots = jnp.sum(products[:, at], axis=1, keepdims=True) * scale
         first = dots[0:1]
-        cross = dots[1:2] - slopes[:, h : h + 1]
+        cross = dots[1:2] - slopes[h]
         second = dots[2:3]
         upper = jnp.maximum(cross, second)
         e_cross = jnp.exp(cross - upper)
@@ -236,8 +236,59 @@
         sums[1] = jnp.where(lane == h + GROUP, e_cross + e_second, sums[1])
         rows[0].append(v0[:, at])
         rows[1].append(e_cross * v0[:, at] + e_second * v1[:, at])
-    stats[...] = jnp.concatenate([tops[0] + sums[0], tops[1] + sums[1]], axis=0)
-    acc[...] = jnp.concatenate([jnp.concatenate(r, axis=1) for r in rows], axis=0)
+    stats = jnp.concatenate([tops[0] + sums[0], tops[1] + sums[1]], axis=0)
+    return stats, jnp.concatenate([jnp.concatenate(r, axis=1) for r in rows], axis=0)
+
+
+def block_table(blocks, seg_blocks, request_row):
+    requests = seg_blocks.shape[0]
+    index = lax.axis_index("seq") * blocks
+
+    def skip(i, carry):
+        request, end, total = carry
+        total = total + seg_blocks[i]
+        passed = total <= index
+        return request + passed.astype(jnp.int32), jnp.where(passed, total, end), total
+
+    zero = jnp.int32(0)
+    request, end, _ = lax.fori_loop(0, requests, skip, (zero, zero, zero))
+    last = requests - 1
+    end = end + seg_blocks[jnp.minimum(request, last)]
+    table = []
+    for b in range(blocks):
+        joined = jnp.bool_(False)
+        if b:
+            joined = index + b < end
+            request = jnp.where(joined, request, request + 1)
+            end = jnp.where(joined, end, end + seg_blocks[jnp.minimum(request, last)])
+        live = request <= last
+        row = request_row[jnp.minimum(request, last)]
+        table.append((row, (end - index - b) * BLK, live, joined & live))
+    return table
+
+
+def own_kernel(
+    blocks,
+    heads,
+    seg_blocks,
+    request_row,
+    slopes,
+    query,
+    key,
+    value,
+    table,
+    lanes,
+    stats,
+    acc,
+):
+    for b, entry in enumerate(block_table(blocks, seg_blocks, request_row)):
+        for i, x in enumerate(entry):
+            table[i, b] = x.astype(jnp.int32)
+    slope = jnp.zeros((1, BLK), jnp.float32)
+    for h in range(heads):
+        slope = jnp.where(iota((1, BLK), 1) % GROUP == h, slopes[h], slope)
+    lanes[...] = slope
+    stats[...], acc[...] = own_terms(heads, query.shape[1] // heads, query, key, value, slopes)
 
 
 def join_kernel(heads, hdim, parts, own_stats, own_acc, out):
@@ -344,22 +395,6 @@
     )
 
 
-def block_table(seg_blocks, request_row, blocks):
-    requests = seg_blocks.shape[0]
-    order = jnp.arange(requests, dtype=jnp.int32)
-    starts = jnp.sum(jnp.where(order[None, :] < order[:, None], seg_blocks[None, :], 0), axis=1)
-    index = lax.axis_index("seq") * blocks + jnp.arange(blocks, dtype=jnp.int32)
-    ends = starts + seg_blocks
-    hit = (index[:, None] >= starts[None, :]) & (index[:, None] < ends[None, :])
-    pick = lambda x: jnp.sum(jnp.where(hit, x[None, :], 0), axis=1)
-    row = pick(request_row)
-    base = pick(ends) * BLK - index * BLK
-    live = jnp.any(hit, axis=1)
-    before = hit & (index[:, None] > starts[None, :]) & (jnp.arange(blocks)[:, None] > 0)
-    joined = jnp.any(before, axis=1)
-    return jnp.stack([row, base, live.astype(jnp.int32), joined.astype(jnp.int32)])
-
-
 def project_and_sum(rows, weight, residual, groups):
     chips = groups // 2
     size, columns = rows.shape[0] // groups, weight.shape[0]
@@ -417,17 +452,25 @@
     )(own_query)
     everyone = lax.all_to_all(copies, "seq", 0, 0, tiled=True)
 
-    table = block_table(seg_blocks, request_row, blocks)
-    lanes = jnp.tile(jnp.pad(slopes, (0, GROUP - heads)), BLK // GROUP)[None]
-    own_stats, own_acc = on_device(
-        functools.partial(own_kernel, heads, hdim),
+    table, lanes, own_stats, own_acc = on_device(
+        functools.partial(own_kernel, blocks, heads),
         (
+            jax.ShapeDtypeStruct((4, blocks), jnp.int32),
+            jax.ShapeDtypeStruct((1, BLK), jnp.float32),
             jax.ShapeDtypeStruct((STEPS, STATS), jnp.float32),
             jax.ShapeDtypeStruct((STEPS, width), jnp.float32),
         ),
-        [vmem] * 4,
+        [smem] * 3 + [vmem] * 3,
         4,
-    )(own_query, new_keys.reshape(STEPS, width), new_values.reshape(STEPS, width), lanes)
+        out_specs=[pl.BlockSpec(memory_space=m) for m in (smem, vmem, vmem, vmem)],
+    )(
+        in_hbm(seg_blocks),
+        in_hbm(request_row),
+        in_hbm(slopes),
+        in_hbm(own_query),
+        in_hbm(new_keys.reshape(STEPS, width)),
+        in_hbm(new_values.reshape(STEPS, width)),
+    )
 
     ready = blocks - 1
     turned = out_weight.shape[::-1]

time: 73.2 us -> 72.1 us (0.985)
  other arithmetic: 2.55 us -> 0 us
  blocking collectives: 30.9 us -> 28.9 us
  waiting for transfers between devices: 6.04 us -> 7.86 us
  Pallas kernels: 11.2 us -> 12.7 us
  starting transfers between devices: 20.4 us -> 21.3 us
  local copies, waits for them, and re-layouts: 1.65 us -> 0.89 us
    all_to_all x1, waiting for transfers between devices: 3.48 us -> 5.3 us  [body(): everyone = lax.all_to_all(copies, 'seq', 0, 0, tiled=True)]
    reduce_sum x2 -> x0, other arithmetic: 1.63 us -> none  [the longest x1 0.86 us: block_table(): pick = lambda x: jnp.sum(jnp.where(hit, x[None, :], 0), axis=1)]
    pallas_call x1, Pallas kernels: 0.38 us -> 1.89 us  [body(): on_device(functools.partial(own_kernel, blocks, heads), (jax.ShapeDtypeSt...]
    all_to_all x1, blocking collectives: 16 us -> 14.7 us  [body(): arrived = lax.all_to_all(partials, 'seq', 0, 0, tiled=True)]
    ppermute x1, starting transfers between devices: 3.49 us -> 4.41 us  [project_and_sum(): got = lax.ppermute(theirs, 'head', [(i, i ^ 1) for i in range(groups)])]
    all_to_all x1, blocking collectives: 14.9 us -> 14.1 us  [body(): lax.all_to_all(attended, 'seq', 0, 0, tiled=True)]
  transfers between devices with their start and end apart: 5 -> 5, of which waited for: 4 -> 4; matrix products, arithmetic and copies ran while one was open for 5% -> 0% of each run, Pallas kernels for 5% -> 8%
where the time goes in v9:
time: 72.1 us; the launch traced here: 71.8 us
  blocking collectives  28.9 us (40%)
  starting transfers between devices  21.3 us (30%)
  Pallas kernels  12.7 us (18%)
  waiting for transfers between devices  7.86 us (11%)
  local copies, waits for them, and re-layouts  0.89 us (1%)
    all_to_all x1, blocking collectives, body(): arrived = lax.all_to_all(partials, 'seq', 0, 0, tiled=True)  14.7 us
    all_to_all x1, blocking collectives, body(): lax.all_to_all(attended, 'seq', 0, 0, tiled=True)  14.1 us
    all_to_all x1, starting transfers between devices, body(): everyone = lax.all_to_all(copies, 'seq', 0, 0, tiled=True)  11.9 us
    all_to_all x1, waiting for transfers between devices, body(): everyone = lax.all_to_all(copies, 'seq', 0, 0, tiled=True)  5.3 us
    ppermute x3, starting transfers between devices, project_and_sum(): lax.ppermute(x, 'head', [(i, (i + 2 * hop) % groups) for i in range(group...  5.06 us
    pallas_call x1, Pallas kernels, body(): on_device(functools.partial(attend_kernel, blocks, hdim), (jax.ShapeDtype...  4.81 us
    ppermute x1, starting transfers between devices, project_and_sum(): got = lax.ppermute(theirs, 'head', [(i, i ^ 1) for i in range(groups)])  4.41 us
    pallas_call x1, Pallas kernels, body(): on_device(stage_kernel, (pltpu.VMEM((ready * BLK, width), jnp.bfloat16),...  3.52 us
  transfers between devices with their start and end apart: 5, of which 4 were waited for; matrix products, arithmetic and copies ran while one was open for 0% of the time, Pallas kernels for 8%

profile of v9, /device:TPU:1, one launch (start us, length us, event | category | flops | bytes accessed | tf_op | source)
XLA Modules:
  0.0 71.8 jit_solution(11619098658937636300)
XLA Ops:
  0.0 0.0 copy-start.1
  0.0 0.7 copy-done.1
  0.7 0.7 shard_map.101
  1.4 11.9 %all-to-all-start = ((bf16[32,2,1792]{2,1,0:T(2,128)(2,1)}), bf16[32,2,1792]{2,1,0:T(2,128)(2,1)S(1)}, u32[]{:S(2)}, u32[]{:S(2)}) async-start(bf16[32,2,1792]{2,1,0:T(2,128)(2,1)} %shard_map.101), calls=%async_computation | async-start | bytes 458752 | tf_op jit(solution)/shard_map/all_to_all | solution.py:453
  13.3 3.5 %shard_map.102 = (bf16[896,1792]{1,0:T(8,128)(2,1)S(1)}, bf16[448,1792]{1,0:T(8,128)(2,1)}) custom-call(bf16[1024,1792]{1,0:T(8,128)(2,1)} %keys.3, bf16[448,1792]{1,0:T(8,128)(2,1)} %bitcast.6), custom_call_target="tpu_custom_call" | custom-call | bytes 6422528 | tf_op jit(solution)/shard_map/pallas_call | solution.py:477
  16.8 1.9 %shard_map.100 = (s32[4,8]{1,0:T(4,128)S(1)}, f32[1,128]{1,0:T(1,128)S(1)}, f32[2,128]{1,0:T(2,128)S(1)}, f32[2,1792]{1,0:T(2,128)S(1)}) custom-call(s32[32]{0:T(128)} %seg_blocks.1, s32[32]{0:T(128)} %request_row.1, f32[14]{0:T(128)} %slopes.1, bf16[2,1792]{1,0:T(2,128)(2,1)} %bitcast.4, bf16[2,1792]{1,0:T(2,128)(2,1)} %bitcast.7, bf16[2,1792]{1,0:T(2,128)(2,1)} %bitcast.8), custom_call_target="tpu_custom_call" | custom-call | tf_op jit(solution)/shard_map/pallas_call | solution.py:455
  18.7 5.3 %all-to-all-done.query = bf16[32,2,1792]{2,1,0:T(2,128)(2,1)S(1)} async-done(((bf16[32,2,1792]{2,1,0:T(2,128)(2,1)}), bf16[32,2,1792]{2,1,0:T(2,128)(2,1)S(1)}, u32[]{:S(2)}, u32[]{:S(2)}) %all-to-all-start) | async-done | bytes 229408 | tf_op jit(solution)/shard_map/all_to_all | solution.py:453
  24.0 4.8 %shard_map.103 = (bf16[32,2,1920]{2,1,0:T(2,128)(2,1)S(1)}, bf16[448,1792]{1,0:T(8,128)(2,1)}) custom-call(s32[4,8]{1,0:T(4,128)S(1)} %get-tuple-element.19.meta, f32[1,128]{1,0:T(1,128)S(1)} %get-tuple-element.20.slopes, bf16[32,2,1792]{2,1,0:T(2,128)(2,1)S(1)} %all-to-all-done.query, ...), custom_call_target="tpu_custom_call", output_to_operand_aliasing={{1}: (7, {})} | custom-call | tf_op jit(solution)/shard_map/pallas_call | solution.py:492
  28.8 0.0 copy-start
  28.8 0.0 copy-start.2
  28.9 14.7 %all_to_all.15 = bf16[32,2,1920]{2,1,0:T(2,128)(2,1)S(1)} all-to-all(bf16[32,2,1920]{2,1,0:T(2,128)(2,1)S(1)} %get-tuple-element.24), channel_id=1, replica_groups=mesh['seq'=32,'head'=8] {'seq'}, dimensions={0} | all-to-all | bytes 491520 | tf_op jit(solution)/shard_map/all_to_all | solution.py:517
  43.6 0.1 reshape.18.parts
  43.7 0.6 shard_map.104
  44.3 14.1 %all_to_all.16 = bf16[32,2,1792]{2,1,0:T(2,128)(2,1)S(1)} all-to-all(bf16[32,2,1792]{2,1,0:T(2,128)(2,1)S(1)} %shard_map.104), channel_id=1, replica_groups=mesh['seq'=32,'head'=8] {'seq'}, dimensions={0} | all-to-all | bytes 458752 | tf_op jit(solution)/shard_map/all_to_all | solution.py:525
  58.4 0.1 reshape.19.rows
  58.5 0.0 copy-done
  58.5 0.6 shard_map.105
  59.1 4.4 %collective-permute-start = (bf16[4,8,448]{2,1,0:T(8,128)(2,1)S(1)}, bf16[4,8,448]{2,1,0:T(8,128)(2,1)S(1)}, u32[]{:S(2)}, u32[]{:S(2)}) collective-permute-start(bf16[4,8,448]{2,1,0:T(8,128)(2,1)S(1)} %get-tuple-element.28), channel_id=1, source_target_pairs={{0,1},{1,0},{2,3},{3,2},{4,5},{5,4},{6,7},{7,6},{8,9},{9,8},{10,11... | collective-permute-start | bytes 86024 | tf_op jit(solution)/shard_map/ppermute | solution.py:408
  63.5 0.9 %collective-permute-done.got = bf16[4,8,448]{2,1,0:T(8,128)(2,1)S(1)} collective-permute-done((bf16[4,8,448]{2,1,0:T(8,128)(2,1)S(1)}, bf16[4,8,448]{2,1,0:T(8,128)(2,1)S(1)}, u32[]{:S(2)}, u32[]{:S(2)}) %collective-permute-start) | collective-permute-done | bytes 28704 | tf_op jit(solution)/shard_map/ppermute | solution.py:408
  64.4 1.4 %collective-permute-start.1 = (bf16[8,448]{1,0:T(8,128)(2,1)S(1)}, bf16[8,448]{1,0:T(8,128)(2,1)S(1)}, u32[]{:S(2)}, u32[]{:S(2)}) collective-permute-start(bf16[8,448]{1,0:T(8,128)(2,1)S(1)} %get-tuple-element.30), channel_id=1, source_target_pairs={{0,2},{1,3},{2,4},{3,5},{4,6},{5,7},{6,0},{7,1},{8,10},{9,11},{10,... | collective-permute-start | bytes 21512 | tf_op jit(solution)/shard_map/ppermute | solution.py:418
  65.7 2.6 %collective-permute-start.2 = (bf16[8,448]{1,0:T(8,128)(2,1)S(1)}, bf16[8,448]{1,0:T(8,128)(2,1)S(1)}, u32[]{:S(2)}, u32[]{:S(2)}) collective-permute-start(bf16[8,448]{1,0:T(8,128)(2,1)S(1)} %get-tuple-element.31), channel_id=1, source_target_pairs={{0,4},{1,5},{2,6},{3,7},{4,0},{5,1},{6,2},{7,3},{8,12},{9,13},{10,... | collective-permute-start | bytes 21512 | tf_op jit(solution)/shard_map/ppermute | solution.py:418
  68.4 1.1 %collective-permute-start.3 = (bf16[8,448]{1,0:T(8,128)(2,1)S(1)}, bf16[8,448]{1,0:T(8,128)(2,1)S(1)}, u32[]{:S(2)}, u32[]{:S(2)}) collective-permute-start(bf16[8,448]{1,0:T(8,128)(2,1)S(1)} %get-tuple-element.32), channel_id=1, source_target_pairs={{0,6},{1,7},{2,0},{3,1},{4,2},{5,3},{6,4},{7,5},{8,14},{9,15},{10,... | collective-permute-start | bytes 21512 | tf_op jit(solution)/shard_map/ppermute | solution.py:418
  69.4 0.0 collective-permute-done.1.rest_0_
  69.4 0.3 collective-permute-done.2.rest_1_
  69.7 1.4 %collective-permute-done.3.rest_2_ = bf16[8,448]{1,0:T(8,128)(2,1)S(1)} collective-permute-done((bf16[8,448]{1,0:T(8,128)(2,1)S(1)}, bf16[8,448]{1,0:T(8,128)(2,1)S(1)}, u32[]{:S(2)}, u32[]{:S(2)}) %collective-permute-start.3) | collective-permute-done | bytes 7200 | tf_op jit(solution)/shard_map/ppermute | solution.py:418
  71.1 0.0 copy-done.2
  71.1 0.6 shard_map.107
  (1 shorter events, 0.0 us)
Async XLA Ops:
  0.0 0.7 copy-start.1
  1.4 22.6 %all-to-all-start = ((bf16[32,2,1792]{2,1,0:T(2,128)(2,1)}), bf16[32,2,1792]{2,1,0:T(2,128)(2,1)S(1)}, u32[]{:S(2)}, u32[]{:S(2)}) async-start(bf16[32,2,1792]{2,1,0:T(2,128)(2,1)} %shard_map.101), calls=%async_computation | async-start | bytes 458752 | tf_op jit(solution)/shard_map/all_to_all | solution.py:453
  28.8 29.6 %copy-start = (bf16[448,1792]{1,0:T(8,128)(2,1)S(1)}, bf16[448,1792]{1,0:T(8,128)(2,1)}, u32[]{:S(2)}) copy-start(bf16[448,1792]{1,0:T(8,128)(2,1)} %get-tuple-element.26.weight) | copy-start | bytes 4816900
  28.8 42.3 %copy-start.2 = (bf16[2,4,448]{2,1,0:T(4,128)(2,1)S(1)}, bf16[2,4,448]{2,1,0:T(4,128)(2,1)}, u32[]{:S(2)}) copy-start(bf16[2,4,448]{2,1,0:T(4,128)(2,1)} %rest_3_.1) | copy-start | bytes 21508
  59.1 5.3 %collective-permute-start = (bf16[4,8,448]{2,1,0:T(8,128)(2,1)S(1)}, bf16[4,8,448]{2,1,0:T(8,128)(2,1)S(1)}, u32[]{:S(2)}, u32[]{:S(2)}) collective-permute-start(bf16[4,8,448]{2,1,0:T(8,128)(2,1)S(1)} %get-tuple-element.28), channel_id=1, source_target_pairs={{0,1},{1,0},{2,3},{3,2},{4,5},{5,4},{6,7},{7,6},{8,9},{9,8},{10,11... | collective-permute-start | bytes 86024 | tf_op jit(solution)/shard_map/ppermute | solution.py:408
  64.4 5.1 %collective-permute-start.1 = (bf16[8,448]{1,0:T(8,128)(2,1)S(1)}, bf16[8,448]{1,0:T(8,128)(2,1)S(1)}, u32[]{:S(2)}, u32[]{:S(2)}) collective-permute-start(bf16[8,448]{1,0:T(8,128)(2,1)S(1)} %get-tuple-element.30), channel_id=1, source_target_pairs={{0,2},{1,3},{2,4},{3,5},{4,6},{5,7},{6,0},{7,1},{8,10},{9,11},{10,... | collective-permute-start | bytes 21512 | tf_op jit(solution)/shard_map/ppermute | solution.py:418
  65.7 4.0 %collective-permute-start.2 = (bf16[8,448]{1,0:T(8,128)(2,1)S(1)}, bf16[8,448]{1,0:T(8,128)(2,1)S(1)}, u32[]{:S(2)}, u32[]{:S(2)}) collective-permute-start(bf16[8,448]{1,0:T(8,128)(2,1)S(1)} %get-tuple-element.31), channel_id=1, source_target_pairs={{0,4},{1,5},{2,6},{3,7},{4,0},{5,1},{6,2},{7,3},{8,12},{9,13},{10,... | collective-permute-start | bytes 21512 | tf_op jit(solution)/shard_map/ppermute | solution.py:418
  68.4 2.8 %collective-permute-start.3 = (bf16[8,448]{1,0:T(8,128)(2,1)S(1)}, bf16[8,448]{1,0:T(8,128)(2,1)S(1)}, u32[]{:S(2)}, u32[]{:S(2)}) collective-permute-start(bf16[8,448]{1,0:T(8,128)(2,1)S(1)} %get-tuple-element.32), channel_id=1, source_target_pairs={{0,6},{1,7},{2,0},{3,1},{4,2},{5,3},{6,4},{7,5},{8,14},{9,15},{10,... | collective-permute-start | bytes 21512 | tf_op jit(solution)/shard_map/ppermute | solution.py:418

commit v10 on v9

--- a/solution.py
+++ b/solution.py
@@ -354,6 +354,10 @@
         theirs[c] = jnp.where(first, b, a).astype(theirs.dtype)
 
 
+def hops(chips):
+    return sorted(range(1, chips), key=lambda hop: -min(hop, chips - hop))
+
+
 def pair_kernel(mine, got, total, *rest):
     shares, both = rest[:-1], rest[-1]
     chips = mine.shape[0]
@@ -361,7 +365,7 @@
     for c in range(chips):
         both[c] = mine[c] + got[c].astype(jnp.float32)
     total[...] = both[chip]
-    for hop, share in enumerate(shares, 1):
+    for hop, share in zip(hops(chips), shares):
         share[...] = both[lax.rem(chip + hop, chips)].astype(share.dtype)
 
 
@@ -376,9 +380,18 @@
         out[s] = y.astype(out.dtype)
 
 
-def copies_kernel(x, out):
-    for r in range(out.shape[0]):
-        out[r] = x[...]
+def copies_kernel(x, out, buffer, sems):
+    size = buffer.shape[0]
+    for r in range(size):
+        buffer[r] = x[...]
+    copies = [
+        pltpu.make_async_copy(buffer, out.at[pl.ds(i * size, size)], sems.at[i])
+        for i in range(out.shape[0] // size)
+    ]
+    for copy in copies:
+        copy.start()
+    for copy in copies:
+        copy.wait()
 
 
 def in_hbm(x):
@@ -416,7 +429,7 @@
     )(mine, got)
     arrived = [
         lax.ppermute(x, "head", [(i, (i + 2 * hop) % groups) for i in range(groups)])
-        for hop, x in enumerate(shares, 1)
+        for hop, x in zip(hops(chips), shares)
     ]
     return on_device(
         finish_kernel,
@@ -447,8 +460,17 @@
     vmem, smem, anywhere = pltpu.VMEM, pltpu.SMEM, pl.ANY
     own_query = queries.reshape(STEPS, width)
 
+    pieces = 8
     copies = on_device(
-        copies_kernel, jax.ShapeDtypeStruct((peers, STEPS, width), jnp.bfloat16), [vmem], 4
+        copies_kernel,
+        jax.ShapeDtypeStruct((peers, STEPS, width), jnp.bfloat16),
+        [vmem],
+        4,
+        out_specs=pl.BlockSpec(memory_space=pl.ANY),
+        scratch_shapes=[
+            pltpu.VMEM((peers // pieces, STEPS, width), jnp.bfloat16),
+            pltpu.SemaphoreType.DMA((pieces,)),
+        ],
     )(own_query)
     everyone = lax.all_to_all(copies, "seq", 0, 0, tiled=True)
 

time: 72.1 us -> 72.6 us (level)
  transfers between devices with their start and end apart: 5 -> 5, of which waited for: 4 -> 3; matrix products, arithmetic and copies ran while one was open for 0% -> 0% of each run, Pallas kernels for 8% -> 8%
where the time goes in v10:
time: 72.6 us; the launch traced here: 71.8 us
  blocking collectives  28.9 us (40%)
  starting transfers between devices  22 us (30%)
  Pallas kernels  12.8 us (18%)
  waiting for transfers between devices  7.2 us (10%)
  local copies, waits for them, and re-layouts  0.89 us (1%)
    all_to_all x1, blocking collectives, body(): arrived = lax.all_to_all(partials, 'seq', 0, 0, tiled=True)  14.7 us
    all_to_all x1, blocking collectives, body(): lax.all_to_all(attended, 'seq', 0, 0, tiled=True)  14.1 us
    all_to_all x1, starting transfers between devices, body(): everyone = lax.all_to_all(copies, 'seq', 0, 0, tiled=True)  11.9 us
    ppermute x3, starting transfers between devices, project_and_sum(): lax.ppermute(x, 'head', [(i, (i + 2 * hop) % groups) for i in range(group...  5.68 us
    all_to_all x1, waiting for transfers between devices, body(): everyone = lax.all_to_all(copies, 'seq', 0, 0, tiled=True)  5.3 us
    pallas_call x1, Pallas kernels, body(): on_device(functools.partial(attend_kernel, blocks, hdim), (jax.ShapeDtype...  4.81 us
    ppermute x1, starting transfers between devices, project_and_sum(): got = lax.ppermute(theirs, 'head', [(i, i ^ 1) for i in range(groups)])  4.41 us
    pallas_call x1, Pallas kernels, body(): on_device(stage_kernel, (pltpu.VMEM((ready * BLK, width), jnp.bfloat16),...  3.52 us
  transfers between devices with their start and end apart: 5, of which 3 were waited for; matrix products, arithmetic and copies ran while one was open for 0% of the time, Pallas kernels for 8%

profile of v10, /device:TPU:1, one launch (start us, length us, event | category | flops | bytes accessed | tf_op | source)
XLA Modules:
  0.0 71.8 jit_solution(14598696489665200428)
XLA Ops:
  0.0 0.0 copy-start.1
  0.0 0.7 copy-done.1
  0.7 0.8 %shard_map.101 = bf16[32,2,1792]{2,1,0:T(2,128)(2,1)} custom-call(bf16[2,1792]{1,0:T(2,128)(2,1)S(1)} %bitcast.5), custom_call_target="tpu_custom_call" | custom-call | tf_op jit(solution)/shard_map/pallas_call | solution.py:464
  1.5 11.9 %all-to-all-start = ((bf16[32,2,1792]{2,1,0:T(2,128)(2,1)}), bf16[32,2,1792]{2,1,0:T(2,128)(2,1)S(1)}, u32[]{:S(2)}, u32[]{:S(2)}) async-start(bf16[32,2,1792]{2,1,0:T(2,128)(2,1)} %shard_map.101), calls=%async_computation | async-start | bytes 458752 | tf_op jit(solution)/shard_map/all_to_all | solution.py:475
  13.4 3.5 %shard_map.102 = (bf16[896,1792]{1,0:T(8,128)(2,1)S(1)}, bf16[448,1792]{1,0:T(8,128)(2,1)}) custom-call(bf16[1024,1792]{1,0:T(8,128)(2,1)} %keys.3, bf16[448,1792]{1,0:T(8,128)(2,1)} %bitcast.6), custom_call_target="tpu_custom_call" | custom-call | bytes 6422528 | tf_op jit(solution)/shard_map/pallas_call | solution.py:499
  16.9 1.9 %shard_map.100 = (s32[4,8]{1,0:T(4,128)S(1)}, f32[1,128]{1,0:T(1,128)S(1)}, f32[2,128]{1,0:T(2,128)S(1)}, f32[2,1792]{1,0:T(2,128)S(1)}) custom-call(s32[32]{0:T(128)} %seg_blocks.1, s32[32]{0:T(128)} %request_row.1, f32[14]{0:T(128)} %slopes.1, bf16[2,1792]{1,0:T(2,128)(2,1)} %bitcast.4, bf16[2,1792]{1,0:T(2,128)(2,1)} %bitcast.7, bf16[2,1792]{1,0:T(2,128)(2,1)} %bitcast.8), custom_call_target="tpu_custom_call" | custom-call | tf_op jit(solution)/shard_map/pallas_call | solution.py:477
  18.8 5.3 %all-to-all-done.query = bf16[32,2,1792]{2,1,0:T(2,128)(2,1)S(1)} async-done(((bf16[32,2,1792]{2,1,0:T(2,128)(2,1)}), bf16[32,2,1792]{2,1,0:T(2,128)(2,1)S(1)}, u32[]{:S(2)}, u32[]{:S(2)}) %all-to-all-start) | async-done | bytes 229408 | tf_op jit(solution)/shard_map/all_to_all | solution.py:475
  24.1 4.8 %shard_map.103 = (bf16[32,2,1920]{2,1,0:T(2,128)(2,1)S(1)}, bf16[448,1792]{1,0:T(8,128)(2,1)}) custom-call(s32[4,8]{1,0:T(4,128)S(1)} %get-tuple-element.19.meta, f32[1,128]{1,0:T(1,128)S(1)} %get-tuple-element.20.slopes, bf16[32,2,1792]{2,1,0:T(2,128)(2,1)S(1)} %all-to-all-done.query, ...), custom_call_target="tpu_custom_call", output_to_operand_aliasing={{1}: (7, {})} | custom-call | tf_op jit(solution)/shard_map/pallas_call | solution.py:514
  28.9 0.0 copy-start
  28.9 0.0 copy-start.2
  28.9 14.7 %all_to_all.15 = bf16[32,2,1920]{2,1,0:T(2,128)(2,1)S(1)} all-to-all(bf16[32,2,1920]{2,1,0:T(2,128)(2,1)S(1)} %get-tuple-element.24), channel_id=1, replica_groups=mesh['seq'=32,'head'=8] {'seq'}, dimensions={0} | all-to-all | bytes 491520 | tf_op jit(solution)/shard_map/all_to_all | solution.py:539
  43.7 0.1 reshape.18.parts
  43.8 0.6 shard_map.104
  44.3 14.1 %all_to_all.16 = bf16[32,2,1792]{2,1,0:T(2,128)(2,1)S(1)} all-to-all(bf16[32,2,1792]{2,1,0:T(2,128)(2,1)S(1)} %shard_map.104), channel_id=1, replica_groups=mesh['seq'=32,'head'=8] {'seq'}, dimensions={0} | all-to-all | bytes 458752 | tf_op jit(solution)/shard_map/all_to_all | solution.py:547
  58.4 0.1 reshape.19.rows
  58.5 0.0 copy-done
  58.6 0.6 shard_map.105
  59.1 4.4 %collective-permute-start = (bf16[4,8,448]{2,1,0:T(8,128)(2,1)S(1)}, bf16[4,8,448]{2,1,0:T(8,128)(2,1)S(1)}, u32[]{:S(2)}, u32[]{:S(2)}) collective-permute-start(bf16[4,8,448]{2,1,0:T(8,128)(2,1)S(1)} %get-tuple-element.28), channel_id=1, source_target_pairs={{0,1},{1,0},{2,3},{3,2},{4,5},{5,4},{6,7},{7,6},{8,9},{9,8},{10,11... | collective-permute-start | bytes 86024 | tf_op jit(solution)/shard_map/ppermute | solution.py:421
  63.6 0.9 %collective-permute-done.got = bf16[4,8,448]{2,1,0:T(8,128)(2,1)S(1)} collective-permute-done((bf16[4,8,448]{2,1,0:T(8,128)(2,1)S(1)}, bf16[4,8,448]{2,1,0:T(8,128)(2,1)S(1)}, u32[]{:S(2)}, u32[]{:S(2)}) %collective-permute-start) | collective-permute-done | bytes 28704 | tf_op jit(solution)/shard_map/ppermute | solution.py:421
  64.4 3.0 %collective-permute-start.1 = (bf16[8,448]{1,0:T(8,128)(2,1)S(1)}, bf16[8,448]{1,0:T(8,128)(2,1)S(1)}, u32[]{:S(2)}, u32[]{:S(2)}) collective-permute-start(bf16[8,448]{1,0:T(8,128)(2,1)S(1)} %get-tuple-element.30), channel_id=1, source_target_pairs={{0,4},{1,5},{2,6},{3,7},{4,0},{5,1},{6,2},{7,3},{8,12},{9,13},{10,... | collective-permute-start | bytes 21512 | tf_op jit(solution)/shard_map/ppermute | solution.py:431
  67.4 0.4 collective-permute-start.2
  67.8 2.3 %collective-permute-start.3 = (bf16[8,448]{1,0:T(8,128)(2,1)S(1)}, bf16[8,448]{1,0:T(8,128)(2,1)S(1)}, u32[]{:S(2)}, u32[]{:S(2)}) collective-permute-start(bf16[8,448]{1,0:T(8,128)(2,1)S(1)} %get-tuple-element.32), channel_id=1, source_target_pairs={{0,6},{1,7},{2,0},{3,1},{4,2},{5,3},{6,4},{7,5},{8,14},{9,15},{10,... | collective-permute-start | bytes 21512 | tf_op jit(solution)/shard_map/ppermute | solution.py:431
  70.1 0.0 collective-permute-done.1.rest_0_
  70.1 1.0 %collective-permute-done.2.rest_1_ = bf16[8,448]{1,0:T(8,128)(2,1)S(1)} collective-permute-done((bf16[8,448]{1,0:T(8,128)(2,1)S(1)}, bf16[8,448]{1,0:T(8,128)(2,1)S(1)}, u32[]{:S(2)}, u32[]{:S(2)}) %collective-permute-start.2) | collective-permute-done | bytes 7200 | tf_op jit(solution)/shard_map/ppermute | solution.py:431
  71.2 0.0 collective-permute-done.3.rest_2_
  71.2 0.0 copy-done.2
  71.2 0.6 shard_map.107
  (1 shorter events, 0.0 us)
Async XLA Ops:
  0.0 0.7 copy-start.1
  1.5 22.6 %all-to-all-start = ((bf16[32,2,1792]{2,1,0:T(2,128)(2,1)}), bf16[32,2,1792]{2,1,0:T(2,128)(2,1)S(1)}, u32[]{:S(2)}, u32[]{:S(2)}) async-start(bf16[32,2,1792]{2,1,0:T(2,128)(2,1)} %shard_map.101), calls=%async_computation | async-start | bytes 458752 | tf_op jit(solution)/shard_map/all_to_all | solution.py:475
  28.9 29.6 %copy-start = (bf16[448,1792]{1,0:T(8,128)(2,1)S(1)}, bf16[448,1792]{1,0:T(8,128)(2,1)}, u32[]{:S(2)}) copy-start(bf16[448,1792]{1,0:T(8,128)(2,1)} %get-tuple-element.26.weight) | copy-start | bytes 4816900
  28.9 42.2 %copy-start.2 = (bf16[2,4,448]{2,1,0:T(4,128)(2,1)S(1)}, bf16[2,4,448]{2,1,0:T(4,128)(2,1)}, u32[]{:S(2)}) copy-start(bf16[2,4,448]{2,1,0:T(4,128)(2,1)} %rest_3_.1) | copy-start | bytes 21508
  59.1 5.3 %collective-permute-start = (bf16[4,8,448]{2,1,0:T(8,128)(2,1)S(1)}, bf16[4,8,448]{2,1,0:T(8,128)(2,1)S(1)}, u32[]{:S(2)}, u32[]{:S(2)}) collective-permute-start(bf16[4,8,448]{2,1,0:T(8,128)(2,1)S(1)} %get-tuple-element.28), channel_id=1, source_target_pairs={{0,1},{1,0},{2,3},{3,2},{4,5},{5,4},{6,7},{7,6},{8,9},{9,8},{10,11... | collective-permute-start | bytes 86024 | tf_op jit(solution)/shard_map/ppermute | solution.py:421
  64.4 5.7 %collective-permute-start.1 = (bf16[8,448]{1,0:T(8,128)(2,1)S(1)}, bf16[8,448]{1,0:T(8,128)(2,1)S(1)}, u32[]{:S(2)}, u32[]{:S(2)}) collective-permute-start(bf16[8,448]{1,0:T(8,128)(2,1)S(1)} %get-tuple-element.30), channel_id=1, source_target_pairs={{0,4},{1,5},{2,6},{3,7},{4,0},{5,1},{6,2},{7,3},{8,12},{9,13},{10,... | collective-permute-start | bytes 21512 | tf_op jit(solution)/shard_map/ppermute | solution.py:431
  67.4 3.7 %collective-permute-start.2 = (bf16[8,448]{1,0:T(8,128)(2,1)S(1)}, bf16[8,448]{1,0:T(8,128)(2,1)S(1)}, u32[]{:S(2)}, u32[]{:S(2)}) collective-permute-start(bf16[8,448]{1,0:T(8,128)(2,1)S(1)} %get-tuple-element.31), channel_id=1, source_target_pairs={{0,2},{1,3},{2,4},{3,5},{4,6},{5,7},{6,0},{7,1},{8,10},{9,11},{10,... | collective-permute-start | bytes 21512 | tf_op jit(solution)/shard_map/ppermute | solution.py:431
  67.8 3.3 %collective-permute-start.3 = (bf16[8,448]{1,0:T(8,128)(2,1)S(1)}, bf16[8,448]{1,0:T(8,128)(2,1)S(1)}, u32[]{:S(2)}, u32[]{:S(2)}) collective-permute-start(bf16[8,448]{1,0:T(8,128)(2,1)S(1)} %get-tuple-element.32), channel_id=1, source_target_pairs={{0,6},{1,7},{2,0},{3,1},{4,2},{5,3},{6,4},{7,5},{8,14},{9,15},{10,... | collective-permute-start | bytes 21512 | tf_op jit(solution)/shard_map/ppermute | solution.py:431

commit v11 on v9

--- a/solution.py
+++ b/solution.py
@@ -354,22 +354,22 @@
         theirs[c] = jnp.where(first, b, a).astype(theirs.dtype)
 
 
-def pair_kernel(mine, got, total, *rest):
-    shares, both = rest[:-1], rest[-1]
-    chips = mine.shape[0]
+def pair_kernel(mine, got, keep, send, both):
     chip = lax.axis_index("head") // 2
-    for c in range(chips):
+    for c in range(mine.shape[0]):
         both[c] = mine[c] + got[c].astype(jnp.float32)
-    total[...] = both[chip]
-    for hop, share in enumerate(shares, 1):
-        share[...] = both[lax.rem(chip + hop, chips)].astype(share.dtype)
-
-
-def finish_kernel(total, *rest):
-    shares, residual, out = rest[:-2], rest[-2], rest[-1]
-    x = total[...]
-    for share in shares:
-        x = x + share[...].astype(jnp.float32)
+    for i, other in enumerate((0, 3)):
+        keep[i] = both[chip ^ other]
+        send[i] = both[chip ^ other ^ 1].astype(send.dtype)
+
+
+def half_kernel(keep, got, total, send):
+    total[...] = keep[0] + got[0].astype(jnp.float32)
+    send[...] = (keep[1] + got[1].astype(jnp.float32)).astype(send.dtype)
+
+
+def finish_kernel(total, got, residual, out):
+    x = total[...] + got[...].astype(jnp.float32)
     for s in range(STEPS):
         rows = [x[r : r + 1] for r in range(s, x.shape[0], STEPS)]
         y = residual[s].astype(jnp.float32) + jnp.concatenate(rows, axis=0)
@@ -406,24 +406,31 @@
         16,
     )(rows, weight)
     got = lax.ppermute(theirs, "head", [(i, i ^ 1) for i in range(groups)])
-    share = jax.ShapeDtypeStruct((size, columns), jnp.bfloat16)
-    total, *shares = on_device(
+    half = (2, size, columns)
+    keep, send = on_device(
         pair_kernel,
-        (jax.ShapeDtypeStruct((size, columns), jnp.float32), *[share] * (chips - 1)),
+        (jax.ShapeDtypeStruct(half, jnp.float32), jax.ShapeDtypeStruct(half, jnp.bfloat16)),
         [pltpu.VMEM] * 2,
         16,
         scratch_shapes=[pltpu.VMEM(each, jnp.float32)],
     )(mine, got)
-    arrived = [
-        lax.ppermute(x, "head", [(i, (i + 2 * hop) % groups) for i in range(groups)])
-        for hop, x in enumerate(shares, 1)
-    ]
+    got = lax.ppermute(send, "head", [(i, i ^ 2) for i in range(groups)])
+    total, send = on_device(
+        half_kernel,
+        (
+            jax.ShapeDtypeStruct(half[1:], jnp.float32),
+            jax.ShapeDtypeStruct(half[1:], jnp.bfloat16),
+        ),
+        [pltpu.VMEM] * 2,
+        16,
+    )(keep, got)
+    got = lax.ppermute(send, "head", [(i, i ^ 6) for i in range(groups)])
     return on_device(
         finish_kernel,
         jax.ShapeDtypeStruct(residual.shape, residual.dtype),
-        [pltpu.VMEM] * (chips + 1),
+        [pltpu.VMEM] * 3,
         16,
-    )(total, *arrived, residual)
+    )(total, got, residual)
 
 
 def body(

time: 72.1 us -> 72.8 us (level); the launches traced: 71.8 us -> 71.4 us
  starting transfers between devices: 21.3 us -> 20.4 us
    ppermute x3 -> x2, starting transfers between devices: 5.06 us -> 4.12 us  [the longest x1 2.74 us: project_and_sum(): got = lax.ppermute(send, 'head', [(i, i ^ 6) for i in range(groups)])]
    ppermute x3 -> x2, waiting for transfers between devices: 1.7 us -> 2.33 us  [the longest x1 1.29 us: project_and_sum(): got = lax.ppermute(send, 'head', [(i, i ^ 2) for i in range(groups)])]
  transfers between devices with their start and end apart: 5 -> 4, of which waited for: 4 -> 4; matrix products, arithmetic and copies ran while one was open for 0% -> 0% of each run, Pallas kernels for 8% -> 8%
where the time goes in v11:
time: 72.8 us; the launch traced here: 71.4 us
  blocking collectives  28.9 us (40%)
  starting transfers between devices  20.4 us (28%)
  Pallas kernels  12.7 us (17%)
  waiting for transfers between devices  8.49 us (12%)
  local copies, waits for them, and re-layouts  0.89 us (1%)
    all_to_all x1, blocking collectives, body(): arrived = lax.all_to_all(partials, 'seq', 0, 0, tiled=True)  14.7 us
    all_to_all x1, blocking collectives, body(): lax.all_to_all(attended, 'seq', 0, 0, tiled=True)  14.1 us
    all_to_all x1, starting transfers between devices, body(): everyone = lax.all_to_all(copies, 'seq', 0, 0, tiled=True)  11.9 us
    all_to_all x1, waiting for transfers between devices, body(): everyone = lax.all_to_all(copies, 'seq', 0, 0, tiled=True)  5.3 us
    pallas_call x1, Pallas kernels, body(): on_device(functools.partial(attend_kernel, blocks, hdim), (jax.ShapeDtype...  4.81 us
    ppermute x1, starting transfers between devices, project_and_sum(): got = lax.ppermute(theirs, 'head', [(i, i ^ 1) for i in range(groups)])  4.41 us
    pallas_call x1, Pallas kernels, body(): on_device(stage_kernel, (pltpu.VMEM((ready * BLK, width), jnp.bfloat16),...  3.52 us
    ppermute x1, starting transfers between devices, project_and_sum(): got = lax.ppermute(send, 'head', [(i, i ^ 6) for i in range(groups)])  2.74 us
  transfers between devices with their start and end apart: 4, of which 4 were waited for; matrix products, arithmetic and copies ran while one was open for 0% of the time, Pallas kernels for 8%

profile of v11, /device:TPU:1, one launch (start us, length us, event | category | flops | bytes accessed | tf_op | source)
XLA Modules:
  0.0 71.4 jit_solution(17167863527677161831)
XLA Ops:
  0.0 0.0 copy-start.1
  0.0 0.7 copy-done.1
  0.7 0.7 shard_map.101
  1.4 11.9 %all-to-all-start = ((bf16[32,2,1792]{2,1,0:T(2,128)(2,1)}), bf16[32,2,1792]{2,1,0:T(2,128)(2,1)S(1)}, u32[]{:S(2)}, u32[]{:S(2)}) async-start(bf16[32,2,1792]{2,1,0:T(2,128)(2,1)} %shard_map.101), calls=%async_computation | async-start | bytes 458752 | tf_op jit(solution)/shard_map/all_to_all | solution.py:460
  13.3 3.5 %shard_map.102 = (bf16[896,1792]{1,0:T(8,128)(2,1)S(1)}, bf16[448,1792]{1,0:T(8,128)(2,1)}) custom-call(bf16[1024,1792]{1,0:T(8,128)(2,1)} %keys.3, bf16[448,1792]{1,0:T(8,128)(2,1)} %bitcast.6), custom_call_target="tpu_custom_call" | custom-call | bytes 6422528 | tf_op jit(solution)/shard_map/pallas_call | solution.py:484
  16.8 1.9 %shard_map.100 = (s32[4,8]{1,0:T(4,128)S(1)}, f32[1,128]{1,0:T(1,128)S(1)}, f32[2,128]{1,0:T(2,128)S(1)}, f32[2,1792]{1,0:T(2,128)S(1)}) custom-call(s32[32]{0:T(128)} %seg_blocks.1, s32[32]{0:T(128)} %request_row.1, f32[14]{0:T(128)} %slopes.1, bf16[2,1792]{1,0:T(2,128)(2,1)} %bitcast.4, bf16[2,1792]{1,0:T(2,128)(2,1)} %bitcast.7, bf16[2,1792]{1,0:T(2,128)(2,1)} %bitcast.8), custom_call_target="tpu_custom_call" | custom-call | tf_op jit(solution)/shard_map/pallas_call | solution.py:462
  18.7 5.3 %all-to-all-done.query = bf16[32,2,1792]{2,1,0:T(2,128)(2,1)S(1)} async-done(((bf16[32,2,1792]{2,1,0:T(2,128)(2,1)}), bf16[32,2,1792]{2,1,0:T(2,128)(2,1)S(1)}, u32[]{:S(2)}, u32[]{:S(2)}) %all-to-all-start) | async-done | bytes 229408 | tf_op jit(solution)/shard_map/all_to_all | solution.py:460
  24.0 4.8 %shard_map.103 = (bf16[32,2,1920]{2,1,0:T(2,128)(2,1)S(1)}, bf16[448,1792]{1,0:T(8,128)(2,1)}) custom-call(s32[4,8]{1,0:T(4,128)S(1)} %get-tuple-element.19.meta, f32[1,128]{1,0:T(1,128)S(1)} %get-tuple-element.20.slopes, bf16[32,2,1792]{2,1,0:T(2,128)(2,1)S(1)} %all-to-all-done.query, ...), custom_call_target="tpu_custom_call", output_to_operand_aliasing={{1}: (7, {})} | custom-call | tf_op jit(solution)/shard_map/pallas_call | solution.py:499
  28.8 0.0 copy-start
  28.8 0.0 copy-start.2
  28.9 14.7 %all_to_all.15 = bf16[32,2,1920]{2,1,0:T(2,128)(2,1)S(1)} all-to-all(bf16[32,2,1920]{2,1,0:T(2,128)(2,1)S(1)} %get-tuple-element.24), channel_id=1, replica_groups=mesh['seq'=32,'head'=8] {'seq'}, dimensions={0} | all-to-all | bytes 491520 | tf_op jit(solution)/shard_map/all_to_all | solution.py:524
  43.6 0.1 reshape.18.parts
  43.7 0.6 shard_map.104
  44.3 14.1 %all_to_all.16 = bf16[32,2,1792]{2,1,0:T(2,128)(2,1)S(1)} all-to-all(bf16[32,2,1792]{2,1,0:T(2,128)(2,1)S(1)} %shard_map.104), channel_id=1, replica_groups=mesh['seq'=32,'head'=8] {'seq'}, dimensions={0} | all-to-all | bytes 458752 | tf_op jit(solution)/shard_map/all_to_all | solution.py:532
  58.4 0.1 reshape.19.rows
  58.5 0.0 copy-done
  58.5 0.6 shard_map.105
  59.1 4.4 %collective-permute-start = (bf16[4,8,448]{2,1,0:T(8,128)(2,1)S(1)}, bf16[4,8,448]{2,1,0:T(8,128)(2,1)S(1)}, u32[]{:S(2)}, u32[]{:S(2)}) collective-permute-start(bf16[4,8,448]{2,1,0:T(8,128)(2,1)S(1)} %get-tuple-element.28), channel_id=1, source_target_pairs={{0,1},{1,0},{2,3},{3,2},{4,5},{5,4},{6,7},{7,6},{8,9},{9,8},{10,11... | collective-permute-start | bytes 86024 | tf_op jit(solution)/shard_map/ppermute | solution.py:408
  63.5 0.9 %collective-permute-done.got = bf16[4,8,448]{2,1,0:T(8,128)(2,1)S(1)} collective-permute-done((bf16[4,8,448]{2,1,0:T(8,128)(2,1)S(1)}, bf16[4,8,448]{2,1,0:T(8,128)(2,1)S(1)}, u32[]{:S(2)}, u32[]{:S(2)}) %collective-permute-start) | collective-permute-done | bytes 28704 | tf_op jit(solution)/shard_map/ppermute | solution.py:408
  64.4 1.4 %collective-permute-start.1 = (bf16[2,8,448]{2,1,0:T(8,128)(2,1)S(1)}, bf16[2,8,448]{2,1,0:T(8,128)(2,1)S(1)}, u32[]{:S(2)}, u32[]{:S(2)}) collective-permute-start(bf16[2,8,448]{2,1,0:T(8,128)(2,1)S(1)} %get-tuple-element.30), channel_id=1, source_target_pairs={{0,2},{1,3},{2,0},{3,1},{4,6},{5,7},{6,4},{7,5},{8,10},{9,11},{10,... | collective-permute-start | bytes 43016 | tf_op jit(solution)/shard_map/ppermute | solution.py:417
  65.7 1.3 %collective-permute-done.1.got = bf16[2,8,448]{2,1,0:T(8,128)(2,1)S(1)} collective-permute-done((bf16[2,8,448]{2,1,0:T(8,128)(2,1)S(1)}, bf16[2,8,448]{2,1,0:T(8,128)(2,1)S(1)}, u32[]{:S(2)}, u32[]{:S(2)}) %collective-permute-start.1) | collective-permute-done | bytes 14368 | tf_op jit(solution)/shard_map/ppermute | solution.py:417
  67.0 2.7 %collective-permute-start.2 = (bf16[8,448]{1,0:T(8,128)(2,1)S(1)}, bf16[8,448]{1,0:T(8,128)(2,1)S(1)}, u32[]{:S(2)}, u32[]{:S(2)}) collective-permute-start(bf16[8,448]{1,0:T(8,128)(2,1)S(1)} %get-tuple-element.32), channel_id=1, source_target_pairs={{0,6},{1,7},{2,4},{3,5},{4,2},{5,3},{6,0},{7,1},{8,14},{9,15},{10,... | collective-permute-start | bytes 21512 | tf_op jit(solution)/shard_map/ppermute | solution.py:427
  69.8 1.0 %collective-permute-done.2.got = bf16[8,448]{1,0:T(8,128)(2,1)S(1)} collective-permute-done((bf16[8,448]{1,0:T(8,128)(2,1)S(1)}, bf16[8,448]{1,0:T(8,128)(2,1)S(1)}, u32[]{:S(2)}, u32[]{:S(2)}) %collective-permute-start.2) | collective-permute-done | bytes 7200 | tf_op jit(solution)/shard_map/ppermute | solution.py:427
  70.8 0.0 copy-done.2
  70.8 0.6 shard_map.108
  (2 shorter events, 0.0 us)
Async XLA Ops:
  0.0 0.7 copy-start.1
  1.4 22.6 %all-to-all-start = ((bf16[32,2,1792]{2,1,0:T(2,128)(2,1)}), bf16[32,2,1792]{2,1,0:T(2,128)(2,1)S(1)}, u32[]{:S(2)}, u32[]{:S(2)}) async-start(bf16[32,2,1792]{2,1,0:T(2,128)(2,1)} %shard_map.101), calls=%async_computation | async-start | bytes 458752 | tf_op jit(solution)/shard_map/all_to_all | solution.py:460
  28.8 29.6 %copy-start = (bf16[448,1792]{1,0:T(8,128)(2,1)S(1)}, bf16[448,1792]{1,0:T(8,128)(2,1)}, u32[]{:S(2)}) copy-start(bf16[448,1792]{1,0:T(8,128)(2,1)} %get-tuple-element.26.weight) | copy-start | bytes 4816900
  28.8 42.0 %copy-start.2 = (bf16[2,4,448]{2,1,0:T(4,128)(2,1)S(1)}, bf16[2,4,448]{2,1,0:T(4,128)(2,1)}, u32[]{:S(2)}) copy-start(bf16[2,4,448]{2,1,0:T(4,128)(2,1)} %residual.1) | copy-start | bytes 21508
  59.1 5.3 %collective-permute-start = (bf16[4,8,448]{2,1,0:T(8,128)(2,1)S(1)}, bf16[4,8,448]{2,1,0:T(8,128)(2,1)S(1)}, u32[]{:S(2)}, u32[]{:S(2)}) collective-permute-start(bf16[4,8,448]{2,1,0:T(8,128)(2,1)S(1)} %get-tuple-element.28), channel_id=1, source_target_pairs={{0,1},{1,0},{2,3},{3,2},{4,5},{5,4},{6,7},{7,6},{8,9},{9,8},{10,11... | collective-permute-start | bytes 86024 | tf_op jit(solution)/shard_map/ppermute | solution.py:408
  64.4 2.7 %collective-permute-start.1 = (bf16[2,8,448]{2,1,0:T(8,128)(2,1)S(1)}, bf16[2,8,448]{2,1,0:T(8,128)(2,1)S(1)}, u32[]{:S(2)}, u32[]{:S(2)}) collective-permute-start(bf16[2,8,448]{2,1,0:T(8,128)(2,1)S(1)} %get-tuple-element.30), channel_id=1, source_target_pairs={{0,2},{1,3},{2,0},{3,1},{4,6},{5,7},{6,4},{7,5},{8,10},{9,11},{10,... | collective-permute-start | bytes 43016 | tf_op jit(solution)/shard_map/ppermute | solution.py:417
  67.0 3.8 %collective-permute-start.2 = (bf16[8,448]{1,0:T(8,128)(2,1)S(1)}, bf16[8,448]{1,0:T(8,128)(2,1)S(1)}, u32[]{:S(2)}, u32[]{:S(2)}) collective-permute-start(bf16[8,448]{1,0:T(8,128)(2,1)S(1)} %get-tuple-element.32), channel_id=1, source_target_pairs={{0,6},{1,7},{2,4},{3,5},{4,2},{5,3},{6,0},{7,1},{8,14},{9,15},{10,... | collective-permute-start | bytes 21512 | tf_op jit(solution)/shard_map/ppermute | solution.py:427
